TPU v7x, 32 devices: a whole 2x2x4 slice. The times are simulated.
32 devices in a mesh: groups: 2 (over y), ffn: 8 (over z, x), width: 2 (over core).
Axes of the slice: x: 2, y: 2, z: 4, core: 2. Of those that a mesh axis runs over, the one named last changes fastest.
Arguments:
- tokens: bfloat16 [128, 8192], P(('groups', 'ffn'), 'width'), parts along dimension 0, may hold values from -6 to 6
- base_up_weight: bfloat16 [8192, 28672], P('width', 'ffn'), may hold values from -0.0625 to 0.0625
- adapter_index_per_row: int32 [128], P(('groups', 'ffn')), parts along dimension 0, may hold values from 0 to 7
- holder_slot_index: int32 [16], P('groups'), parts along dimension 0, may hold values from 0 to 7, each once
- down_factor_pool: bfloat16 [16, 8192, 64], P(('groups', 'ffn'), 'width'), parts along dimension 0, may hold values from -0.0625 to 0.0625
- up_factor_table: bfloat16 [16, 64, 28672], P('groups', 'width', 'ffn'), parts along dimension 0, may hold values from -0.75 to 0.75
Outputs:
- projected: bfloat16 [128, 28672], P(('groups', 'width'), 'ffn'), parts along dimension 0
There are 2 independent parts, one for each index of `groups`. A program takes and returns all parts, laid end to end along the dimension named above; an argument that names none is the same for every part. Nothing has to cross between parts.
Inputs may be any that keep to these rules, and one draw needn't show every extreme that they name: `holder_slot_index`: each adapter sits in exactly one slot.
All inputs are finite; a program needn't handle non-finite values.
Results may differ from a plain program's by a relative error of at most 0.004.
Values may be sent and summed in bfloat16 or wider, within the bound.
No kernel may reach another device: no remote copies, remote signals or barrier semaphores. Data moves between devices by JAX's collectives and lax.ppermute only.
A program may use at most 128 MiB of HBM per device.

v0:
```python
import math

import jax
import jax.numpy as jnp
from jax import lax
from jax.sharding import PartitionSpec as P


def on_device(
    tokens,
    base_up_weight,
    adapter_index_per_row,
    holder_slot_index,
    down_factor_pool,
    up_factor_table,
):
    gathered, row_ids = (
        lax.all_gather(tokens, "ffn", axis=0, tiled=True),
        lax.all_gather(adapter_index_per_row, "ffn", axis=0, tiled=True),
    )
    total_rows = gathered.shape[0]
    adapter_store = holder_slot_index.shape[0]
    rank_portion = up_factor_table.shape[1]
    column_range = base_up_weight.shape[1]
    base = jnp.dot(gathered, base_up_weight, preferred_element_type=jnp.float32)
    matches = row_ids[:, None] == jnp.arange(adapter_store, dtype=jnp.int32)[None, :]
    slot = jnp.sum(jnp.where(matches, holder_slot_index[None, :], 0), axis=1)
    mine = slot == lax.axis_index("ffn")
    masked_values = jnp.where(mine[:, None], gathered, jnp.zeros_like(gathered))
    reduced_input = jnp.dot(masked_values, down_factor_pool[0], preferred_element_type=jnp.float32)
    summed = lax.psum(reduced_input, ("ffn", "width"))
    own_half = lax.dynamic_slice_in_dim(
        summed, lax.axis_index("width") * rank_portion, rank_portion, 1
    )
    low_bf = own_half.astype(jnp.bfloat16)
    block = math.gcd(total_rows, 256)
    low_blocks = low_bf.reshape(total_rows // block, block, rank_portion)
    id_blocks = row_ids.reshape(total_rows // block, block)
    lookup_matrix = up_factor_table.reshape(adapter_store * rank_portion, column_range)
    adapter_range = jnp.arange(adapter_store, dtype=jnp.int32)

    def expand(pair):
        rows, index_values = pair
        picked = (index_values[:, None] == adapter_range[None, :])[:, :, None]
        spread = jnp.where(picked, rows[:, None, :], jnp.zeros((), jnp.bfloat16))
        spread = spread.reshape(rows.shape[0], adapter_store * rank_portion)
        return jnp.dot(spread, lookup_matrix, preferred_element_type=jnp.float32)

    delta = lax.map(expand, (low_blocks, id_blocks)).reshape(total_rows, column_range)
    summed_out = lax.psum_scatter(base + delta, "width", scatter_dimension=0, tiled=True)
    return summed_out.astype(jnp.bfloat16)


def solution(mesh):
    placed = (
        P(("groups", "ffn"), "width"),
        P("width", "ffn"),
        P(("groups", "ffn")),
        P("groups"),
        P(("groups", "ffn"), "width", None),
        P("groups", "width", "ffn"),
    )
    return jax.shard_map(
        on_device,
        mesh=mesh,
        in_specs=placed,
        out_specs=P(("groups", "width"), "ffn"),
        check_vma=False,
    )
```

profile of v0, /device:TPU:0, one launch (start us, length us, event | category | flops | bytes accessed | tf_op | source)
XLA Modules:
  0.0 142.0 jit_solution(7784522790403894612)
XLA Ops:
  6.5 0.0 copy-start
  6.5 0.0 reduce-scatter.2.cloned.1.call-start
  6.5 1.4 dynamic-slice.2
  8.6 0.9 dynamic-update-slice
  9.4 13.1 %all-reduce = s32[64]{0:T(128)S(1)} all-reduce(s32[64]{0:T(128)S(1)} %dynamic-update-slice), channel_id=1, replica_groups=mesh['groups'=2,'ffn'=8,'width'=2] {'ffn'}, use_global_device_ids=true, to_apply=%add | all-reduce | flops 64 | bytes 512
  22.5 0.7 select_reduce_fusion
  23.2 31.7 %all_gather.6 = bf16[64,4096]{1,0:T(8,128)(2,1)S(1)} all-gather(bf16[8,4096]{1,0:T(8,128)(2,1)} %param.6), channel_id=1, replica_groups=mesh['groups'=2,'ffn'=8,'width'=2] {'ffn'}, dimensions={0}, use_global_device_ids=true | all-gather | bytes 589824 | tf_op jit(solution)/shard_map/all_gather | solution.py:18
  55.0 1.4 fusion
  56.4 57.6 %psum.7 = bf16[64,64]{0,1:T(8,128)(2,1)S(1)} all-reduce(f32[64,64]{0,1:T(8,128)S(1)} %fusion), channel_id=1, replica_groups=mesh['groups'=2,'ffn'=8,'width'=2] {'ffn','width'}, use_global_device_ids=true, to_apply=%region_1.2 | all-reduce | flops 4096 | bytes 24576 | tf_op jit(solution)/shard_map/psum | solution.py:31
  114.0 0.0 copy-done
  114.0 0.5 convolution_bitcast_fusion
  114.5 13.0 %convolution_add_fusion = f32[64,3584]{1,0:T(8,128)} fusion(f32[64,3584]{1,0:T(8,128)S(1)} %convolution_bitcast_fusion, bf16[64,4096]{1,0:T(8,128)(2,1)S(1)} %all_gather.6, bf16[4096,3584]{1,0:T(8,128)(2,1)} %param.7), kind=kOutput, calls=%fused_computation | convolution fusion | flops 1879277568 | bytes 31719424 | tf_op jit(solution)/shard_map/dot_general | solution.py:25
  127.5 0.0 reduce-scatter.2.cloned.1.call-update
  127.5 5.9 %reduce-scatter.2.cloned.1.call-done = f32[32,3584]{1,0:T(8,128)} async-done(((f32[64,3584]{1,0:T(8,128)}), f32[32,3584]{1,0:T(8,128)}) %reduce-scatter.2.cloned.1.call-update) | async-done | bytes 458768 | tf_op jit(solution)/shard_map/reduce_scatter | solution.py:50
  133.4 1.7 %convert_element_type.7 = bf16[32,3584]{1,0:T(8,128)(2,1)} convert(f32[32,3584]{1,0:T(8,128)} %reduce-scatter.2.cloned.1.call-done) | non-fusion elementwise | flops 114688 | bytes 688128 | tf_op jit(solution)/shard_map/convert_element_type | solution.py:51
  (4 shorter events, 0.0 us)
Async XLA Ops:
  6.5 107.5 %copy-start = (bf16[8,32,3584]{2,1,0:T(8,128)(2,1)S(1)}, bf16[8,32,3584]{2,1,0:T(8,128)(2,1)}, u32[]{:S(2)}) copy-start(bf16[8,32,3584]{2,1,0:T(8,128)(2,1)} %param.11) | copy-start | bytes 5505028
  6.5 126.9 %reduce-scatter.2.cloned.1.call-start = ((), (), s32[]{:S(2)}) async-start(), calls=%async_computation.1 | async-start | bytes 1376256 | tf_op jit(solution)/shard_map/reduce_scatter | solution.py:50
Sparse Core Ops, SparseCore 0:
  127.7 5.6 reduce-scatter.1
where the time goes:
time: 142 us
  blocking collectives  102 us (72%)
  matrix products  14.9 us (10%)
  between operations  14.1 us (10%)
  waiting for transfers between devices  5.87 us (4%)
  other arithmetic  2.48 us (2%)
  local copies, waits for them, and re-layouts  2.24 us (2%)
    psum x1, blocking collectives, on_device(): summed = lax.psum(reduced_input, ('ffn', 'width'))  57.6 us
    all_gather x1, blocking collectives, on_device(): lax.all_gather(tokens, 'ffn', axis=0, tiled=True)  31.7 us
    unnamed x1, blocking collectives  13.1 us
    dot_general x1, matrix products, on_device(): base = jnp.dot(gathered, base_up_weight, preferred_element_type=jnp.float32)  13 us
    reduce_scatter x1, waiting for transfers between devices, on_device(): lax.psum_scatter(base + delta, 'width', scatter_dimension=0, tiled=True)  5.85 us
  transfers between devices with their start and end apart: 1, of which 1 were waited for; matrix products, arithmetic and copies ran while one was open for 0% of the time, Pallas kernels for 0%

commit v1 on v0

v1 whole, which is shorter than its diff:
```python
import functools
import math

import jax
import jax.numpy as jnp
from jax import lax
from jax.experimental import pallas as pl
from jax.experimental.pallas import tpu as pltpu
from jax.sharding import PartitionSpec as P

F32, BF16 = jnp.float32, jnp.bfloat16
VMEM = pl.BlockSpec(memory_space=pltpu.VMEM)
SMEM = pl.BlockSpec(memory_space=pltpu.SMEM)
LANES = 128


def call(kernel, out, in_specs, vmem, scratch=(), flops=0, bytes_accessed=0, aliases=None):
    many = isinstance(out, (list, tuple))
    return pl.pallas_call(
        kernel,
        out_shape=out,
        in_specs=in_specs,
        out_specs=[VMEM] * len(out) if many else VMEM,
        scratch_shapes=list(scratch),
        input_output_aliases=aliases or {},
        compiler_params=pltpu.CompilerParams(vmem_limit_bytes=vmem),
        cost_estimate=pl.CostEstimate(flops=flops, bytes_accessed=bytes_accessed, transcendentals=0),
    )


def pinned(array):
    return pltpu.with_memory_space_constraint(array, pltpu.VMEM)


def pack_kernel(ids, tokens, message):
    rows, wide = tokens.shape
    message[:, :wide] = tokens[...]
    place = lax.broadcasted_iota(jnp.int32, (rows, LANES), 0)
    value = jnp.zeros((rows, LANES), jnp.int32)
    for i in range(rows):
        value = jnp.where(place == i, ids[i], value)
    message[:, wide:] = value.astype(F32).astype(BF16)


def assemble_kernel(n, holder, down, *refs):
    blocks, (x, ids, low, stage, id_stage) = refs[:n], refs[n:]
    rows, wide = blocks[0].shape[0], x.shape[1]
    me = lax.axis_index("ffn")
    for k in range(n):
        at = jnp.bitwise_xor(me, k)
        stage[at] = blocks[k][:, :wide].astype(F32)
        id_stage[at] = blocks[k][:, wide:].astype(F32)
    whole = stage[...].reshape(n * rows, wide).astype(BF16)
    x[...] = whole
    row_ids = id_stage[...].reshape(n * rows, LANES)
    ids[...] = row_ids
    held = jnp.int32(0)
    for a in range(holder.shape[0]):
        held = held + jnp.where(holder[a] == me, a, 0)
    part = lax.dot_general(whole, down[...], (((1,), (1,)), ((), ())), preferred_element_type=F32)
    part = jnp.where(row_ids[:, : part.shape[1]] == held.astype(F32), part, 0.0)
    half = n * rows // 2
    low[...] = jnp.concatenate([part[:half], part[half:]], axis=1)


def add_kernel(a, b, out):
    out[...] = a[...] + b[...]


def base_kernel(offset, step, x, w, _, own, send):
    half, wide = own.shape
    mine = lax.axis_index("width") == 0
    for c in range(0, wide, step):
        s = min(step, wide - c)
        both = jnp.dot(x[...], w[:, offset + c : offset + c + s], preferred_element_type=F32)
        own[:, c : c + s] = jnp.where(mine, both[:half], both[half:])
        send[:, c : c + s] = jnp.where(mine, both[half:], both[:half]).astype(send.dtype)


def finish_kernel(pieces, low, ids, up_own, up_peer, *refs):
    own, got, out = refs[:pieces], refs[pieces : 2 * pieces], refs[2 * pieces]
    count, part, wide = up_own.shape
    half, rank = out.shape[0], 2 * part
    w = lax.axis_index("width")
    mine = w == 0
    rows = jnp.where(mine, low[:, :rank], low[:, rank:]).astype(BF16)
    row_ids = ids[pl.ds(pl.multiple_of(w * half, half), half), :][:, :1]
    lane = lax.broadcasted_iota(jnp.int32, (half, count * part), 1)
    picked = (lane // part).astype(F32) == row_ids
    source = lax.broadcasted_iota(jnp.int32, (rank, count * part), 0)
    target = lax.broadcasted_iota(jnp.int32, (rank, count * part), 1) % part

    def spread(which):
        copies = (source == target + which * part).astype(F32).astype(BF16)
        values = jnp.dot(rows, copies, preferred_element_type=F32)
        return jnp.where(picked, values, 0.0).astype(BF16)

    a, b = spread(w), spread(1 - w)
    c = 0
    for o, g in zip(own, got):
        s = o.shape[1]
        delta = jnp.dot(a, up_own[:, :, c : c + s].reshape(count * part, s), preferred_element_type=F32)
        delta = delta + jnp.dot(b, up_peer[:, :, c : c + s].reshape(count * part, s), preferred_element_type=F32)
        out[:, c : c + s] = (o[...] + g[...].astype(F32) + delta).astype(BF16)
        c += s


def small(n, tokens, base_up_weight, row_ids, holder, pool, table):
    rows, wide = tokens.shape
    columns = base_up_weight.shape[1]
    rank = pool.shape[2]
    half = n * rows // 2

    def swap(v):
        return lax.ppermute(v, "width", [(0, 1), (1, 0)])

    def partner(v, k):
        return lax.ppermute(v, "ffn", [(i, i ^ k) for i in range(n)])

    weight = pinned(base_up_weight)
    up_own = pinned(table)
    up_peer = pinned(swap(table))
    down = pinned(jnp.swapaxes(pool[0], 0, 1))

    message = call(
        pack_kernel, jax.ShapeDtypeStruct((rows, wide + LANES), BF16), [SMEM, VMEM], 1 << 20,
        flops=40 << 30, bytes_accessed=1 << 17,
    )(row_ids, tokens)
    blocks = [message] + [partner(message, k) for k in range(1, n)]

    x, ids, low = call(
        functools.partial(assemble_kernel, n),
        [
            jax.ShapeDtypeStruct((n * rows, wide), BF16),
            jax.ShapeDtypeStruct((n * rows, LANES), F32),
            jax.ShapeDtypeStruct((half, 2 * rank), F32),
        ],
        [SMEM, VMEM] + [VMEM] * n,
        6 << 20,
        scratch=[pltpu.VMEM((n, rows, wide), F32), pltpu.VMEM((n, rows, LANES), F32)],
        flops=1 << 25,
    )(holder, down, *blocks)

    def add(a, b):
        return call(add_kernel, jax.ShapeDtypeStruct(a.shape, F32), [VMEM, VMEM], 1 << 20)(a, b)

    steps = [swap] + [functools.partial(partner, k=1 << i) for i in range(n.bit_length() - 1)]
    units = columns // LANES
    cuts = [0] + [LANES * (units * (2 * i + 1) // (2 * len(steps) - 1)) for i in range(len(steps))]
    own, got = [], []
    for step, a, b in zip(steps, cuts[:-1], cuts[1:]):
        other = step(low)
        o, s = call(
            functools.partial(base_kernel, a, 512),
            [jax.ShapeDtypeStruct((half, b - a), F32), jax.ShapeDtypeStruct((half, b - a), F32)],
            [VMEM, VMEM, VMEM],
            4 << 20,
            flops=2 * 2 * half * wide * (b - a),
            bytes_accessed=2 * wide * (b - a),
        )(x, weight, low)
        own.append(o)
        got.append(swap(s))
        low = add(low, other)

    return call(
        functools.partial(finish_kernel, len(own)),
        jax.ShapeDtypeStruct((half, columns), BF16),
        [VMEM] * (4 + 2 * len(own)),
        8 << 20,
    )(low, ids, up_own, up_peer, *own, *got)


def large(tokens, base_up_weight, adapter_index_per_row, holder_slot_index, down_factor_pool, up_factor_table):
    gathered = lax.all_gather(tokens, "ffn", axis=0, tiled=True)
    row_ids = lax.all_gather(adapter_index_per_row, "ffn", axis=0, tiled=True)
    total_rows = gathered.shape[0]
    adapter_store = holder_slot_index.shape[0]
    rank_portion = up_factor_table.shape[1]
    column_range = base_up_weight.shape[1]
    base = jnp.dot(gathered, base_up_weight, preferred_element_type=F32)
    matches = row_ids[:, None] == jnp.arange(adapter_store, dtype=jnp.int32)[None, :]
    slot = jnp.sum(jnp.where(matches, holder_slot_index[None, :], 0), axis=1)
    mine = slot == lax.axis_index("ffn")
    masked_values = jnp.where(mine[:, None], gathered, jnp.zeros_like(gathered))
    reduced_input = jnp.dot(masked_values, down_factor_pool[0], preferred_element_type=F32)
    summed = lax.psum(reduced_input, ("ffn", "width"))
    own_half = lax.dynamic_slice_in_dim(summed, lax.axis_index("width") * rank_portion, rank_portion, 1)
    low_bf = own_half.astype(BF16)
    block = math.gcd(total_rows, 256)
    low_blocks = low_bf.reshape(total_rows // block, block, rank_portion)
    id_blocks = row_ids.reshape(total_rows // block, block)
    lookup_matrix = up_factor_table.reshape(adapter_store * rank_portion, column_range)
    adapter_range = jnp.arange(adapter_store, dtype=jnp.int32)

    def expand(pair):
        rows, index_values = pair
        picked = (index_values[:, None] == adapter_range[None, :])[:, :, None]
        spread = jnp.where(picked, rows[:, None, :], jnp.zeros((), BF16))
        spread = spread.reshape(rows.shape[0], adapter_store * rank_portion)
        return jnp.dot(spread, lookup_matrix, preferred_element_type=F32)

    delta = lax.map(expand, (low_blocks, id_blocks)).reshape(total_rows, column_range)
    summed_out = lax.psum_scatter(base + delta, "width", scatter_dimension=0, tiled=True)
    return summed_out.astype(BF16)


def solution(mesh):
    n, cores = mesh.shape["ffn"], mesh.shape["width"]
    short = n <= 8 and n & (n - 1) == 0 and n > 1 and cores == 2
    placed = (
        P(("groups", "ffn"), "width"),
        P("width", "ffn"),
        P(("groups", "ffn")),
        P("groups"),
        P(("groups", "ffn"), "width", None),
        P("groups", "width", "ffn"),
    )
    return jax.shard_map(
        functools.partial(small, n) if short else large,
        mesh=mesh,
        in_specs=placed,
        out_specs=P(("groups", "width"), "ffn"),
        check_vma=False,
    )
```

time: 142 us -> 42.4 us (0.30)
  blocking collectives: 102 us -> 0 us
  starting transfers between devices: 0.01 us -> 20.8 us
  matrix products: 14.9 us -> 0 us
  between operations: 14.1 us -> 0.12 us
  Pallas kernels: 0 us -> 8.8 us
  waiting for transfers between devices: 5.87 us -> 11.1 us
  other arithmetic: 2.48 us -> 0 us
    psum x1 -> x0, blocking collectives: 57.6 us -> none  [on_device(): summed = lax.psum(reduced_input, ('ffn', 'width'))]
    all_gather x1 -> x0, blocking collectives: 31.7 us -> none  [on_device(): lax.all_gather(tokens, 'ffn', axis=0, tiled=True)]
    ppermute x0 -> x16, starting transfers between devices: none -> 20.8 us  [the longest x10 19.7 us: partner(): return lax.ppermute(v, 'ffn', [(i, i ^ k) for i in range(n)])]
    dot_general x3 -> x0, matrix products: 14.9 us -> none  [the longest x1 13 us: on_device(): base = jnp.dot(gathered, base_up_weight, preferred_element_type=jnp.float32)]
    unnamed x1 -> x0, blocking collectives: 13.1 us -> none
    ppermute x0 -> x16, waiting for transfers between devices: none -> 11.1 us  [the longest x10 8.63 us: partner(): return lax.ppermute(v, 'ffn', [(i, i ^ k) for i in range(n)])]
    pallas_call x0 -> x11, Pallas kernels: none -> 8.8 us  [the longest x4 5.65 us: small(): call(functools.partial(base_kernel, a, 512), [jax.ShapeDtypeStruct((half,...]
    reduce_scatter x1 -> x0, waiting for transfers between devices: 5.85 us -> none  [on_device(): lax.psum_scatter(base + delta, 'width', scatter_dimension=0, tiled=True)]
  transfers between devices with their start and end apart: 1 -> 16, of which waited for: 1 -> 9; matrix products, arithmetic and copies ran while one was open for 0% -> 0% of each run, Pallas kernels for 0% -> 17%
where the time goes in v1:
time: 42.4 us; the launch traced here: 42.3 us
  starting transfers between devices  20.8 us (49%)
  waiting for transfers between devices  11.1 us (26%)
  Pallas kernels  8.8 us (21%)
  local copies, waits for them, and re-layouts  1.51 us (4%)
    ppermute x10, starting transfers between devices, partner(): return lax.ppermute(v, 'ffn', [(i, i ^ k) for i in range(n)])  19.7 us
    ppermute x10, waiting for transfers between devices, partner(): return lax.ppermute(v, 'ffn', [(i, i ^ k) for i in range(n)])  8.63 us
    pallas_call x4, Pallas kernels, small(): call(functools.partial(base_kernel, a, 512), [jax.ShapeDtypeStruct((half,...  5.65 us
    ppermute x6, waiting for transfers between devices, swap(): return lax.ppermute(v, 'width', [(0, 1), (1, 0)])  2.43 us
    pallas_call x1, Pallas kernels, small(): call(functools.partial(finish_kernel, len(own)), jax.ShapeDtypeStruct((ha...  1.59 us
    unnamed x12, local copies, waits for them, and re-layouts  1.51 us
    ppermute x6, starting transfers between devices, swap(): return lax.ppermute(v, 'width', [(0, 1), (1, 0)])  1.06 us
    pallas_call x1, Pallas kernels, small(): call(functools.partial(assemble_kernel, n), [jax.ShapeDtypeStruct((n * ro...  0.99 us
  transfers between devices with their start and end apart: 16, of which 9 were waited for; matrix products, arithmetic and copies ran while one was open for 0% of the time, Pallas kernels for 17%

profile of v1, /device:TPU:0, one launch (start us, length us, event | category | flops | bytes accessed | tf_op | source)
XLA Modules:
  0.0 42.3 jit_solution(12656705630409027835)
XLA Ops:
  0.5 0.8 %copy-done.4 = bf16[8,4096]{1,0:T(8,128)(2,1)S(1)} copy-done((bf16[8,4096]{1,0:T(8,128)(2,1)S(1)}, bf16[8,4096]{1,0:T(8,128)(2,1)}, u32[]{:S(2)}) %copy-start.4) | copy-done | bytes 65560
  1.3 0.7 %copy-done.5 = s32[8]{0:T(128)S(1)} copy-done((s32[8]{0:T(128)S(1)}, s32[8]{0:T(128)}, u32[]{:S(2)}) %copy-start.5) | copy-done | bytes 56
  2.0 0.6 %shard_map.64.refs_0_ = bf16[8,4224]{1,0:T(8,128)(2,1)S(1)} custom-call(s32[8]{0:T(128)S(1)} %copy-done.5, bf16[8,4096]{1,0:T(8,128)(2,1)S(1)} %copy-done.4), custom_call_target="tpu_custom_call" | custom-call | flops 42949672960 | bytes 131072 | tf_op jit(solution)/shard_map/pallas_call | solution.py:125
  2.5 5.7 %collective-permute-start.6 = (bf16[8,4224]{1,0:T(8,128)(2,1)S(1)}, bf16[8,4224]{1,0:T(8,128)(2,1)S(1)}, u32[]{:S(2)}, u32[]{:S(2)}) collective-permute-start(bf16[8,4224]{1,0:T(8,128)(2,1)S(1)} %shard_map.64.refs_0_), channel_id=1, source_target_pairs={{0,14},{2,12},{4,10},{6,8},{8,6},{10,4},{12,2},{14,0},{1,15},{3,13... | collective-permute-start | bytes 202760 | tf_op jit(solution)/shard_map/ppermute | solution.py:118
  8.4 0.8 %collective-permute-start.4 = (bf16[8,4224]{1,0:T(8,128)(2,1)S(1)}, bf16[8,4224]{1,0:T(8,128)(2,1)S(1)}, u32[]{:S(2)}, u32[]{:S(2)}) collective-permute-start(bf16[8,4224]{1,0:T(8,128)(2,1)S(1)} %shard_map.64.refs_0_), channel_id=1, source_target_pairs={{0,10},{2,8},{4,14},{6,12},{8,2},{10,0},{12,6},{14,4},{1,11},{3,9}... | collective-permute-start | bytes 202760 | tf_op jit(solution)/shard_map/ppermute | solution.py:118
  9.2 2.0 %collective-permute-start.3 = (bf16[8,4224]{1,0:T(8,128)(2,1)S(1)}, bf16[8,4224]{1,0:T(8,128)(2,1)S(1)}, u32[]{:S(2)}, u32[]{:S(2)}) collective-permute-start(bf16[8,4224]{1,0:T(8,128)(2,1)S(1)} %shard_map.64.refs_0_), channel_id=1, source_target_pairs={{0,8},{2,10},{4,12},{6,14},{8,0},{10,2},{12,4},{14,6},{1,9},{3,11}... | collective-permute-start | bytes 202760 | tf_op jit(solution)/shard_map/ppermute | solution.py:118
  11.2 2.3 %collective-permute-start.2 = (bf16[8,4224]{1,0:T(8,128)(2,1)S(1)}, bf16[8,4224]{1,0:T(8,128)(2,1)S(1)}, u32[]{:S(2)}, u32[]{:S(2)}) collective-permute-start(bf16[8,4224]{1,0:T(8,128)(2,1)S(1)} %shard_map.64.refs_0_), channel_id=1, source_target_pairs={{0,6},{2,4},{4,2},{6,0},{8,14},{10,12},{12,10},{14,8},{1,7},{3,5},... | collective-permute-start | bytes 202760 | tf_op jit(solution)/shard_map/ppermute | solution.py:118
  13.5 1.6 %collective-permute-done.5.refs_6_ = bf16[8,4224]{1,0:T(8,128)(2,1)S(1)} collective-permute-done((bf16[8,4224]{1,0:T(8,128)(2,1)S(1)}, bf16[8,4224]{1,0:T(8,128)(2,1)S(1)}, u32[]{:S(2)}, u32[]{:S(2)}) %collective-permute-start.5) | collective-permute-done | bytes 67616 | tf_op jit(solution)/shard_map/ppermute | solution.py:118
  15.1 3.1 %collective-permute-start.1 = (bf16[8,4224]{1,0:T(8,128)(2,1)S(1)}, bf16[8,4224]{1,0:T(8,128)(2,1)S(1)}, u32[]{:S(2)}, u32[]{:S(2)}) collective-permute-start(bf16[8,4224]{1,0:T(8,128)(2,1)S(1)} %shard_map.64.refs_0_), channel_id=1, source_target_pairs={{0,4},{2,6},{4,0},{6,2},{8,12},{10,14},{12,8},{14,10},{1,5},{3,7},... | collective-permute-start | bytes 202760 | tf_op jit(solution)/shard_map/ppermute | solution.py:118
  18.2 0.7 %collective-permute-done.4.refs_5_ = bf16[8,4224]{1,0:T(8,128)(2,1)S(1)} collective-permute-done((bf16[8,4224]{1,0:T(8,128)(2,1)S(1)}, bf16[8,4224]{1,0:T(8,128)(2,1)S(1)}, u32[]{:S(2)}, u32[]{:S(2)}) %collective-permute-start.4) | collective-permute-done | bytes 67616 | tf_op jit(solution)/shard_map/ppermute | solution.py:118
  18.9 1.9 %collective-permute-start = (bf16[8,4224]{1,0:T(8,128)(2,1)S(1)}, bf16[8,4224]{1,0:T(8,128)(2,1)S(1)}, u32[]{:S(2)}, u32[]{:S(2)}) collective-permute-start(bf16[8,4224]{1,0:T(8,128)(2,1)S(1)} %shard_map.64.refs_0_), channel_id=1, source_target_pairs={{0,2},{2,0},{4,6},{6,4},{8,10},{10,8},{12,14},{14,12},{1,3},{3,1},... | collective-permute-start | bytes 202760 | tf_op jit(solution)/shard_map/ppermute | solution.py:118
  21.0 2.1 %collective-permute-done.refs_1_ = bf16[8,4224]{1,0:T(8,128)(2,1)S(1)} collective-permute-done((bf16[8,4224]{1,0:T(8,128)(2,1)S(1)}, bf16[8,4224]{1,0:T(8,128)(2,1)S(1)}, u32[]{:S(2)}, u32[]{:S(2)}) %collective-permute-start) | collective-permute-done | bytes 67616 | tf_op jit(solution)/shard_map/ppermute | solution.py:118
  23.2 1.0 %shard_map.65 = (bf16[64,4096]{1,0:T(8,128)(2,1)S(1)}, f32[64,128]{1,0:T(8,128)S(1)}, f32[32,128]{1,0:T(8,128)S(1)}) custom-call(s32[8]{0:T(128)S(1)} %copy-done.3, bf16[64,4096]{1,0:T(8,128)(2,1)S(1)} %bitcast.3, bf16[8,4224]{1,0:T(8,128)(2,1)S(1)} %shard_map.64.refs_0_, bf16[8,4224]{1,0:T(8,128)(2,1)S(1)} %collective-permute-done.refs_1_, ...), custom_call_target="tpu_custom_call" | custom-call | flops 33554432 | tf_op jit(solution)/shard_map/pallas_call | solution.py:131
  24.2 1.2 %collective-permute-done.7.b = f32[32,128]{1,0:T(8,128)S(1)} collective-permute-done((f32[32,128]{1,0:T(8,128)S(1)}, f32[32,128]{1,0:T(8,128)S(1)}, u32[]{:S(2)}, u32[]{:S(2)}) %collective-permute-start.7) | collective-permute-done | bytes 16416 | tf_op jit(solution)/shard_map/ppermute | solution.py:115
  25.4 1.9 %collective-permute-start.8 = (f32[32,128]{1,0:T(8,128)S(1)}, f32[32,128]{1,0:T(8,128)S(1)}, u32[]{:S(2)}, u32[]{:S(2)}) collective-permute-start(f32[32,128]{1,0:T(8,128)S(1)} %shard_map.66.a._), channel_id=1, source_target_pairs={{0,2},{2,0},{4,6},{6,4},{8,10},{10,8},{12,14},{14,12},{1,3},{3,1},... | collective-permute-start | bytes 49160 | tf_op jit(solution)/shard_map/ppermute | solution.py:118
  27.3 1.6 %shard_map.71 = (f32[32,1024]{1,0:T(8,128)S(1)}, f32[32,1024]{1,0:T(8,128)S(1)}) custom-call(bf16[64,4096]{1,0:T(8,128)(2,1)S(1)} %get-tuple-element.18.x, bf16[4096,3584]{1,0:T(8,128)(2,1)S(1)} %copy-done, f32[32,128]{1,0:T(8,128)S(1)} %shard_map.66.a._), custom_call_target="tpu_custom_call" | custom-call | flops 536870912 | bytes 8388608 | tf_op jit(solution)/shard_map/pallas_call | solution.py:153
  29.2 1.6 %shard_map.72 = (f32[32,1024]{1,0:T(8,128)S(1)}, f32[32,1024]{1,0:T(8,128)S(1)}) custom-call(bf16[64,4096]{1,0:T(8,128)(2,1)S(1)} %get-tuple-element.18.x, bf16[4096,3584]{1,0:T(8,128)(2,1)S(1)} %copy-done, f32[32,128]{1,0:T(8,128)S(1)} %shard_map.67.a._), custom_call_target="tpu_custom_call" | custom-call | flops 536870912 | bytes 8388608 | tf_op jit(solution)/shard_map/pallas_call | solution.py:153
  31.2 1.6 %collective-permute-done.9.b = f32[32,128]{1,0:T(8,128)S(1)} collective-permute-done((f32[32,128]{1,0:T(8,128)S(1)}, f32[32,128]{1,0:T(8,128)S(1)}, u32[]{:S(2)}, u32[]{:S(2)}) %collective-permute-start.9) | collective-permute-done | bytes 16416 | tf_op jit(solution)/shard_map/ppermute | solution.py:118
  32.9 1.6 %shard_map.73 = (f32[32,1024]{1,0:T(8,128)S(1)}, f32[32,1024]{1,0:T(8,128)S(1)}) custom-call(bf16[64,4096]{1,0:T(8,128)(2,1)S(1)} %get-tuple-element.18.x, bf16[4096,3584]{1,0:T(8,128)(2,1)S(1)} %copy-done, f32[32,128]{1,0:T(8,128)S(1)} %shard_map.68.a._), custom_call_target="tpu_custom_call" | custom-call | flops 536870912 | bytes 8388608 | tf_op jit(solution)/shard_map/pallas_call | solution.py:153
  34.5 1.9 %collective-permute-start.10 = (f32[32,128]{1,0:T(8,128)S(1)}, f32[32,128]{1,0:T(8,128)S(1)}, u32[]{:S(2)}, u32[]{:S(2)}) collective-permute-start(f32[32,128]{1,0:T(8,128)S(1)} %shard_map.68.a._), channel_id=1, source_target_pairs={{0,8},{2,10},{4,12},{6,14},{8,0},{10,2},{12,4},{14,6},{1,9},{3,11}... | collective-permute-start | bytes 49160 | tf_op jit(solution)/shard_map/ppermute | solution.py:118
  36.4 0.9 %shard_map.70 = (f32[32,512]{1,0:T(8,128)S(1)}, f32[32,512]{1,0:T(8,128)S(1)}) custom-call(bf16[64,4096]{1,0:T(8,128)(2,1)S(1)} %get-tuple-element.18.x, bf16[4096,3584]{1,0:T(8,128)(2,1)S(1)} %copy-done, f32[32,128]{1,0:T(8,128)S(1)} %get-tuple-element.16.a._), custom_call_target="tpu_custom_call" | custom-call | flops 268435456 | bytes 4194304 | tf_op jit(solution)/shard_map/pallas_call | solution.py:153
  37.3 2.1 %collective-permute-done.10.b = f32[32,128]{1,0:T(8,128)S(1)} collective-permute-done((f32[32,128]{1,0:T(8,128)S(1)}, f32[32,128]{1,0:T(8,128)S(1)}, u32[]{:S(2)}, u32[]{:S(2)}) %collective-permute-start.10) | collective-permute-done | bytes 16416 | tf_op jit(solution)/shard_map/ppermute | solution.py:118
  39.4 1.2 %collective-permute-done.12.refs_4_ = f32[32,512]{1,0:T(8,128)S(1)} collective-permute-done((f32[32,512]{1,0:T(8,128)S(1)}, f32[32,512]{1,0:T(8,128)S(1)}, u32[]{:S(2)}, u32[]{:S(2)}) %collective-permute-start.12) | collective-permute-done | bytes 65568 | tf_op jit(solution)/shard_map/ppermute | solution.py:115
  40.7 1.6 %shard_map.74 = bf16[32,3584]{1,0:T(8,128)(2,1)} custom-call(f32[32,128]{1,0:T(8,128)S(1)} %shard_map.69.low, f32[64,128]{1,0:T(8,128)S(1)} %get-tuple-element.17.ids, bf16[8,32,3584]{2,1,0:T(8,128)(2,1)S(1)} %copy-done.1, bf16[8,32,3584]{2,1,0:T(8,128)(2,1)S(1)} %collective-permute-done.11.up_peer, f32[32,512]{1,0:T(8,128)S(1)} %get-tuple-element.19.refs_0_, ...), custom_call_target="tpu_custom_call" | custom-call | tf_op jit(solution)/shard_map/pallas_call | solution.py:165
  (31 shorter events, 1.8 us)
Async XLA Ops:
  0.0 23.2 %copy-start.2 = (bf16[1,4096,64]{1,2,0:T(8,128)(2,1)S(1)}, bf16[1,4096,64]{1,2,0:T(8,128)(2,1)}, u32[]{:S(2)}) copy-start(bf16[1,4096,64]{1,2,0:T(8,128)(2,1)} %param.10) | copy-start | bytes 1572868
  0.0 23.2 %copy-start.3 = (s32[8]{0:T(128)S(1)}, s32[8]{0:T(128)}, u32[]{:S(2)}) copy-start(s32[8]{0:T(128)} %holder.1) | copy-start | bytes 100
  0.0 40.7 %collective-permute-start.11 = (bf16[8,32,3584]{2,1,0:T(8,128)(2,1)}, bf16[8,32,3584]{2,1,0:T(8,128)(2,1)S(1)}, u32[]{:S(2)}, u32[]{:S(2)}) collective-permute-start(bf16[8,32,3584]{2,1,0:T(8,128)(2,1)} %up_own.1), channel_id=1, source_target_pairs={{0,1},{1,0},{2,3},{3,2},{4,5},{5,4},{6,7},{7,6},{8,9},{9,8},{10,11... | collective-permute-start | bytes 5505032 | tf_op jit(solution)/shard_map/ppermute | solution.py:115
  0.5 0.8 %copy-start.4 = (bf16[8,4096]{1,0:T(8,128)(2,1)S(1)}, bf16[8,4096]{1,0:T(8,128)(2,1)}, u32[]{:S(2)}) copy-start(bf16[8,4096]{1,0:T(8,128)(2,1)} %tokens.1) | copy-start | bytes 196612
  1.3 0.7 %copy-start.5 = (s32[8]{0:T(128)S(1)}, s32[8]{0:T(128)}, u32[]{:S(2)}) copy-start(s32[8]{0:T(128)} %ids.1) | copy-start | bytes 100
  2.0 25.3 %copy-start = (bf16[4096,3584]{1,0:T(8,128)(2,1)S(1)}, bf16[4096,3584]{1,0:T(8,128)(2,1)}, u32[]{:S(2)}) copy-start(bf16[4096,3584]{1,0:T(8,128)(2,1)} %w.7) | copy-start | bytes 88080384
  2.5 8.7 %collective-permute-start.6 = (bf16[8,4224]{1,0:T(8,128)(2,1)S(1)}, bf16[8,4224]{1,0:T(8,128)(2,1)S(1)}, u32[]{:S(2)}, u32[]{:S(2)}) collective-permute-start(bf16[8,4224]{1,0:T(8,128)(2,1)S(1)} %shard_map.64.refs_0_), channel_id=1, source_target_pairs={{0,14},{2,12},{4,10},{6,8},{8,6},{10,4},{12,2},{14,0},{1,15},{3,13... | collective-permute-start | bytes 202760 | tf_op jit(solution)/shard_map/ppermute | solution.py:118
  8.2 6.9 %collective-permute-start.5 = (bf16[8,4224]{1,0:T(8,128)(2,1)S(1)}, bf16[8,4224]{1,0:T(8,128)(2,1)S(1)}, u32[]{:S(2)}, u32[]{:S(2)}) collective-permute-start(bf16[8,4224]{1,0:T(8,128)(2,1)S(1)} %shard_map.64.refs_0_), channel_id=1, source_target_pairs={{0,12},{2,14},{4,8},{6,10},{8,4},{10,6},{12,0},{14,2},{1,13},{3,15... | collective-permute-start | bytes 202760 | tf_op jit(solution)/shard_map/ppermute | solution.py:118
  8.4 10.5 %collective-permute-start.4 = (bf16[8,4224]{1,0:T(8,128)(2,1)S(1)}, bf16[8,4224]{1,0:T(8,128)(2,1)S(1)}, u32[]{:S(2)}, u32[]{:S(2)}) collective-permute-start(bf16[8,4224]{1,0:T(8,128)(2,1)S(1)} %shard_map.64.refs_0_), channel_id=1, source_target_pairs={{0,10},{2,8},{4,14},{6,12},{8,2},{10,0},{12,6},{14,4},{1,11},{3,9}... | collective-permute-start | bytes 202760 | tf_op jit(solution)/shard_map/ppermute | solution.py:118
  9.2 11.6 %collective-permute-start.3 = (bf16[8,4224]{1,0:T(8,128)(2,1)S(1)}, bf16[8,4224]{1,0:T(8,128)(2,1)S(1)}, u32[]{:S(2)}, u32[]{:S(2)}) collective-permute-start(bf16[8,4224]{1,0:T(8,128)(2,1)S(1)} %shard_map.64.refs_0_), channel_id=1, source_target_pairs={{0,8},{2,10},{4,12},{6,14},{8,0},{10,2},{12,4},{14,6},{1,9},{3,11}... | collective-permute-start | bytes 202760 | tf_op jit(solution)/shard_map/ppermute | solution.py:118
  11.2 9.6 %collective-permute-start.2 = (bf16[8,4224]{1,0:T(8,128)(2,1)S(1)}, bf16[8,4224]{1,0:T(8,128)(2,1)S(1)}, u32[]{:S(2)}, u32[]{:S(2)}) collective-permute-start(bf16[8,4224]{1,0:T(8,128)(2,1)S(1)} %shard_map.64.refs_0_), channel_id=1, source_target_pairs={{0,6},{2,4},{4,2},{6,0},{8,14},{10,12},{12,10},{14,8},{1,7},{3,5},... | collective-permute-start | bytes 202760 | tf_op jit(solution)/shard_map/ppermute | solution.py:118
  15.1 5.9 %collective-permute-start.1 = (bf16[8,4224]{1,0:T(8,128)(2,1)S(1)}, bf16[8,4224]{1,0:T(8,128)(2,1)S(1)}, u32[]{:S(2)}, u32[]{:S(2)}) collective-permute-start(bf16[8,4224]{1,0:T(8,128)(2,1)S(1)} %shard_map.64.refs_0_), channel_id=1, source_target_pairs={{0,4},{2,6},{4,0},{6,2},{8,12},{10,14},{12,8},{14,10},{1,5},{3,7},... | collective-permute-start | bytes 202760 | tf_op jit(solution)/shard_map/ppermute | solution.py:118
  18.9 4.3 %collective-permute-start = (bf16[8,4224]{1,0:T(8,128)(2,1)S(1)}, bf16[8,4224]{1,0:T(8,128)(2,1)S(1)}, u32[]{:S(2)}, u32[]{:S(2)}) collective-permute-start(bf16[8,4224]{1,0:T(8,128)(2,1)S(1)} %shard_map.64.refs_0_), channel_id=1, source_target_pairs={{0,2},{2,0},{4,6},{6,4},{8,10},{10,8},{12,14},{14,12},{1,3},{3,1},... | collective-permute-start | bytes 202760 | tf_op jit(solution)/shard_map/ppermute | solution.py:118
  24.2 1.2 %collective-permute-start.7 = (f32[32,128]{1,0:T(8,128)S(1)}, f32[32,128]{1,0:T(8,128)S(1)}, u32[]{:S(2)}, u32[]{:S(2)}) collective-permute-start(f32[32,128]{1,0:T(8,128)S(1)} %get-tuple-element.16.a._), channel_id=1, source_target_pairs={{0,1},{1,0},{2,3},{3,2},{4,5},{5,4},{6,7},{7,6},{8,9},{9,8},{10,11... | collective-permute-start | bytes 49160 | tf_op jit(solution)/shard_map/ppermute | solution.py:115
  25.4 3.7 %collective-permute-start.8 = (f32[32,128]{1,0:T(8,128)S(1)}, f32[32,128]{1,0:T(8,128)S(1)}, u32[]{:S(2)}, u32[]{:S(2)}) collective-permute-start(f32[32,128]{1,0:T(8,128)S(1)} %shard_map.66.a._), channel_id=1, source_target_pairs={{0,2},{2,0},{4,6},{6,4},{8,10},{10,8},{12,14},{14,12},{1,3},{3,1},... | collective-permute-start | bytes 49160 | tf_op jit(solution)/shard_map/ppermute | solution.py:118
  28.9 11.8 %collective-permute-start.13 = (f32[32,1024]{1,0:T(8,128)S(1)}, f32[32,1024]{1,0:T(8,128)S(1)}, u32[]{:S(2)}, u32[]{:S(2)}) collective-permute-start(f32[32,1024]{1,0:T(8,128)S(1)} %get-tuple-element.24), channel_id=1, source_target_pairs={{0,1},{1,0},{2,3},{3,2},{4,5},{5,4},{6,7},{7,6},{8,9},{9,8},{10,11... | collective-permute-start | bytes 393224 | tf_op jit(solution)/shard_map/ppermute | solution.py:115
  29.1 3.7 %collective-permute-start.9 = (f32[32,128]{1,0:T(8,128)S(1)}, f32[32,128]{1,0:T(8,128)S(1)}, u32[]{:S(2)}, u32[]{:S(2)}) collective-permute-start(f32[32,128]{1,0:T(8,128)S(1)} %shard_map.67.a._), channel_id=1, source_target_pairs={{0,4},{2,6},{4,0},{6,2},{8,12},{10,14},{12,8},{14,10},{1,5},{3,7},... | collective-permute-start | bytes 49160 | tf_op jit(solution)/shard_map/ppermute | solution.py:118
  30.8 9.9 %collective-permute-start.14 = (f32[32,1024]{1,0:T(8,128)S(1)}, f32[32,1024]{1,0:T(8,128)S(1)}, u32[]{:S(2)}, u32[]{:S(2)}) collective-permute-start(f32[32,1024]{1,0:T(8,128)S(1)} %get-tuple-element.25), channel_id=1, source_target_pairs={{0,1},{1,0},{2,3},{3,2},{4,5},{5,4},{6,7},{7,6},{8,9},{9,8},{10,11... | collective-permute-start | bytes 393224 | tf_op jit(solution)/shard_map/ppermute | solution.py:115
  34.5 6.2 %copy-start.1 = (bf16[8,32,3584]{2,1,0:T(8,128)(2,1)S(1)}, bf16[8,32,3584]{2,1,0:T(8,128)(2,1)}, u32[]{:S(2)}) copy-start(bf16[8,32,3584]{2,1,0:T(8,128)(2,1)} %up_own.1) | copy-start | bytes 5505028
  34.5 6.2 %collective-permute-start.15 = (f32[32,1024]{1,0:T(8,128)S(1)}, f32[32,1024]{1,0:T(8,128)S(1)}, u32[]{:S(2)}, u32[]{:S(2)}) collective-permute-start(f32[32,1024]{1,0:T(8,128)S(1)} %get-tuple-element.26), channel_id=1, source_target_pairs={{0,1},{1,0},{2,3},{3,2},{4,5},{5,4},{6,7},{7,6},{8,9},{9,8},{10,11... | collective-permute-start | bytes 393224 | tf_op jit(solution)/shard_map/ppermute | solution.py:115
  34.5 4.8 %collective-permute-start.10 = (f32[32,128]{1,0:T(8,128)S(1)}, f32[32,128]{1,0:T(8,128)S(1)}, u32[]{:S(2)}, u32[]{:S(2)}) collective-permute-start(f32[32,128]{1,0:T(8,128)S(1)} %shard_map.68.a._), channel_id=1, source_target_pairs={{0,8},{2,10},{4,12},{6,14},{8,0},{10,2},{12,4},{14,6},{1,9},{3,11}... | collective-permute-start | bytes 49160 | tf_op jit(solution)/shard_map/ppermute | solution.py:118
  39.4 1.3 %collective-permute-start.12 = (f32[32,512]{1,0:T(8,128)S(1)}, f32[32,512]{1,0:T(8,128)S(1)}, u32[]{:S(2)}, u32[]{:S(2)}) collective-permute-start(f32[32,512]{1,0:T(8,128)S(1)} %get-tuple-element.23), channel_id=1, source_target_pairs={{0,1},{1,0},{2,3},{3,2},{4,5},{5,4},{6,7},{7,6},{8,9},{9,8},{10,11... | collective-permute-start | bytes 196616 | tf_op jit(solution)/shard_map/ppermute | solution.py:115

commit v2 on v1

--- a/solution.py
+++ b/solution.py
@@ -11,7 +11,10 @@
 F32, BF16 = jnp.float32, jnp.bfloat16
 VMEM = pl.BlockSpec(memory_space=pltpu.VMEM)
 SMEM = pl.BlockSpec(memory_space=pltpu.SMEM)
+HBM = pl.BlockSpec(memory_space=pltpu.HBM)
+ANY = pl.BlockSpec(memory_space=pl.ANY)
 LANES = 128
+SPLITS = {2: (20, 28), 3: (10, 22, 28), 4: (5, 14, 24, 28)}
 
 
 def call(kernel, out, in_specs, vmem, scratch=(), flops=0, bytes_accessed=0, aliases=None):
@@ -32,24 +35,44 @@
     return pltpu.with_memory_space_constraint(array, pltpu.VMEM)
 
 
-def pack_kernel(ids, tokens, message):
+def far(array):
+    return pltpu.with_memory_space_constraint(array, pltpu.HBM)
+
+
+def pack_kernel(ids_far, tokens, message, ids, sems):
     rows, wide = tokens.shape
-    message[:, :wide] = tokens[...]
+    copies = [
+        pltpu.make_async_copy(ids_far, ids, sems.at[0]),
+        pltpu.make_async_copy(tokens, message.at[0, :, pl.ds(0, wide)], sems.at[1]),
+    ]
+    for copy in copies:
+        copy.start()
+    copies[0].wait()
     place = lax.broadcasted_iota(jnp.int32, (rows, LANES), 0)
     value = jnp.zeros((rows, LANES), jnp.int32)
     for i in range(rows):
         value = jnp.where(place == i, ids[i], value)
-    message[:, wide:] = value.astype(F32).astype(BF16)
-
-
-def assemble_kernel(n, holder, down, *refs):
-    blocks, (x, ids, low, stage, id_stage) = refs[:n], refs[n:]
-    rows, wide = blocks[0].shape[0], x.shape[1]
+    message[0, :, wide:] = value.astype(F32).astype(BF16)
+    copies[1].wait()
+
+
+def join_kernel(*refs):
+    at = 0
+    for part in refs[:-1]:
+        for i in range(part.shape[0]):
+            refs[-1][at] = part[i]
+            at += 1
+
+
+def assemble_kernel(order, holder, down, *refs):
+    parts, (x, ids, low, stage, id_stage) = refs[: len(order)], refs[len(order) :]
+    n, rows, wide = stage.shape
     me = lax.axis_index("ffn")
-    for k in range(n):
-        at = jnp.bitwise_xor(me, k)
-        stage[at] = blocks[k][:, :wide].astype(F32)
-        id_stage[at] = blocks[k][:, wide:].astype(F32)
+    for part, sources in zip(parts, order):
+        for i, k in enumerate(sources):
+            at = jnp.bitwise_xor(me, k)
+            stage[at] = part[i, :, :wide].astype(F32)
+            id_stage[at] = part[i, :, wide:].astype(F32)
     whole = stage[...].reshape(n * rows, wide).astype(BF16)
     x[...] = whole
     row_ids = id_stage[...].reshape(n * rows, LANES)
@@ -63,7 +86,7 @@
     low[...] = jnp.concatenate([part[:half], part[half:]], axis=1)
 
 
-def add_kernel(a, b, out):
+def add_kernel(a, b, _, out):
     out[...] = a[...] + b[...]
 
 
@@ -105,11 +128,34 @@
         c += s
 
 
+def gather(n, message, partner):
+    rows, wide = message.shape[1:]
+
+    def join(parts):
+        count = sum(p.shape[0] for p in parts)
+        return call(
+            join_kernel, jax.ShapeDtypeStruct((count, rows, wide), BF16), [VMEM] * len(parts), 1 << 20
+        )(*parts)
+
+    if n == 2:
+        return [message, partner(message, 1)], [[0], [1]]
+    if n == 4:
+        second, first = partner(message, 2), partner(message, 1)
+        return [message, second, first, partner(second, 1)], [[0], [2], [1], [3]]
+    first, second, fourth = partner(message, 1), partner(message, 2), partner(message, 4)
+    sixth = partner(fourth, 2)
+    near = partner(join([second, fourth]), 1)
+    sixth_after, _ = lax.optimization_barrier((sixth, first))
+    far = partner(sixth_after, 1)
+    return [message, first, second, fourth, sixth, near, far], [[0], [1], [2], [4], [6], [3, 5], [7]]
+
+
 def small(n, tokens, base_up_weight, row_ids, holder, pool, table):
     rows, wide = tokens.shape
     columns = base_up_weight.shape[1]
     rank = pool.shape[2]
     half = n * rows // 2
+    both = ("ffn", "width")
 
     def swap(v):
         return lax.ppermute(v, "width", [(0, 1), (1, 0)])
@@ -117,50 +163,53 @@
     def partner(v, k):
         return lax.ppermute(v, "ffn", [(i, i ^ k) for i in range(n)])
 
+    def across(v, k):
+        return lax.ppermute(v, both, [(2 * i + w, 2 * (i ^ k) + 1 - w) for i in range(n) for w in range(2)])
+
     weight = pinned(base_up_weight)
-    up_own = pinned(table)
-    up_peer = pinned(swap(table))
     down = pinned(jnp.swapaxes(pool[0], 0, 1))
 
     message = call(
-        pack_kernel, jax.ShapeDtypeStruct((rows, wide + LANES), BF16), [SMEM, VMEM], 1 << 20,
-        flops=40 << 30, bytes_accessed=1 << 17,
-    )(row_ids, tokens)
-    blocks = [message] + [partner(message, k) for k in range(1, n)]
+        pack_kernel, jax.ShapeDtypeStruct((1, rows, wide + LANES), BF16), [HBM, HBM], 1 << 20,
+        scratch=[pltpu.SMEM((rows,), jnp.int32), pltpu.SemaphoreType.DMA((2,))], flops=40 << 30, bytes_accessed=1 << 17,
+    )(far(row_ids), far(tokens))
+    parts, order = gather(n, message, partner)
 
     x, ids, low = call(
-        functools.partial(assemble_kernel, n),
+        functools.partial(assemble_kernel, order),
         [
             jax.ShapeDtypeStruct((n * rows, wide), BF16),
             jax.ShapeDtypeStruct((n * rows, LANES), F32),
             jax.ShapeDtypeStruct((half, 2 * rank), F32),
         ],
-        [SMEM, VMEM] + [VMEM] * n,
+        [SMEM, VMEM] + [VMEM] * len(parts),
         6 << 20,
         scratch=[pltpu.VMEM((n, rows, wide), F32), pltpu.VMEM((n, rows, LANES), F32)],
-        flops=1 << 25,
-    )(holder, down, *blocks)
-
-    def add(a, b):
-        return call(add_kernel, jax.ShapeDtypeStruct(a.shape, F32), [VMEM, VMEM], 1 << 20)(a, b)
-
-    steps = [swap] + [functools.partial(partner, k=1 << i) for i in range(n.bit_length() - 1)]
+    )(holder, down, *parts)
+
+    def add(a, b, after):
+        return call(add_kernel, jax.ShapeDtypeStruct(a.shape, F32), [VMEM, VMEM, ANY], 1 << 20)(a, b, after)
+
+    steps = [swap] + [functools.partial(across, k=1 << i) for i in range(n.bit_length() - 1)]
     units = columns // LANES
-    cuts = [0] + [LANES * (units * (2 * i + 1) // (2 * len(steps) - 1)) for i in range(len(steps))]
-    own, got = [], []
+    cuts = [0] + [LANES * (units * c // 28) for c in SPLITS[len(steps)]]
+    own, got, up_own, up_peer = [], [], pinned(table), None
     for step, a, b in zip(steps, cuts[:-1], cuts[1:]):
         other = step(low)
         o, s = call(
             functools.partial(base_kernel, a, 512),
             [jax.ShapeDtypeStruct((half, b - a), F32), jax.ShapeDtypeStruct((half, b - a), F32)],
-            [VMEM, VMEM, VMEM],
+            [VMEM, VMEM, ANY],
             4 << 20,
-            flops=2 * 2 * half * wide * (b - a),
-            bytes_accessed=2 * wide * (b - a),
         )(x, weight, low)
         own.append(o)
+        low = add(low, other, o)
+        if len(own) < len(steps):
+            s, low = lax.optimization_barrier((s, low))
         got.append(swap(s))
-        low = add(low, other)
+        if len(own) == 1:
+            table, low = lax.optimization_barrier((table, low))
+            up_peer = pinned(swap(table))
 
     return call(
         functools.partial(finish_kernel, len(own)),

time: 42.4 us -> 34.3 us (0.81)
  waiting for transfers between devices: 11.1 us -> 5.4 us
  starting transfers between devices: 20.8 us -> 19.2 us
  local copies, waits for them, and re-layouts: 1.51 us -> 0.35 us
    ppermute x10 -> x6, starting transfers between devices: 19.7 us -> 12 us  [partner(): return lax.ppermute(v, 'ffn', [(i, i ^ k) for i in range(n)])]
    ppermute x0 -> x3, starting transfers between devices: none -> 5.61 us  [across(): lax.ppermute(v, both, [(2 * i + w, 2 * (i ^ k) + 1 - w) for i in range(n)...]
    ppermute x10 -> x6, waiting for transfers between devices: 8.63 us -> 3.74 us  [partner(): return lax.ppermute(v, 'ffn', [(i, i ^ k) for i in range(n)])]
    ppermute x6, waiting for transfers between devices: 2.43 us -> 1.15 us  [swap(): return lax.ppermute(v, 'width', [(0, 1), (1, 0)])]
    unnamed x12 -> x8, local copies, waits for them, and re-layouts: 1.51 us -> 0.35 us
    ppermute x0 -> x3, waiting for transfers between devices: none -> 0.52 us  [across(): lax.ppermute(v, both, [(2 * i + w, 2 * (i ^ k) + 1 - w) for i in range(n)...]
    ppermute x6, starting transfers between devices: 1.06 us -> 1.54 us  [swap(): return lax.ppermute(v, 'width', [(0, 1), (1, 0)])]
    pallas_call x6 -> x7, Pallas kernels: 1.56 us -> 2.01 us  [the longest x1 1.01 us: small(): call(pack_kernel, jax.ShapeDtypeStruct((1, rows, wide + LANES), BF16), [H...]
  transfers between devices with their start and end apart: 16 -> 15, of which waited for: 9 -> 6; matrix products, arithmetic and copies ran while one was open for 0% -> 0% of each run, Pallas kernels for 17% -> 16%
where the time goes in v2:
time: 34.3 us; the launch traced here: 34.1 us
  starting transfers between devices  19.2 us (56%)
  Pallas kernels  9.07 us (26%)
  waiting for transfers between devices  5.4 us (16%)
  local copies, waits for them, and re-layouts  0.35 us (1%)
    ppermute x6, starting transfers between devices, partner(): return lax.ppermute(v, 'ffn', [(i, i ^ k) for i in range(n)])  12 us
    ppermute x3, starting transfers between devices, across(): lax.ppermute(v, both, [(2 * i + w, 2 * (i ^ k) + 1 - w) for i in range(n)...  5.61 us
    pallas_call x4, Pallas kernels, small(): call(functools.partial(base_kernel, a, 512), [jax.ShapeDtypeStruct((half,...  5.49 us
    ppermute x6, waiting for transfers between devices, partner(): return lax.ppermute(v, 'ffn', [(i, i ^ k) for i in range(n)])  3.74 us
    pallas_call x1, Pallas kernels, small(): call(functools.partial(finish_kernel, len(own)), jax.ShapeDtypeStruct((ha...  1.57 us
    ppermute x6, starting transfers between devices, swap(): return lax.ppermute(v, 'width', [(0, 1), (1, 0)])  1.54 us
    ppermute x6, waiting for transfers between devices, swap(): return lax.ppermute(v, 'width', [(0, 1), (1, 0)])  1.15 us
    pallas_call x1, Pallas kernels, small(): call(pack_kernel, jax.ShapeDtypeStruct((1, rows, wide + LANES), BF16), [H...  1.01 us
  transfers between devices with their start and end apart: 15, of which 6 were waited for; matrix products, arithmetic and copies ran while one was open for 0% of the time, Pallas kernels for 16%

profile of v2, /device:TPU:0, one launch (start us, length us, event | category | flops | bytes accessed | tf_op | source)
XLA Modules:
  0.0 34.1 jit_solution(8508308368190008711)
XLA Ops:
  0.0 1.0 %shard_map.64.refs_0_ = bf16[1,8,4224]{2,1,0:T(8,128)(2,1)S(1)} custom-call(s32[8]{0:T(128)} %ids_far.1, bf16[8,4096]{1,0:T(8,128)(2,1)} %tokens.1), custom_call_target="tpu_custom_call" | custom-call | flops 42949672960 | bytes 131072 | tf_op jit(solution)/shard_map/pallas_call | solution.py:172
  1.0 4.1 %collective-permute-start.2 = (bf16[1,8,4224]{2,1,0:T(8,128)(2,1)S(1)}, bf16[1,8,4224]{2,1,0:T(8,128)(2,1)S(1)}, u32[]{:S(2)}, u32[]{:S(2)}) collective-permute-start(bf16[1,8,4224]{2,1,0:T(8,128)(2,1)S(1)} %shard_map.64.refs_0_), channel_id=1, source_target_pairs={{0,8},{2,10},{4,12},{6,14},{8,0},{10,2},{12,4},{14,6},{1,9},{3,11}... | collective-permute-start | bytes 202760 | tf_op jit(solution)/shard_map/ppermute | solution.py:164
  5.1 1.6 %collective-permute-start.1 = (bf16[1,8,4224]{2,1,0:T(8,128)(2,1)S(1)}, bf16[1,8,4224]{2,1,0:T(8,128)(2,1)S(1)}, u32[]{:S(2)}, u32[]{:S(2)}) collective-permute-start(bf16[1,8,4224]{2,1,0:T(8,128)(2,1)S(1)} %shard_map.64.refs_0_), channel_id=1, source_target_pairs={{0,4},{2,6},{4,0},{6,2},{8,12},{10,14},{12,8},{14,10},{1,5},{3,7},... | collective-permute-start | bytes 202760 | tf_op jit(solution)/shard_map/ppermute | solution.py:164
  6.7 1.5 %collective-permute-start = (bf16[1,8,4224]{2,1,0:T(8,128)(2,1)S(1)}, bf16[1,8,4224]{2,1,0:T(8,128)(2,1)S(1)}, u32[]{:S(2)}, u32[]{:S(2)}) collective-permute-start(bf16[1,8,4224]{2,1,0:T(8,128)(2,1)S(1)} %shard_map.64.refs_0_), channel_id=1, source_target_pairs={{0,2},{2,0},{4,6},{6,4},{8,10},{10,8},{12,14},{14,12},{1,3},{3,1},... | collective-permute-start | bytes 202760 | tf_op jit(solution)/shard_map/ppermute | solution.py:164
  8.2 1.4 %collective-permute-start.3 = (bf16[1,8,4224]{2,1,0:T(8,128)(2,1)S(1)}, bf16[1,8,4224]{2,1,0:T(8,128)(2,1)S(1)}, u32[]{:S(2)}, u32[]{:S(2)}) collective-permute-start(bf16[1,8,4224]{2,1,0:T(8,128)(2,1)S(1)} %collective-permute-done.2.refs_1_.refs_3_), channel_id=1, source_target_pairs={{0,4},{2,6},{4,0},{6,2},{8,12},{10,14},{12,8},{14,10},{1,5},{3,7},... | collective-permute-start | bytes 202760 | tf_op jit(solution)/shard_map/ppermute | solution.py:164
  9.6 1.6 %collective-permute-start.4 = (bf16[2,8,4224]{2,1,0:T(8,128)(2,1)S(1)}, bf16[2,8,4224]{2,1,0:T(8,128)(2,1)S(1)}, u32[]{:S(2)}, u32[]{:S(2)}) collective-permute-start(bf16[2,8,4224]{2,1,0:T(8,128)(2,1)S(1)} %shard_map.65), channel_id=1, source_target_pairs={{0,2},{2,0},{4,6},{6,4},{8,10},{10,8},{12,14},{14,12},{1,3},{3,1},... | collective-permute-start | bytes 405512 | tf_op jit(solution)/shard_map/ppermute | solution.py:164
  11.2 1.3 %collective-permute-done.3.refs_4_ = bf16[1,8,4224]{2,1,0:T(8,128)(2,1)S(1)} collective-permute-done((bf16[1,8,4224]{2,1,0:T(8,128)(2,1)S(1)}, bf16[1,8,4224]{2,1,0:T(8,128)(2,1)S(1)}, u32[]{:S(2)}, u32[]{:S(2)}) %collective-permute-start.3) | collective-permute-done | bytes 67616 | tf_op jit(solution)/shard_map/ppermute | solution.py:164
  12.5 1.9 %collective-permute-start.5 = (bf16[1,8,4224]{2,1,0:T(8,128)(2,1)S(1)}, bf16[1,8,4224]{2,1,0:T(8,128)(2,1)S(1)}, u32[]{:S(2)}, u32[]{:S(2)}) collective-permute-start(bf16[1,8,4224]{2,1,0:T(8,128)(2,1)S(1)} %collective-permute-done.3.refs_4_), channel_id=1, source_target_pairs={{0,2},{2,0},{4,6},{6,4},{8,10},{10,8},{12,14},{14,12},{1,3},{3,1},... | collective-permute-start | bytes 202760 | tf_op jit(solution)/shard_map/ppermute | solution.py:164
  14.4 2.4 %collective-permute-done.5.refs_6_ = bf16[1,8,4224]{2,1,0:T(8,128)(2,1)S(1)} collective-permute-done((bf16[1,8,4224]{2,1,0:T(8,128)(2,1)S(1)}, bf16[1,8,4224]{2,1,0:T(8,128)(2,1)S(1)}, u32[]{:S(2)}, u32[]{:S(2)}) %collective-permute-start.5) | collective-permute-done | bytes 67616 | tf_op jit(solution)/shard_map/ppermute | solution.py:164
  16.8 1.0 %shard_map.66 = (bf16[64,4096]{1,0:T(8,128)(2,1)S(1)}, f32[64,128]{1,0:T(8,128)S(1)}, f32[32,128]{1,0:T(8,128)S(1)}) custom-call(s32[8]{0:T(128)S(1)} %copy-done.3, bf16[64,4096]{1,0:T(8,128)(2,1)S(1)} %bitcast.3, bf16[1,8,4224]{2,1,0:T(8,128)(2,1)S(1)} %shard_map.64.refs_0_, bf16[1,8,4224]{2,1,0:T(8,128)(2,1)S(1)} %collective-permute-done.refs_1_, ...), custom_call_target="tpu_custom_call" | custom-call | tf_op jit(solution)/shard_map/pallas_call | solution.py:178
  17.8 1.0 %shard_map.67 = (f32[32,640]{1,0:T(8,128)S(1)}, f32[32,640]{1,0:T(8,128)S(1)}) custom-call(bf16[64,4096]{1,0:T(8,128)(2,1)S(1)} %get-tuple-element.26.x, bf16[4096,3584]{1,0:T(8,128)(2,1)S(1)} %copy-done, f32[32,128]{1,0:T(8,128)S(1)} %get-tuple-element.27._.a), custom_call_target="tpu_custom_call" | custom-call | tf_op jit(solution)/shard_map/pallas_call | solution.py:199
  19.0 0.3 copy-done.1
  19.3 0.5 %collective-permute-start.10 = (bf16[8,32,3584]{2,1,0:T(8,128)(2,1)S(1)}, bf16[8,32,3584]{2,1,0:T(8,128)(2,1)S(1)}, u32[]{:S(2)}, u32[]{:S(2)}) collective-permute-start(bf16[8,32,3584]{2,1,0:T(8,128)(2,1)S(1)} %copy-done.1), channel_id=1, source_target_pairs={{0,1},{1,0},{2,3},{3,2},{4,5},{5,4},{6,7},{7,6},{8,9},{9,8},{10,11... | collective-permute-start | bytes 5505032 | tf_op jit(solution)/shard_map/ppermute | solution.py:161
  19.8 1.5 %collective-permute-start.7 = (f32[32,128]{1,0:T(8,128)S(1)}, f32[32,128]{1,0:T(8,128)S(1)}, u32[]{:S(2)}, u32[]{:S(2)}) collective-permute-start(f32[32,128]{1,0:T(8,128)S(1)} %shard_map.68._.a), channel_id=1, source_target_pairs={{0,3},{1,2},{2,1},{3,0},{4,7},{5,6},{6,5},{7,4},{8,11},{9,10},{10,... | collective-permute-start | bytes 49160 | tf_op jit(solution)/shard_map/ppermute | solution.py:167
  21.3 1.7 %shard_map.69 = (f32[32,1152]{1,0:T(8,128)S(1)}, f32[32,1152]{1,0:T(8,128)S(1)}) custom-call(bf16[64,4096]{1,0:T(8,128)(2,1)S(1)} %get-tuple-element.26.x, bf16[4096,3584]{1,0:T(8,128)(2,1)S(1)} %copy-done, f32[32,128]{1,0:T(8,128)S(1)} %shard_map.68._.a), custom_call_target="tpu_custom_call" | custom-call | tf_op jit(solution)/shard_map/pallas_call | solution.py:199
  23.1 1.1 %collective-permute-start.8 = (f32[32,128]{1,0:T(8,128)S(1)}, f32[32,128]{1,0:T(8,128)S(1)}, u32[]{:S(2)}, u32[]{:S(2)}) collective-permute-start(f32[32,128]{1,0:T(8,128)S(1)} %shard_map.70._.a), channel_id=1, source_target_pairs={{0,5},{1,4},{2,7},{3,6},{4,1},{5,0},{6,3},{7,2},{8,13},{9,12},{10,... | collective-permute-start | bytes 49160 | tf_op jit(solution)/shard_map/ppermute | solution.py:167
  24.2 1.9 %shard_map.71 = (f32[32,1280]{1,0:T(8,128)S(1)}, f32[32,1280]{1,0:T(8,128)S(1)}) custom-call(bf16[64,4096]{1,0:T(8,128)(2,1)S(1)} %get-tuple-element.26.x, bf16[4096,3584]{1,0:T(8,128)(2,1)S(1)} %copy-done, f32[32,128]{1,0:T(8,128)S(1)} %shard_map.70._.a), custom_call_target="tpu_custom_call" | custom-call | tf_op jit(solution)/shard_map/pallas_call | solution.py:199
  26.3 0.5 %collective-permute-start.13 = (f32[32,1280]{1,0:T(8,128)S(1)}, f32[32,1280]{1,0:T(8,128)S(1)}, u32[]{:S(2)}, u32[]{:S(2)}) collective-permute-start(f32[32,1280]{1,0:T(8,128)S(1)} %get-tuple-element.43), channel_id=1, source_target_pairs={{0,1},{1,0},{2,3},{3,2},{4,5},{5,4},{6,7},{7,6},{8,9},{9,8},{10,11... | collective-permute-start | bytes 491528 | tf_op jit(solution)/shard_map/ppermute | solution.py:161
  26.9 2.9 %collective-permute-start.9 = (f32[32,128]{1,0:T(8,128)S(1)}, f32[32,128]{1,0:T(8,128)S(1)}, u32[]{:S(2)}, u32[]{:S(2)}) collective-permute-start(f32[32,128]{1,0:T(8,128)S(1)} %shard_map.72._.a), channel_id=1, source_target_pairs={{0,9},{1,8},{2,11},{3,10},{4,13},{5,12},{6,15},{7,14},{8,1},{9,0},... | collective-permute-start | bytes 49160 | tf_op jit(solution)/shard_map/ppermute | solution.py:167
  29.8 0.2 collective-permute-start.11
  30.1 0.8 %shard_map.73 = (f32[32,512]{1,0:T(8,128)S(1)}, f32[32,512]{1,0:T(8,128)S(1)}) custom-call(bf16[64,4096]{1,0:T(8,128)(2,1)S(1)} %get-tuple-element.26.x, bf16[4096,3584]{1,0:T(8,128)(2,1)S(1)} %copy-done, f32[32,128]{1,0:T(8,128)S(1)} %shard_map.72._.a), custom_call_target="tpu_custom_call" | custom-call | tf_op jit(solution)/shard_map/pallas_call | solution.py:199
  30.9 0.4 %collective-permute-done.9.b = f32[32,128]{1,0:T(8,128)S(1)} collective-permute-done((f32[32,128]{1,0:T(8,128)S(1)}, f32[32,128]{1,0:T(8,128)S(1)}, u32[]{:S(2)}, u32[]{:S(2)}) %collective-permute-start.9) | collective-permute-done | bytes 16416 | tf_op jit(solution)/shard_map/ppermute | solution.py:167
  31.5 1.0 %collective-permute-done.14.refs_7_ = f32[32,512]{1,0:T(8,128)S(1)} collective-permute-done((f32[32,512]{1,0:T(8,128)S(1)}, f32[32,512]{1,0:T(8,128)S(1)}, u32[]{:S(2)}, u32[]{:S(2)}) %collective-permute-start.14) | collective-permute-done | bytes 65568 | tf_op jit(solution)/shard_map/ppermute | solution.py:161
  32.5 1.6 %shard_map.75 = bf16[32,3584]{1,0:T(8,128)(2,1)} custom-call(f32[32,128]{1,0:T(8,128)S(1)} %shard_map.74.low, f32[64,128]{1,0:T(8,128)S(1)} %get-tuple-element.39.ids, bf16[8,32,3584]{2,1,0:T(8,128)(2,1)S(1)} %copy-done.1, bf16[8,32,3584]{2,1,0:T(8,128)(2,1)S(1)} %collective-permute-done.10.up_peer, f32[32,640]{1,0:T(8,128)S(1)} %get-tuple-element.29._.refs_0_, ...), custom_call_target="tpu_custom_call" | custom-call | tf_op jit(solution)/shard_map/pallas_call | solution.py:214
  (26 shorter events, 0.7 us)
Async XLA Ops:
  0.0 16.8 %copy-start.2 = (bf16[1,4096,64]{1,2,0:T(8,128)(2,1)S(1)}, bf16[1,4096,64]{1,2,0:T(8,128)(2,1)}, u32[]{:S(2)}) copy-start(bf16[1,4096,64]{1,2,0:T(8,128)(2,1)} %param.10) | copy-start | bytes 1572868
  0.0 16.8 %copy-start.3 = (s32[8]{0:T(128)S(1)}, s32[8]{0:T(128)}, u32[]{:S(2)}) copy-start(s32[8]{0:T(128)} %holder.1) | copy-start | bytes 100
  0.0 17.8 %copy-start = (bf16[4096,3584]{1,0:T(8,128)(2,1)S(1)}, bf16[4096,3584]{1,0:T(8,128)(2,1)}, u32[]{:S(2)}) copy-start(bf16[4096,3584]{1,0:T(8,128)(2,1)} %w.7) | copy-start | bytes 88080384
  1.0 7.2 %collective-permute-start.2 = (bf16[1,8,4224]{2,1,0:T(8,128)(2,1)S(1)}, bf16[1,8,4224]{2,1,0:T(8,128)(2,1)S(1)}, u32[]{:S(2)}, u32[]{:S(2)}) collective-permute-start(bf16[1,8,4224]{2,1,0:T(8,128)(2,1)S(1)} %shard_map.64.refs_0_), channel_id=1, source_target_pairs={{0,8},{2,10},{4,12},{6,14},{8,0},{10,2},{12,4},{14,6},{1,9},{3,11}... | collective-permute-start | bytes 202760 | tf_op jit(solution)/shard_map/ppermute | solution.py:164
  5.1 4.5 %collective-permute-start.1 = (bf16[1,8,4224]{2,1,0:T(8,128)(2,1)S(1)}, bf16[1,8,4224]{2,1,0:T(8,128)(2,1)S(1)}, u32[]{:S(2)}, u32[]{:S(2)}) collective-permute-start(bf16[1,8,4224]{2,1,0:T(8,128)(2,1)S(1)} %shard_map.64.refs_0_), channel_id=1, source_target_pairs={{0,4},{2,6},{4,0},{6,2},{8,12},{10,14},{12,8},{14,10},{1,5},{3,7},... | collective-permute-start | bytes 202760 | tf_op jit(solution)/shard_map/ppermute | solution.py:164
  6.7 4.5 %collective-permute-start = (bf16[1,8,4224]{2,1,0:T(8,128)(2,1)S(1)}, bf16[1,8,4224]{2,1,0:T(8,128)(2,1)S(1)}, u32[]{:S(2)}, u32[]{:S(2)}) collective-permute-start(bf16[1,8,4224]{2,1,0:T(8,128)(2,1)S(1)} %shard_map.64.refs_0_), channel_id=1, source_target_pairs={{0,2},{2,0},{4,6},{6,4},{8,10},{10,8},{12,14},{14,12},{1,3},{3,1},... | collective-permute-start | bytes 202760 | tf_op jit(solution)/shard_map/ppermute | solution.py:164
  8.2 4.3 %collective-permute-start.3 = (bf16[1,8,4224]{2,1,0:T(8,128)(2,1)S(1)}, bf16[1,8,4224]{2,1,0:T(8,128)(2,1)S(1)}, u32[]{:S(2)}, u32[]{:S(2)}) collective-permute-start(bf16[1,8,4224]{2,1,0:T(8,128)(2,1)S(1)} %collective-permute-done.2.refs_1_.refs_3_), channel_id=1, source_target_pairs={{0,4},{2,6},{4,0},{6,2},{8,12},{10,14},{12,8},{14,10},{1,5},{3,7},... | collective-permute-start | bytes 202760 | tf_op jit(solution)/shard_map/ppermute | solution.py:164
  9.6 7.2 %collective-permute-start.4 = (bf16[2,8,4224]{2,1,0:T(8,128)(2,1)S(1)}, bf16[2,8,4224]{2,1,0:T(8,128)(2,1)S(1)}, u32[]{:S(2)}, u32[]{:S(2)}) collective-permute-start(bf16[2,8,4224]{2,1,0:T(8,128)(2,1)S(1)} %shard_map.65), channel_id=1, source_target_pairs={{0,2},{2,0},{4,6},{6,4},{8,10},{10,8},{12,14},{14,12},{1,3},{3,1},... | collective-permute-start | bytes 405512 | tf_op jit(solution)/shard_map/ppermute | solution.py:164
  12.5 4.3 %collective-permute-start.5 = (bf16[1,8,4224]{2,1,0:T(8,128)(2,1)S(1)}, bf16[1,8,4224]{2,1,0:T(8,128)(2,1)S(1)}, u32[]{:S(2)}, u32[]{:S(2)}) collective-permute-start(bf16[1,8,4224]{2,1,0:T(8,128)(2,1)S(1)} %collective-permute-done.3.refs_4_), channel_id=1, source_target_pairs={{0,2},{2,0},{4,6},{6,4},{8,10},{10,8},{12,14},{14,12},{1,3},{3,1},... | collective-permute-start | bytes 202760 | tf_op jit(solution)/shard_map/ppermute | solution.py:164
  17.8 1.2 %collective-permute-start.6 = (f32[32,128]{1,0:T(8,128)S(1)}, f32[32,128]{1,0:T(8,128)S(1)}, u32[]{:S(2)}, u32[]{:S(2)}) collective-permute-start(f32[32,128]{1,0:T(8,128)S(1)} %get-tuple-element.27._.a), channel_id=1, source_target_pairs={{0,1},{1,0},{2,3},{3,2},{4,5},{5,4},{6,7},{7,6},{8,9},{9,8},{10,11... | collective-permute-start | bytes 49160 | tf_op jit(solution)/shard_map/ppermute | solution.py:161
  17.8 1.5 %copy-start.1 = (bf16[8,32,3584]{2,1,0:T(8,128)(2,1)S(1)}, bf16[8,32,3584]{2,1,0:T(8,128)(2,1)}, u32[]{:S(2)}) copy-start(bf16[8,32,3584]{2,1,0:T(8,128)(2,1)} %up_own.1) | copy-start | bytes 5505028
  19.3 13.2 %collective-permute-start.10 = (bf16[8,32,3584]{2,1,0:T(8,128)(2,1)S(1)}, bf16[8,32,3584]{2,1,0:T(8,128)(2,1)S(1)}, u32[]{:S(2)}, u32[]{:S(2)}) collective-permute-start(bf16[8,32,3584]{2,1,0:T(8,128)(2,1)S(1)} %copy-done.1), channel_id=1, source_target_pairs={{0,1},{1,0},{2,3},{3,2},{4,5},{5,4},{6,7},{7,6},{8,9},{9,8},{10,11... | collective-permute-start | bytes 5505032 | tf_op jit(solution)/shard_map/ppermute | solution.py:161
  19.8 3.2 %collective-permute-start.7 = (f32[32,128]{1,0:T(8,128)S(1)}, f32[32,128]{1,0:T(8,128)S(1)}, u32[]{:S(2)}, u32[]{:S(2)}) collective-permute-start(f32[32,128]{1,0:T(8,128)S(1)} %shard_map.68._.a), channel_id=1, source_target_pairs={{0,3},{1,2},{2,1},{3,0},{4,7},{5,6},{6,5},{7,4},{8,11},{9,10},{10,... | collective-permute-start | bytes 49160 | tf_op jit(solution)/shard_map/ppermute | solution.py:167
  23.1 3.2 %collective-permute-start.8 = (f32[32,128]{1,0:T(8,128)S(1)}, f32[32,128]{1,0:T(8,128)S(1)}, u32[]{:S(2)}, u32[]{:S(2)}) collective-permute-start(f32[32,128]{1,0:T(8,128)S(1)} %shard_map.70._.a), channel_id=1, source_target_pairs={{0,5},{1,4},{2,7},{3,6},{4,1},{5,0},{6,3},{7,2},{8,13},{9,12},{10,... | collective-permute-start | bytes 49160 | tf_op jit(solution)/shard_map/ppermute | solution.py:167
  26.3 6.2 %collective-permute-start.13 = (f32[32,1280]{1,0:T(8,128)S(1)}, f32[32,1280]{1,0:T(8,128)S(1)}, u32[]{:S(2)}, u32[]{:S(2)}) collective-permute-start(f32[32,1280]{1,0:T(8,128)S(1)} %get-tuple-element.43), channel_id=1, source_target_pairs={{0,1},{1,0},{2,3},{3,2},{4,5},{5,4},{6,7},{7,6},{8,9},{9,8},{10,11... | collective-permute-start | bytes 491528 | tf_op jit(solution)/shard_map/ppermute | solution.py:161
  26.8 5.7 %collective-permute-start.12 = (f32[32,1152]{1,0:T(8,128)S(1)}, f32[32,1152]{1,0:T(8,128)S(1)}, u32[]{:S(2)}, u32[]{:S(2)}) collective-permute-start(f32[32,1152]{1,0:T(8,128)S(1)} %get-tuple-element.42), channel_id=1, source_target_pairs={{0,1},{1,0},{2,3},{3,2},{4,5},{5,4},{6,7},{7,6},{8,9},{9,8},{10,11... | collective-permute-start | bytes 442376 | tf_op jit(solution)/shard_map/ppermute | solution.py:161
  26.9 4.4 %collective-permute-start.9 = (f32[32,128]{1,0:T(8,128)S(1)}, f32[32,128]{1,0:T(8,128)S(1)}, u32[]{:S(2)}, u32[]{:S(2)}) collective-permute-start(f32[32,128]{1,0:T(8,128)S(1)} %shard_map.72._.a), channel_id=1, source_target_pairs={{0,9},{1,8},{2,11},{3,10},{4,13},{5,12},{6,15},{7,14},{8,1},{9,0},... | collective-permute-start | bytes 49160 | tf_op jit(solution)/shard_map/ppermute | solution.py:167
  29.8 1.7 %collective-permute-start.11 = (f32[32,640]{1,0:T(8,128)S(1)}, f32[32,640]{1,0:T(8,128)S(1)}, u32[]{:S(2)}, u32[]{:S(2)}) collective-permute-start(f32[32,640]{1,0:T(8,128)S(1)} %get-tuple-element.41), channel_id=1, source_target_pairs={{0,1},{1,0},{2,3},{3,2},{4,5},{5,4},{6,7},{7,6},{8,9},{9,8},{10,11... | collective-permute-start | bytes 245768 | tf_op jit(solution)/shard_map/ppermute | solution.py:161
  31.3 1.3 %collective-permute-start.14 = (f32[32,512]{1,0:T(8,128)S(1)}, f32[32,512]{1,0:T(8,128)S(1)}, u32[]{:S(2)}, u32[]{:S(2)}) collective-permute-start(f32[32,512]{1,0:T(8,128)S(1)} %get-tuple-element.44), channel_id=1, source_target_pairs={{0,1},{1,0},{2,3},{3,2},{4,5},{5,4},{6,7},{7,6},{8,9},{9,8},{10,11... | collective-permute-start | bytes 196616 | tf_op jit(solution)/shard_map/ppermute | solution.py:161

commit v3 on v2

--- a/solution.py
+++ b/solution.py
@@ -14,7 +14,7 @@
 HBM = pl.BlockSpec(memory_space=pltpu.HBM)
 ANY = pl.BlockSpec(memory_space=pl.ANY)
 LANES = 128
-SPLITS = {2: (20, 28), 3: (10, 22, 28), 4: (5, 14, 24, 28)}
+SPLITS = {2: (20, 28), 3: (10, 22, 28), 4: (5, 14, 23, 28)}
 
 
 def call(kernel, out, in_specs, vmem, scratch=(), flops=0, bytes_accessed=0, aliases=None):
@@ -90,18 +90,22 @@
     out[...] = a[...] + b[...]
 
 
-def base_kernel(offset, step, x, w, _, own, send):
+def base_kernel(offset, step, x, w, _, *refs):
+    own, send = refs[-2:]
     half, wide = own.shape
+    kept = send.shape[1] - wide
     mine = lax.axis_index("width") == 0
+    if kept:
+        send[:, :kept] = refs[0][...]
     for c in range(0, wide, step):
         s = min(step, wide - c)
         both = jnp.dot(x[...], w[:, offset + c : offset + c + s], preferred_element_type=F32)
         own[:, c : c + s] = jnp.where(mine, both[:half], both[half:])
-        send[:, c : c + s] = jnp.where(mine, both[half:], both[:half]).astype(send.dtype)
-
-
-def finish_kernel(pieces, low, ids, up_own, up_peer, *refs):
-    own, got, out = refs[:pieces], refs[pieces : 2 * pieces], refs[2 * pieces]
+        send[:, kept + c : kept + c + s] = jnp.where(mine, both[half:], both[:half])
+
+
+def delta_kernel(low, ids, up_own, up_peer, got, *refs):
+    own, out = refs[:-1], refs[-1]
     count, part, wide = up_own.shape
     half, rank = out.shape[0], 2 * part
     w = lax.axis_index("width")
@@ -120,15 +124,24 @@
 
     a, b = spread(w), spread(1 - w)
     c = 0
-    for o, g in zip(own, got):
+    for o in own:
         s = o.shape[1]
         delta = jnp.dot(a, up_own[:, :, c : c + s].reshape(count * part, s), preferred_element_type=F32)
         delta = delta + jnp.dot(b, up_peer[:, :, c : c + s].reshape(count * part, s), preferred_element_type=F32)
-        out[:, c : c + s] = (o[...] + g[...].astype(F32) + delta).astype(BF16)
+        total = o[...] + delta
+        if c < got.shape[1]:
+            total = total + got[:, c : c + s]
+        out[:, c : c + s] = total
         c += s
 
 
-def gather(n, message, partner):
+def finish_kernel(total, got, out):
+    done = out.shape[1] - got.shape[1]
+    out[:, :done] = total[:, :done].astype(BF16)
+    out[:, done:] = (total[:, done:] + got[...]).astype(BF16)
+
+
+def gather(n, message, partner, table, swap):
     rows, wide = message.shape[1:]
 
     def join(parts):
@@ -138,16 +151,17 @@
         )(*parts)
 
     if n == 2:
-        return [message, partner(message, 1)], [[0], [1]]
+        return [message, partner(message, 1)], [[0], [1]], swap(table)
     if n == 4:
         second, first = partner(message, 2), partner(message, 1)
-        return [message, second, first, partner(second, 1)], [[0], [2], [1], [3]]
+        return [message, second, first, partner(second, 1)], [[0], [2], [1], [3]], swap(table)
     first, second, fourth = partner(message, 1), partner(message, 2), partner(message, 4)
     sixth = partner(fourth, 2)
     near = partner(join([second, fourth]), 1)
-    sixth_after, _ = lax.optimization_barrier((sixth, first))
-    far = partner(sixth_after, 1)
-    return [message, first, second, fourth, sixth, near, far], [[0], [1], [2], [4], [6], [3, 5], [7]]
+    sixth, _ = lax.optimization_barrier((sixth, first))
+    far = partner(sixth, 1)
+    parts = [message, first, second, fourth, sixth, near, far]
+    return parts, [[0], [1], [2], [4], [6], [3, 5], [7]], swap(table)
 
 
 def small(n, tokens, base_up_weight, row_ids, holder, pool, table):
@@ -173,7 +187,7 @@
         pack_kernel, jax.ShapeDtypeStruct((1, rows, wide + LANES), BF16), [HBM, HBM], 1 << 20,
         scratch=[pltpu.SMEM((rows,), jnp.int32), pltpu.SemaphoreType.DMA((2,))], flops=40 << 30, bytes_accessed=1 << 17,
     )(far(row_ids), far(tokens))
-    parts, order = gather(n, message, partner)
+    parts, order, up_peer = gather(n, message, partner, table, swap)
 
     x, ids, low = call(
         functools.partial(assemble_kernel, order),
@@ -193,30 +207,35 @@
     steps = [swap] + [functools.partial(across, k=1 << i) for i in range(n.bit_length() - 1)]
     units = columns // LANES
     cuts = [0] + [LANES * (units * c // 28) for c in SPLITS[len(steps)]]
-    own, got, up_own, up_peer = [], [], pinned(table), None
-    for step, a, b in zip(steps, cuts[:-1], cuts[1:]):
+    own, sent = [], None
+    for i, (step, a, b) in enumerate(zip(steps, cuts[:-1], cuts[1:])):
         other = step(low)
+        last = i == len(steps) - 1
+        kept = [] if sent is None or last else [sent]
         o, s = call(
             functools.partial(base_kernel, a, 512),
-            [jax.ShapeDtypeStruct((half, b - a), F32), jax.ShapeDtypeStruct((half, b - a), F32)],
-            [VMEM, VMEM, ANY],
+            [
+                jax.ShapeDtypeStruct((half, b - a), F32),
+                jax.ShapeDtypeStruct((half, b - a if last else b), F32),
+            ],
+            [VMEM, VMEM, ANY] + [VMEM] * len(kept),
             4 << 20,
-        )(x, weight, low)
+        )(x, weight, low, *kept)
         own.append(o)
         low = add(low, other, o)
-        if len(own) < len(steps):
-            s, low = lax.optimization_barrier((s, low))
-        got.append(swap(s))
-        if len(own) == 1:
-            table, low = lax.optimization_barrier((table, low))
-            up_peer = pinned(swap(table))
-
-    return call(
-        functools.partial(finish_kernel, len(own)),
-        jax.ShapeDtypeStruct((half, columns), BF16),
-        [VMEM] * (4 + 2 * len(own)),
-        8 << 20,
-    )(low, ids, up_own, up_peer, *own, *got)
+        if last:
+            late = swap(s)
+        else:
+            sent = s
+            if i == len(steps) - 2:
+                sent, low = lax.optimization_barrier((sent, low))
+                early = swap(sent)
+
+    total = call(
+        delta_kernel, jax.ShapeDtypeStruct((half, columns), F32), [VMEM] * (5 + len(own)), 8 << 20,
+        flops=4 << 30,
+    )(low, ids, pinned(table), up_peer, early, *own)
+    return call(finish_kernel, jax.ShapeDtypeStruct((half, columns), BF16), [VMEM, VMEM], 4 << 20)(total, late)
 
 
 def large(tokens, base_up_weight, adapter_index_per_row, holder_slot_index, down_factor_pool, up_factor_table):

time: 34.3 us -> 32.7 us (0.953)
  starting transfers between devices: 19.2 us -> 16.5 us
  waiting for transfers between devices: 5.4 us -> 6.91 us
    ppermute x6, waiting for transfers between devices: 3.74 us -> 5.72 us  [partner(): return lax.ppermute(v, 'ffn', [(i, i ^ k) for i in range(n)])]
    ppermute x6, starting transfers between devices: 12 us -> 10.7 us  [partner(): return lax.ppermute(v, 'ffn', [(i, i ^ k) for i in range(n)])]
    ppermute x6 -> x4, waiting for transfers between devices: 1.15 us -> 0.15 us  [swap(): return lax.ppermute(v, 'width', [(0, 1), (1, 0)])]
    ppermute x3, starting transfers between devices: 5.61 us -> 4.82 us  [across(): lax.ppermute(v, both, [(2 * i + w, 2 * (i ^ k) + 1 - w) for i in range(n)...]
    ppermute x6 -> x4, starting transfers between devices: 1.54 us -> 0.95 us  [swap(): return lax.ppermute(v, 'width', [(0, 1), (1, 0)])]
    ppermute x3, waiting for transfers between devices: 0.52 us -> 1.05 us  [across(): lax.ppermute(v, both, [(2 * i + w, 2 * (i ^ k) + 1 - w) for i in range(n)...]
    pallas_call x1 -> x2, Pallas kernels: 1.57 us -> 1.54 us  [the longest x1 0.82 us: small(): call(delta_kernel, jax.ShapeDtypeStruct((half, columns), F32), [VMEM] * (...]
  transfers between devices with their start and end apart: 15 -> 13, of which waited for: 6 -> 6; matrix products, arithmetic and copies ran while one was open for 0% -> 0% of each run, Pallas kernels for 16% -> 26%
where the time goes in v3:
time: 32.7 us; the launch traced here: 32.5 us
  starting transfers between devices  16.5 us (50%)
  Pallas kernels  9.01 us (28%)
  waiting for transfers between devices  6.91 us (21%)
    ppermute x6, starting transfers between devices, partner(): return lax.ppermute(v, 'ffn', [(i, i ^ k) for i in range(n)])  10.7 us
    ppermute x6, waiting for transfers between devices, partner(): return lax.ppermute(v, 'ffn', [(i, i ^ k) for i in range(n)])  5.72 us
    pallas_call x4, Pallas kernels, small(): call(functools.partial(base_kernel, a, 512), [jax.ShapeDtypeStruct((half,...  5.46 us
    ppermute x3, starting transfers between devices, across(): lax.ppermute(v, both, [(2 * i + w, 2 * (i ^ k) + 1 - w) for i in range(n)...  4.82 us
    ppermute x3, waiting for transfers between devices, across(): lax.ppermute(v, both, [(2 * i + w, 2 * (i ^ k) + 1 - w) for i in range(n)...  1.05 us
    pallas_call x1, Pallas kernels, small(): call(pack_kernel, jax.ShapeDtypeStruct((1, rows, wide + LANES), BF16), [H...  1.01 us
    pallas_call x1, Pallas kernels, small(): call(functools.partial(assemble_kernel, order), [jax.ShapeDtypeStruct((n...  0.98 us
    ppermute x4, starting transfers between devices, swap(): return lax.ppermute(v, 'width', [(0, 1), (1, 0)])  0.95 us
  transfers between devices with their start and end apart: 13, of which 6 were waited for; matrix products, arithmetic and copies ran while one was open for 0% of the time, Pallas kernels for 26%

profile of v3, /device:TPU:0, one launch (start us, length us, event | category | flops | bytes accessed | tf_op | source)
XLA Modules:
  0.0 32.5 jit_solution(3765166028561834710)
XLA Ops:
  0.0 0.5 %collective-permute-start.10 = (bf16[8,32,3584]{2,1,0:T(8,128)(2,1)}, bf16[8,32,3584]{2,1,0:T(8,128)(2,1)S(1)}, u32[]{:S(2)}, u32[]{:S(2)}) collective-permute-start(bf16[8,32,3584]{2,1,0:T(8,128)(2,1)} %up_own.1), channel_id=1, source_target_pairs={{0,1},{1,0},{2,3},{3,2},{4,5},{5,4},{6,7},{7,6},{8,9},{9,8},{10,11... | collective-permute-start | bytes 5505032 | tf_op jit(solution)/shard_map/ppermute | solution.py:175
  0.5 1.0 %shard_map.64.refs_0_ = bf16[1,8,4224]{2,1,0:T(8,128)(2,1)S(1)} custom-call(s32[8]{0:T(128)} %ids_far.1, bf16[8,4096]{1,0:T(8,128)(2,1)} %tokens.1), custom_call_target="tpu_custom_call" | custom-call | flops 42949672960 | bytes 131072 | tf_op jit(solution)/shard_map/pallas_call | solution.py:186
  1.5 3.7 %collective-permute-start.2 = (bf16[1,8,4224]{2,1,0:T(8,128)(2,1)S(1)}, bf16[1,8,4224]{2,1,0:T(8,128)(2,1)S(1)}, u32[]{:S(2)}, u32[]{:S(2)}) collective-permute-start(bf16[1,8,4224]{2,1,0:T(8,128)(2,1)S(1)} %shard_map.64.refs_0_), channel_id=1, source_target_pairs={{0,8},{2,10},{4,12},{6,14},{8,0},{10,2},{12,4},{14,6},{1,9},{3,11}... | collective-permute-start | bytes 202760 | tf_op jit(solution)/shard_map/ppermute | solution.py:178
  5.1 1.6 %collective-permute-start.1 = (bf16[1,8,4224]{2,1,0:T(8,128)(2,1)S(1)}, bf16[1,8,4224]{2,1,0:T(8,128)(2,1)S(1)}, u32[]{:S(2)}, u32[]{:S(2)}) collective-permute-start(bf16[1,8,4224]{2,1,0:T(8,128)(2,1)S(1)} %shard_map.64.refs_0_), channel_id=1, source_target_pairs={{0,4},{2,6},{4,0},{6,2},{8,12},{10,14},{12,8},{14,10},{1,5},{3,7},... | collective-permute-start | bytes 202760 | tf_op jit(solution)/shard_map/ppermute | solution.py:178
  6.7 1.5 %collective-permute-start = (bf16[1,8,4224]{2,1,0:T(8,128)(2,1)S(1)}, bf16[1,8,4224]{2,1,0:T(8,128)(2,1)S(1)}, u32[]{:S(2)}, u32[]{:S(2)}) collective-permute-start(bf16[1,8,4224]{2,1,0:T(8,128)(2,1)S(1)} %shard_map.64.refs_0_), channel_id=1, source_target_pairs={{0,2},{2,0},{4,6},{6,4},{8,10},{10,8},{12,14},{14,12},{1,3},{3,1},... | collective-permute-start | bytes 202760 | tf_op jit(solution)/shard_map/ppermute | solution.py:178
  8.2 1.1 %collective-permute-done.2.refs_1_.refs_3_ = bf16[1,8,4224]{2,1,0:T(8,128)(2,1)S(1)} collective-permute-done((bf16[1,8,4224]{2,1,0:T(8,128)(2,1)S(1)}, bf16[1,8,4224]{2,1,0:T(8,128)(2,1)S(1)}, u32[]{:S(2)}, u32[]{:S(2)}) %collective-permute-start.2) | collective-permute-done | bytes 67616 | tf_op jit(solution)/shard_map/ppermute | solution.py:178
  9.3 0.8 %collective-permute-start.3 = (bf16[1,8,4224]{2,1,0:T(8,128)(2,1)S(1)}, bf16[1,8,4224]{2,1,0:T(8,128)(2,1)S(1)}, u32[]{:S(2)}, u32[]{:S(2)}) collective-permute-start(bf16[1,8,4224]{2,1,0:T(8,128)(2,1)S(1)} %collective-permute-done.2.refs_1_.refs_3_), channel_id=1, source_target_pairs={{0,4},{2,6},{4,0},{6,2},{8,12},{10,14},{12,8},{14,10},{1,5},{3,7},... | collective-permute-start | bytes 202760 | tf_op jit(solution)/shard_map/ppermute | solution.py:178
  10.1 1.6 %collective-permute-start.4 = (bf16[2,8,4224]{2,1,0:T(8,128)(2,1)S(1)}, bf16[2,8,4224]{2,1,0:T(8,128)(2,1)S(1)}, u32[]{:S(2)}, u32[]{:S(2)}) collective-permute-start(bf16[2,8,4224]{2,1,0:T(8,128)(2,1)S(1)} %shard_map.65), channel_id=1, source_target_pairs={{0,2},{2,0},{4,6},{6,4},{8,10},{10,8},{12,14},{14,12},{1,3},{3,1},... | collective-permute-start | bytes 405512 | tf_op jit(solution)/shard_map/ppermute | solution.py:178
  11.7 1.9 %collective-permute-done.3.refs_4_ = bf16[1,8,4224]{2,1,0:T(8,128)(2,1)S(1)} collective-permute-done((bf16[1,8,4224]{2,1,0:T(8,128)(2,1)S(1)}, bf16[1,8,4224]{2,1,0:T(8,128)(2,1)S(1)}, u32[]{:S(2)}, u32[]{:S(2)}) %collective-permute-start.3) | collective-permute-done | bytes 67616 | tf_op jit(solution)/shard_map/ppermute | solution.py:178
  13.6 1.6 %collective-permute-start.5 = (bf16[1,8,4224]{2,1,0:T(8,128)(2,1)S(1)}, bf16[1,8,4224]{2,1,0:T(8,128)(2,1)S(1)}, u32[]{:S(2)}, u32[]{:S(2)}) collective-permute-start(bf16[1,8,4224]{2,1,0:T(8,128)(2,1)S(1)} %collective-permute-done.3.refs_4_), channel_id=1, source_target_pairs={{0,2},{2,0},{4,6},{6,4},{8,10},{10,8},{12,14},{14,12},{1,3},{3,1},... | collective-permute-start | bytes 202760 | tf_op jit(solution)/shard_map/ppermute | solution.py:178
  15.2 2.7 %collective-permute-done.5.refs_6_ = bf16[1,8,4224]{2,1,0:T(8,128)(2,1)S(1)} collective-permute-done((bf16[1,8,4224]{2,1,0:T(8,128)(2,1)S(1)}, bf16[1,8,4224]{2,1,0:T(8,128)(2,1)S(1)}, u32[]{:S(2)}, u32[]{:S(2)}) %collective-permute-start.5) | collective-permute-done | bytes 67616 | tf_op jit(solution)/shard_map/ppermute | solution.py:178
  17.9 1.0 %shard_map.66 = (bf16[64,4096]{1,0:T(8,128)(2,1)S(1)}, f32[64,128]{1,0:T(8,128)S(1)}, f32[32,128]{1,0:T(8,128)S(1)}) custom-call(s32[8]{0:T(128)S(1)} %copy-done.2, bf16[64,4096]{1,0:T(8,128)(2,1)S(1)} %bitcast.3, bf16[1,8,4224]{2,1,0:T(8,128)(2,1)S(1)} %shard_map.64.refs_0_, bf16[1,8,4224]{2,1,0:T(8,128)(2,1)S(1)} %collective-permute-done.refs_1_, ...), custom_call_target="tpu_custom_call" | custom-call | tf_op jit(solution)/shard_map/pallas_call | solution.py:192
  18.9 1.0 %shard_map.67 = (f32[32,640]{1,0:T(8,128)S(1)}, f32[32,640]{1,0:T(8,128)S(1)}) custom-call(bf16[64,4096]{1,0:T(8,128)(2,1)S(1)} %get-tuple-element.20.x, bf16[4096,3584]{1,0:T(8,128)(2,1)S(1)} %copy-done, f32[32,128]{1,0:T(8,128)S(1)} %get-tuple-element.21._.a), custom_call_target="tpu_custom_call" | custom-call | tf_op jit(solution)/shard_map/pallas_call | solution.py:215
  20.1 1.6 %collective-permute-start.7 = (f32[32,128]{1,0:T(8,128)S(1)}, f32[32,128]{1,0:T(8,128)S(1)}, u32[]{:S(2)}, u32[]{:S(2)}) collective-permute-start(f32[32,128]{1,0:T(8,128)S(1)} %shard_map.68._.a), channel_id=1, source_target_pairs={{0,3},{1,2},{2,1},{3,0},{4,7},{5,6},{6,5},{7,4},{8,11},{9,10},{10,... | collective-permute-start | bytes 49160 | tf_op jit(solution)/shard_map/ppermute | solution.py:181
  21.7 1.7 %shard_map.69 = (f32[32,1152]{1,0:T(8,128)S(1)}, f32[32,1792]{1,0:T(8,128)S(1)}) custom-call(bf16[64,4096]{1,0:T(8,128)(2,1)S(1)} %get-tuple-element.20.x, bf16[4096,3584]{1,0:T(8,128)(2,1)S(1)} %copy-done, f32[32,128]{1,0:T(8,128)S(1)} %shard_map.68._.a, f32[32,640]{1,0:T(8,128)S(1)} %get-tuple-element.23.refs_0_), custom_call_target="tpu_custom_call" | custom-call | tf_op jit(solution)/shard_map/pallas_call | solution.py:215
  23.5 0.6 %collective-permute-start.8 = (f32[32,128]{1,0:T(8,128)S(1)}, f32[32,128]{1,0:T(8,128)S(1)}, u32[]{:S(2)}, u32[]{:S(2)}) collective-permute-start(f32[32,128]{1,0:T(8,128)S(1)} %shard_map.70._.a), channel_id=1, source_target_pairs={{0,5},{1,4},{2,7},{3,6},{4,1},{5,0},{6,3},{7,2},{8,13},{9,12},{10,... | collective-permute-start | bytes 49160 | tf_op jit(solution)/shard_map/ppermute | solution.py:181
  24.1 1.7 %shard_map.71 = (f32[32,1152]{1,0:T(8,128)S(1)}, f32[32,2944]{1,0:T(8,128)S(1)}) custom-call(bf16[64,4096]{1,0:T(8,128)(2,1)S(1)} %get-tuple-element.20.x, bf16[4096,3584]{1,0:T(8,128)(2,1)S(1)} %copy-done, f32[32,128]{1,0:T(8,128)S(1)} %shard_map.70._.a, f32[32,1792]{1,0:T(8,128)S(1)} %get-tuple-element.25.refs_0_), custom_call_target="tpu_custom_call" | custom-call | tf_op jit(solution)/shard_map/pallas_call | solution.py:215
  25.8 0.9 %collective-permute-done.8.b = f32[32,128]{1,0:T(8,128)S(1)} collective-permute-done((f32[32,128]{1,0:T(8,128)S(1)}, f32[32,128]{1,0:T(8,128)S(1)}, u32[]{:S(2)}, u32[]{:S(2)}) %collective-permute-start.8) | collective-permute-done | bytes 16416 | tf_op jit(solution)/shard_map/ppermute | solution.py:181
  26.9 2.5 %collective-permute-start.9 = (f32[32,128]{1,0:T(8,128)S(1)}, f32[32,128]{1,0:T(8,128)S(1)}, u32[]{:S(2)}, u32[]{:S(2)}) collective-permute-start(f32[32,128]{1,0:T(8,128)S(1)} %shard_map.72._.a), channel_id=1, source_target_pairs={{0,9},{1,8},{2,11},{3,10},{4,13},{5,12},{6,15},{7,14},{8,1},{9,0},... | collective-permute-start | bytes 49160 | tf_op jit(solution)/shard_map/ppermute | solution.py:181
  29.4 1.0 %shard_map.73 = (f32[32,640]{1,0:T(8,128)S(1)}, f32[32,640]{1,0:T(8,128)S(1)}) custom-call(bf16[64,4096]{1,0:T(8,128)(2,1)S(1)} %get-tuple-element.20.x, bf16[4096,3584]{1,0:T(8,128)(2,1)S(1)} %copy-done, f32[32,128]{1,0:T(8,128)S(1)} %shard_map.72._.a), custom_call_target="tpu_custom_call" | custom-call | tf_op jit(solution)/shard_map/pallas_call | solution.py:215
  30.4 0.3 collective-permute-start.12
  30.7 0.2 collective-permute-done.9.b
  31.0 0.8 %shard_map.75.total = f32[32,3584]{1,0:T(8,128)S(1)} custom-call(f32[32,128]{1,0:T(8,128)S(1)} %shard_map.74.low, f32[64,128]{1,0:T(8,128)S(1)} %get-tuple-element.30.ids, bf16[8,32,3584]{2,1,0:T(8,128)(2,1)S(1)} %copy-done.3, bf16[8,32,3584]{2,1,0:T(8,128)(2,1)S(1)} %collective-permute-done.10.up_peer, f32[32,2944]{1,0:T(8,128)S(1)} %collective-permute-done.11.got, ...), custom_call_target="tpu_custom_call" | custom-call | flops 4294967296 | tf_op jit(solution)/shard_map/pallas_call | solution.py:234
  31.8 0.7 %shard_map.76 = bf16[32,3584]{1,0:T(8,128)(2,1)} custom-call(f32[32,3584]{1,0:T(8,128)S(1)} %shard_map.75.total, f32[32,640]{1,0:T(8,128)S(1)} %collective-permute-done.12.got), custom_call_target="tpu_custom_call" | custom-call | tf_op jit(solution)/shard_map/pallas_call | solution.py:238
  (23 shorter events, 0.4 us)
Async XLA Ops:
  0.0 17.9 %copy-start.1 = (bf16[1,4096,64]{1,2,0:T(8,128)(2,1)S(1)}, bf16[1,4096,64]{1,2,0:T(8,128)(2,1)}, u32[]{:S(2)}) copy-start(bf16[1,4096,64]{1,2,0:T(8,128)(2,1)} %param.10) | copy-start | bytes 1572868
  0.0 17.9 %copy-start.2 = (s32[8]{0:T(128)S(1)}, s32[8]{0:T(128)}, u32[]{:S(2)}) copy-start(s32[8]{0:T(128)} %holder.1) | copy-start | bytes 100
  0.0 30.9 %collective-permute-start.10 = (bf16[8,32,3584]{2,1,0:T(8,128)(2,1)}, bf16[8,32,3584]{2,1,0:T(8,128)(2,1)S(1)}, u32[]{:S(2)}, u32[]{:S(2)}) collective-permute-start(bf16[8,32,3584]{2,1,0:T(8,128)(2,1)} %up_own.1), channel_id=1, source_target_pairs={{0,1},{1,0},{2,3},{3,2},{4,5},{5,4},{6,7},{7,6},{8,9},{9,8},{10,11... | collective-permute-start | bytes 5505032 | tf_op jit(solution)/shard_map/ppermute | solution.py:175
  0.5 18.5 %copy-start = (bf16[4096,3584]{1,0:T(8,128)(2,1)S(1)}, bf16[4096,3584]{1,0:T(8,128)(2,1)}, u32[]{:S(2)}) copy-start(bf16[4096,3584]{1,0:T(8,128)(2,1)} %w.7) | copy-start | bytes 88080384
  1.5 7.8 %collective-permute-start.2 = (bf16[1,8,4224]{2,1,0:T(8,128)(2,1)S(1)}, bf16[1,8,4224]{2,1,0:T(8,128)(2,1)S(1)}, u32[]{:S(2)}, u32[]{:S(2)}) collective-permute-start(bf16[1,8,4224]{2,1,0:T(8,128)(2,1)S(1)} %shard_map.64.refs_0_), channel_id=1, source_target_pairs={{0,8},{2,10},{4,12},{6,14},{8,0},{10,2},{12,4},{14,6},{1,9},{3,11}... | collective-permute-start | bytes 202760 | tf_op jit(solution)/shard_map/ppermute | solution.py:178
  5.1 5.0 %collective-permute-start.1 = (bf16[1,8,4224]{2,1,0:T(8,128)(2,1)S(1)}, bf16[1,8,4224]{2,1,0:T(8,128)(2,1)S(1)}, u32[]{:S(2)}, u32[]{:S(2)}) collective-permute-start(bf16[1,8,4224]{2,1,0:T(8,128)(2,1)S(1)} %shard_map.64.refs_0_), channel_id=1, source_target_pairs={{0,4},{2,6},{4,0},{6,2},{8,12},{10,14},{12,8},{14,10},{1,5},{3,7},... | collective-permute-start | bytes 202760 | tf_op jit(solution)/shard_map/ppermute | solution.py:178
  6.7 5.0 %collective-permute-start = (bf16[1,8,4224]{2,1,0:T(8,128)(2,1)S(1)}, bf16[1,8,4224]{2,1,0:T(8,128)(2,1)S(1)}, u32[]{:S(2)}, u32[]{:S(2)}) collective-permute-start(bf16[1,8,4224]{2,1,0:T(8,128)(2,1)S(1)} %shard_map.64.refs_0_), channel_id=1, source_target_pairs={{0,2},{2,0},{4,6},{6,4},{8,10},{10,8},{12,14},{14,12},{1,3},{3,1},... | collective-permute-start | bytes 202760 | tf_op jit(solution)/shard_map/ppermute | solution.py:178
  9.3 4.3 %collective-permute-start.3 = (bf16[1,8,4224]{2,1,0:T(8,128)(2,1)S(1)}, bf16[1,8,4224]{2,1,0:T(8,128)(2,1)S(1)}, u32[]{:S(2)}, u32[]{:S(2)}) collective-permute-start(bf16[1,8,4224]{2,1,0:T(8,128)(2,1)S(1)} %collective-permute-done.2.refs_1_.refs_3_), channel_id=1, source_target_pairs={{0,4},{2,6},{4,0},{6,2},{8,12},{10,14},{12,8},{14,10},{1,5},{3,7},... | collective-permute-start | bytes 202760 | tf_op jit(solution)/shard_map/ppermute | solution.py:178
  10.1 7.8 %collective-permute-start.4 = (bf16[2,8,4224]{2,1,0:T(8,128)(2,1)S(1)}, bf16[2,8,4224]{2,1,0:T(8,128)(2,1)S(1)}, u32[]{:S(2)}, u32[]{:S(2)}) collective-permute-start(bf16[2,8,4224]{2,1,0:T(8,128)(2,1)S(1)} %shard_map.65), channel_id=1, source_target_pairs={{0,2},{2,0},{4,6},{6,4},{8,10},{10,8},{12,14},{14,12},{1,3},{3,1},... | collective-permute-start | bytes 405512 | tf_op jit(solution)/shard_map/ppermute | solution.py:178
  13.6 4.3 %collective-permute-start.5 = (bf16[1,8,4224]{2,1,0:T(8,128)(2,1)S(1)}, bf16[1,8,4224]{2,1,0:T(8,128)(2,1)S(1)}, u32[]{:S(2)}, u32[]{:S(2)}) collective-permute-start(bf16[1,8,4224]{2,1,0:T(8,128)(2,1)S(1)} %collective-permute-done.3.refs_4_), channel_id=1, source_target_pairs={{0,2},{2,0},{4,6},{6,4},{8,10},{10,8},{12,14},{14,12},{1,3},{3,1},... | collective-permute-start | bytes 202760 | tf_op jit(solution)/shard_map/ppermute | solution.py:178
  18.9 1.2 %collective-permute-start.6 = (f32[32,128]{1,0:T(8,128)S(1)}, f32[32,128]{1,0:T(8,128)S(1)}, u32[]{:S(2)}, u32[]{:S(2)}) collective-permute-start(f32[32,128]{1,0:T(8,128)S(1)} %get-tuple-element.21._.a), channel_id=1, source_target_pairs={{0,1},{1,0},{2,3},{3,2},{4,5},{5,4},{6,7},{7,6},{8,9},{9,8},{10,11... | collective-permute-start | bytes 49160 | tf_op jit(solution)/shard_map/ppermute | solution.py:175
  20.1 3.4 %collective-permute-start.7 = (f32[32,128]{1,0:T(8,128)S(1)}, f32[32,128]{1,0:T(8,128)S(1)}, u32[]{:S(2)}, u32[]{:S(2)}) collective-permute-start(f32[32,128]{1,0:T(8,128)S(1)} %shard_map.68._.a), channel_id=1, source_target_pairs={{0,3},{1,2},{2,1},{3,0},{4,7},{5,6},{6,5},{7,4},{8,11},{9,10},{10,... | collective-permute-start | bytes 49160 | tf_op jit(solution)/shard_map/ppermute | solution.py:181
  23.5 3.2 %collective-permute-start.8 = (f32[32,128]{1,0:T(8,128)S(1)}, f32[32,128]{1,0:T(8,128)S(1)}, u32[]{:S(2)}, u32[]{:S(2)}) collective-permute-start(f32[32,128]{1,0:T(8,128)S(1)} %shard_map.70._.a), channel_id=1, source_target_pairs={{0,5},{1,4},{2,7},{3,6},{4,1},{5,0},{6,3},{7,2},{8,13},{9,12},{10,... | collective-permute-start | bytes 49160 | tf_op jit(solution)/shard_map/ppermute | solution.py:181
  26.7 4.3 %copy-start.3 = (bf16[8,32,3584]{2,1,0:T(8,128)(2,1)S(1)}, bf16[8,32,3584]{2,1,0:T(8,128)(2,1)}, u32[]{:S(2)}) copy-start(bf16[8,32,3584]{2,1,0:T(8,128)(2,1)} %up_own.1) | copy-start | bytes 5505028
  26.7 4.2 %collective-permute-start.11 = (f32[32,2944]{1,0:T(8,128)S(1)}, f32[32,2944]{1,0:T(8,128)S(1)}, u32[]{:S(2)}, u32[]{:S(2)}) collective-permute-start(f32[32,2944]{1,0:T(8,128)S(1)} %get-tuple-element.31), channel_id=1, source_target_pairs={{0,1},{1,0},{2,3},{3,2},{4,5},{5,4},{6,7},{7,6},{8,9},{9,8},{10,11... | collective-permute-start | bytes 1130504 | tf_op jit(solution)/shard_map/ppermute | solution.py:175
  26.9 4.1 %collective-permute-start.9 = (f32[32,128]{1,0:T(8,128)S(1)}, f32[32,128]{1,0:T(8,128)S(1)}, u32[]{:S(2)}, u32[]{:S(2)}) collective-permute-start(f32[32,128]{1,0:T(8,128)S(1)} %shard_map.72._.a), channel_id=1, source_target_pairs={{0,9},{1,8},{2,11},{3,10},{4,13},{5,12},{6,15},{7,14},{8,1},{9,0},... | collective-permute-start | bytes 49160 | tf_op jit(solution)/shard_map/ppermute | solution.py:181
  30.4 1.4 %collective-permute-start.12 = (f32[32,640]{1,0:T(8,128)S(1)}, f32[32,640]{1,0:T(8,128)S(1)}, u32[]{:S(2)}, u32[]{:S(2)}) collective-permute-start(f32[32,640]{1,0:T(8,128)S(1)} %get-tuple-element.32), channel_id=1, source_target_pairs={{0,1},{1,0},{2,3},{3,2},{4,5},{5,4},{6,7},{7,6},{8,9},{9,8},{10,11... | collective-permute-start | bytes 245768 | tf_op jit(solution)/shard_map/ppermute | solution.py:175

commit v4 on v3

--- a/solution.py
+++ b/solution.py
@@ -39,11 +39,12 @@
     return pltpu.with_memory_space_constraint(array, pltpu.HBM)
 
 
-def pack_kernel(ids_far, tokens, message, ids, sems):
+def pack_kernel(ids_far, holder_far, tokens, message, held, ids, holder, sems):
     rows, wide = tokens.shape
     copies = [
         pltpu.make_async_copy(ids_far, ids, sems.at[0]),
-        pltpu.make_async_copy(tokens, message.at[0, :, pl.ds(0, wide)], sems.at[1]),
+        pltpu.make_async_copy(holder_far, holder, sems.at[1]),
+        pltpu.make_async_copy(tokens, message.at[0, :, pl.ds(0, wide)], sems.at[2]),
     ]
     for copy in copies:
         copy.start()
@@ -54,6 +55,12 @@
         value = jnp.where(place == i, ids[i], value)
     message[0, :, wide:] = value.astype(F32).astype(BF16)
     copies[1].wait()
+    me = lax.axis_index("ffn")
+    mine = jnp.int32(0)
+    for a in range(holder.shape[0]):
+        mine = mine + jnp.where(holder[a] == me, a, 0)
+    held[...] = jnp.full(held.shape, mine, jnp.int32).astype(F32)
+    copies[2].wait()
 
 
 def join_kernel(*refs):
@@ -64,7 +71,7 @@
             at += 1
 
 
-def assemble_kernel(order, holder, down, *refs):
+def assemble_kernel(order, held, down, _, *refs):
     parts, (x, ids, low, stage, id_stage) = refs[: len(order)], refs[len(order) :]
     n, rows, wide = stage.shape
     me = lax.axis_index("ffn")
@@ -77,11 +84,8 @@
     x[...] = whole
     row_ids = id_stage[...].reshape(n * rows, LANES)
     ids[...] = row_ids
-    held = jnp.int32(0)
-    for a in range(holder.shape[0]):
-        held = held + jnp.where(holder[a] == me, a, 0)
     part = lax.dot_general(whole, down[...], (((1,), (1,)), ((), ())), preferred_element_type=F32)
-    part = jnp.where(row_ids[:, : part.shape[1]] == held.astype(F32), part, 0.0)
+    part = jnp.where(row_ids[:, : part.shape[1]] == held[:1, : part.shape[1]], part, 0.0)
     half = n * rows // 2
     low[...] = jnp.concatenate([part[:half], part[half:]], axis=1)
 
@@ -141,7 +145,7 @@
     out[:, done:] = (total[:, done:] + got[...]).astype(BF16)
 
 
-def gather(n, message, partner, table, swap):
+def gather(n, message, partner, across, swap):
     rows, wide = message.shape[1:]
 
     def join(parts):
@@ -151,17 +155,17 @@
         )(*parts)
 
     if n == 2:
-        return [message, partner(message, 1)], [[0], [1]], swap(table)
+        return [message, partner(message, 1)], [[0], [1]]
     if n == 4:
         second, first = partner(message, 2), partner(message, 1)
-        return [message, second, first, partner(second, 1)], [[0], [2], [1], [3]], swap(table)
+        return [message, second, first, partner(second, 1)], [[0], [2], [1], [3]]
     first, second, fourth = partner(message, 1), partner(message, 2), partner(message, 4)
     sixth = partner(fourth, 2)
     near = partner(join([second, fourth]), 1)
     sixth, _ = lax.optimization_barrier((sixth, first))
     far = partner(sixth, 1)
     parts = [message, first, second, fourth, sixth, near, far]
-    return parts, [[0], [1], [2], [4], [6], [3, 5], [7]], swap(table)
+    return parts, [[0], [1], [2], [4], [6], [3, 5], [7]]
 
 
 def small(n, tokens, base_up_weight, row_ids, holder, pool, table):
@@ -181,13 +185,21 @@
         return lax.ppermute(v, both, [(2 * i + w, 2 * (i ^ k) + 1 - w) for i in range(n) for w in range(2)])
 
     weight = pinned(base_up_weight)
+    up_own = pinned(table)
     down = pinned(jnp.swapaxes(pool[0], 0, 1))
 
-    message = call(
-        pack_kernel, jax.ShapeDtypeStruct((1, rows, wide + LANES), BF16), [HBM, HBM], 1 << 20,
-        scratch=[pltpu.SMEM((rows,), jnp.int32), pltpu.SemaphoreType.DMA((2,))], flops=40 << 30, bytes_accessed=1 << 17,
-    )(far(row_ids), far(tokens))
-    parts, order, up_peer = gather(n, message, partner, table, swap)
+    message, held = call(
+        pack_kernel,
+        [jax.ShapeDtypeStruct((1, rows, wide + LANES), BF16), jax.ShapeDtypeStruct((8, LANES), F32)],
+        [HBM, HBM, HBM],
+        1 << 20,
+        scratch=[
+            pltpu.SMEM(row_ids.shape, jnp.int32),
+            pltpu.SMEM(holder.shape, jnp.int32),
+            pltpu.SemaphoreType.DMA((3,)),
+        ], flops=40 << 30, bytes_accessed=1 << 17,
+    )(far(row_ids), far(holder), far(tokens))
+    parts, order = gather(n, message, partner, across, swap)
 
     x, ids, low = call(
         functools.partial(assemble_kernel, order),
@@ -196,10 +208,10 @@
             jax.ShapeDtypeStruct((n * rows, LANES), F32),
             jax.ShapeDtypeStruct((half, 2 * rank), F32),
         ],
-        [SMEM, VMEM] + [VMEM] * len(parts),
+        [VMEM, VMEM, ANY] + [VMEM] * len(parts),
         6 << 20,
         scratch=[pltpu.VMEM((n, rows, wide), F32), pltpu.VMEM((n, rows, LANES), F32)],
-    )(holder, down, *parts)
+    )(held, down, up_own, *parts)
 
     def add(a, b, after):
         return call(add_kernel, jax.ShapeDtypeStruct(a.shape, F32), [VMEM, VMEM, ANY], 1 << 20)(a, b, after)
@@ -227,6 +239,9 @@
             late = swap(s)
         else:
             sent = s
+            if i == 0:
+                up_own, low = lax.optimization_barrier((up_own, low))
+                up_peer = swap(up_own)
             if i == len(steps) - 2:
                 sent, low = lax.optimization_barrier((sent, low))
                 early = swap(sent)
@@ -234,7 +249,7 @@
     total = call(
         delta_kernel, jax.ShapeDtypeStruct((half, columns), F32), [VMEM] * (5 + len(own)), 8 << 20,
         flops=4 << 30,
-    )(low, ids, pinned(table), up_peer, early, *own)
+    )(low, ids, up_own, up_peer, early, *own)
     return call(finish_kernel, jax.ShapeDtypeStruct((half, columns), BF16), [VMEM, VMEM], 4 << 20)(total, late)
 
 

time: 32.7 us -> 31.7 us (0.969)
  waiting for transfers between devices: 6.91 us -> 4.49 us
  starting transfers between devices: 16.5 us -> 18.5 us
  Pallas kernels: 9.01 us -> 8.47 us
    ppermute x6, waiting for transfers between devices: 5.72 us -> 3.74 us  [partner(): return lax.ppermute(v, 'ffn', [(i, i ^ k) for i in range(n)])]
    ppermute x6, starting transfers between devices: 10.7 us -> 12 us  [partner(): return lax.ppermute(v, 'ffn', [(i, i ^ k) for i in range(n)])]
    pallas_call x1, Pallas kernels: 0.98 us -> 0.44 us  [small(): call(functools.partial(assemble_kernel, order), [jax.ShapeDtypeStruct((n...]
    ppermute x3, waiting for transfers between devices: 1.05 us -> 0.6 us  [across(): lax.ppermute(v, both, [(2 * i + w, 2 * (i ^ k) + 1 - w) for i in range(n)...]
    ppermute x3, starting transfers between devices: 4.82 us -> 5.2 us  [across(): lax.ppermute(v, both, [(2 * i + w, 2 * (i ^ k) + 1 - w) for i in range(n)...]
  transfers between devices with their start and end apart: 13 -> 13, of which waited for: 6 -> 5; matrix products, arithmetic and copies ran while one was open for 0% -> 0% of each run, Pallas kernels for 26% -> 20%
where the time goes in v4:
time: 31.7 us; the launch traced here: 31.5 us
  starting transfers between devices  18.5 us (58%)
  Pallas kernels  8.47 us (27%)
  waiting for transfers between devices  4.49 us (14%)
    ppermute x6, starting transfers between devices, partner(): return lax.ppermute(v, 'ffn', [(i, i ^ k) for i in range(n)])  12 us
    pallas_call x4, Pallas kernels, small(): call(functools.partial(base_kernel, a, 512), [jax.ShapeDtypeStruct((half,...  5.45 us
    ppermute x3, starting transfers between devices, across(): lax.ppermute(v, both, [(2 * i + w, 2 * (i ^ k) + 1 - w) for i in range(n)...  5.2 us
    ppermute x6, waiting for transfers between devices, partner(): return lax.ppermute(v, 'ffn', [(i, i ^ k) for i in range(n)])  3.74 us
    ppermute x4, starting transfers between devices, swap(): return lax.ppermute(v, 'width', [(0, 1), (1, 0)])  1.23 us
    pallas_call x1, Pallas kernels, small(): call(pack_kernel, [jax.ShapeDtypeStruct((1, rows, wide + LANES), BF16), j...  1.02 us
    pallas_call x1, Pallas kernels, small(): call(delta_kernel, jax.ShapeDtypeStruct((half, columns), F32), [VMEM] * (...  0.82 us
    pallas_call x1, Pallas kernels, small(): call(finish_kernel, jax.ShapeDtypeStruct((half, columns), BF16), [VMEM, V...  0.72 us
  transfers between devices with their start and end apart: 13, of which 5 were waited for; matrix products, arithmetic and copies ran while one was open for 0% of the time, Pallas kernels for 20%

profile of v4, /device:TPU:0, one launch (start us, length us, event | category | flops | bytes accessed | tf_op | source)
XLA Modules:
  0.0 31.5 jit_solution(5158225915876197263)
XLA Ops:
  0.0 1.0 %shard_map.64 = (bf16[1,8,4224]{2,1,0:T(8,128)(2,1)S(1)}, f32[8,128]{1,0:T(8,128)S(1)}) custom-call(s32[8]{0:T(128)} %ids_far.1, s32[8]{0:T(128)} %holder_far.1, bf16[8,4096]{1,0:T(8,128)(2,1)} %tokens.1), custom_call_target="tpu_custom_call" | custom-call | flops 42949672960 | bytes 131072 | tf_op jit(solution)/shard_map/pallas_call | solution.py:191
  1.0 4.1 %collective-permute-start.2 = (bf16[1,8,4224]{2,1,0:T(8,128)(2,1)S(1)}, bf16[1,8,4224]{2,1,0:T(8,128)(2,1)S(1)}, u32[]{:S(2)}, u32[]{:S(2)}) collective-permute-start(bf16[1,8,4224]{2,1,0:T(8,128)(2,1)S(1)} %get-tuple-element.24.refs_0_), channel_id=1, source_target_pairs={{0,8},{2,10},{4,12},{6,14},{8,0},{10,2},{12,4},{14,6},{1,9},{3,11}... | collective-permute-start | bytes 202760 | tf_op jit(solution)/shard_map/ppermute | solution.py:182
  5.1 1.6 %collective-permute-start.1 = (bf16[1,8,4224]{2,1,0:T(8,128)(2,1)S(1)}, bf16[1,8,4224]{2,1,0:T(8,128)(2,1)S(1)}, u32[]{:S(2)}, u32[]{:S(2)}) collective-permute-start(bf16[1,8,4224]{2,1,0:T(8,128)(2,1)S(1)} %get-tuple-element.24.refs_0_), channel_id=1, source_target_pairs={{0,4},{2,6},{4,0},{6,2},{8,12},{10,14},{12,8},{14,10},{1,5},{3,7},... | collective-permute-start | bytes 202760 | tf_op jit(solution)/shard_map/ppermute | solution.py:182
  6.7 1.5 %collective-permute-start = (bf16[1,8,4224]{2,1,0:T(8,128)(2,1)S(1)}, bf16[1,8,4224]{2,1,0:T(8,128)(2,1)S(1)}, u32[]{:S(2)}, u32[]{:S(2)}) collective-permute-start(bf16[1,8,4224]{2,1,0:T(8,128)(2,1)S(1)} %get-tuple-element.24.refs_0_), channel_id=1, source_target_pairs={{0,2},{2,0},{4,6},{6,4},{8,10},{10,8},{12,14},{14,12},{1,3},{3,1},... | collective-permute-start | bytes 202760 | tf_op jit(solution)/shard_map/ppermute | solution.py:182
  8.2 1.4 %collective-permute-start.3 = (bf16[1,8,4224]{2,1,0:T(8,128)(2,1)S(1)}, bf16[1,8,4224]{2,1,0:T(8,128)(2,1)S(1)}, u32[]{:S(2)}, u32[]{:S(2)}) collective-permute-start(bf16[1,8,4224]{2,1,0:T(8,128)(2,1)S(1)} %collective-permute-done.2.refs_1_.refs_3_), channel_id=1, source_target_pairs={{0,4},{2,6},{4,0},{6,2},{8,12},{10,14},{12,8},{14,10},{1,5},{3,7},... | collective-permute-start | bytes 202760 | tf_op jit(solution)/shard_map/ppermute | solution.py:182
  9.6 1.6 %collective-permute-start.4 = (bf16[2,8,4224]{2,1,0:T(8,128)(2,1)S(1)}, bf16[2,8,4224]{2,1,0:T(8,128)(2,1)S(1)}, u32[]{:S(2)}, u32[]{:S(2)}) collective-permute-start(bf16[2,8,4224]{2,1,0:T(8,128)(2,1)S(1)} %shard_map.65), channel_id=1, source_target_pairs={{0,2},{2,0},{4,6},{6,4},{8,10},{10,8},{12,14},{14,12},{1,3},{3,1},... | collective-permute-start | bytes 405512 | tf_op jit(solution)/shard_map/ppermute | solution.py:182
  11.2 1.3 %collective-permute-done.3.refs_4_ = bf16[1,8,4224]{2,1,0:T(8,128)(2,1)S(1)} collective-permute-done((bf16[1,8,4224]{2,1,0:T(8,128)(2,1)S(1)}, bf16[1,8,4224]{2,1,0:T(8,128)(2,1)S(1)}, u32[]{:S(2)}, u32[]{:S(2)}) %collective-permute-start.3) | collective-permute-done | bytes 67616 | tf_op jit(solution)/shard_map/ppermute | solution.py:182
  12.5 1.9 %collective-permute-start.5 = (bf16[1,8,4224]{2,1,0:T(8,128)(2,1)S(1)}, bf16[1,8,4224]{2,1,0:T(8,128)(2,1)S(1)}, u32[]{:S(2)}, u32[]{:S(2)}) collective-permute-start(bf16[1,8,4224]{2,1,0:T(8,128)(2,1)S(1)} %collective-permute-done.3.refs_4_), channel_id=1, source_target_pairs={{0,2},{2,0},{4,6},{6,4},{8,10},{10,8},{12,14},{14,12},{1,3},{3,1},... | collective-permute-start | bytes 202760 | tf_op jit(solution)/shard_map/ppermute | solution.py:182
  14.4 2.4 %collective-permute-done.5.refs_6_ = bf16[1,8,4224]{2,1,0:T(8,128)(2,1)S(1)} collective-permute-done((bf16[1,8,4224]{2,1,0:T(8,128)(2,1)S(1)}, bf16[1,8,4224]{2,1,0:T(8,128)(2,1)S(1)}, u32[]{:S(2)}, u32[]{:S(2)}) %collective-permute-start.5) | collective-permute-done | bytes 67616 | tf_op jit(solution)/shard_map/ppermute | solution.py:182
  16.8 0.4 %shard_map.66 = (bf16[64,4096]{1,0:T(8,128)(2,1)S(1)}, f32[64,128]{1,0:T(8,128)S(1)}, f32[32,128]{1,0:T(8,128)S(1)}) custom-call(f32[8,128]{1,0:T(8,128)S(1)} %get-tuple-element.23.held, bf16[64,4096]{1,0:T(8,128)(2,1)S(1)} %bitcast.3, bf16[8,32,3584]{2,1,0:T(8,128)(2,1)S(1)} %copy-done.1, bf16[1,8,4224]{2,1,0:T(8,128)(2,1)S(1)} %get-tuple-element.24.refs_0_, ...), custom_call_target="tpu_custom_call" | custom-call | tf_op jit(solution)/shard_map/pallas_call | solution.py:204
  17.3 1.0 %shard_map.67 = (f32[32,640]{1,0:T(8,128)S(1)}, f32[32,640]{1,0:T(8,128)S(1)}) custom-call(bf16[64,4096]{1,0:T(8,128)(2,1)S(1)} %get-tuple-element.26.x, bf16[4096,3584]{1,0:T(8,128)(2,1)S(1)} %copy-done, f32[32,128]{1,0:T(8,128)S(1)} %get-tuple-element.27._.a), custom_call_target="tpu_custom_call" | custom-call | tf_op jit(solution)/shard_map/pallas_call | solution.py:227
  18.5 0.4 %collective-permute-start.10 = (bf16[8,32,3584]{2,1,0:T(8,128)(2,1)S(1)}, bf16[8,32,3584]{2,1,0:T(8,128)(2,1)S(1)}, u32[]{:S(2)}, u32[]{:S(2)}) collective-permute-start(bf16[8,32,3584]{2,1,0:T(8,128)(2,1)S(1)} %copy-done.1), channel_id=1, source_target_pairs={{0,1},{1,0},{2,3},{3,2},{4,5},{5,4},{6,7},{7,6},{8,9},{9,8},{10,11... | collective-permute-start | bytes 5505032 | tf_op jit(solution)/shard_map/ppermute | solution.py:179
  18.9 1.6 %collective-permute-start.7 = (f32[32,128]{1,0:T(8,128)S(1)}, f32[32,128]{1,0:T(8,128)S(1)}, u32[]{:S(2)}, u32[]{:S(2)}) collective-permute-start(f32[32,128]{1,0:T(8,128)S(1)} %shard_map.68._.a), channel_id=1, source_target_pairs={{0,3},{1,2},{2,1},{3,0},{4,7},{5,6},{6,5},{7,4},{8,11},{9,10},{10,... | collective-permute-start | bytes 49160 | tf_op jit(solution)/shard_map/ppermute | solution.py:185
  20.5 1.7 %shard_map.69 = (f32[32,1152]{1,0:T(8,128)S(1)}, f32[32,1792]{1,0:T(8,128)S(1)}) custom-call(bf16[64,4096]{1,0:T(8,128)(2,1)S(1)} %get-tuple-element.26.x, bf16[4096,3584]{1,0:T(8,128)(2,1)S(1)} %copy-done, f32[32,128]{1,0:T(8,128)S(1)} %shard_map.68._.a, f32[32,640]{1,0:T(8,128)S(1)} %get-tuple-element.30.refs_0_), custom_call_target="tpu_custom_call" | custom-call | tf_op jit(solution)/shard_map/pallas_call | solution.py:227
  22.2 1.1 %collective-permute-start.8 = (f32[32,128]{1,0:T(8,128)S(1)}, f32[32,128]{1,0:T(8,128)S(1)}, u32[]{:S(2)}, u32[]{:S(2)}) collective-permute-start(f32[32,128]{1,0:T(8,128)S(1)} %shard_map.70._.a), channel_id=1, source_target_pairs={{0,5},{1,4},{2,7},{3,6},{4,1},{5,0},{6,3},{7,2},{8,13},{9,12},{10,... | collective-permute-start | bytes 49160 | tf_op jit(solution)/shard_map/ppermute | solution.py:185
  23.3 1.7 %shard_map.71 = (f32[32,1152]{1,0:T(8,128)S(1)}, f32[32,2944]{1,0:T(8,128)S(1)}) custom-call(bf16[64,4096]{1,0:T(8,128)(2,1)S(1)} %get-tuple-element.26.x, bf16[4096,3584]{1,0:T(8,128)(2,1)S(1)} %copy-done, f32[32,128]{1,0:T(8,128)S(1)} %shard_map.70._.a, f32[32,1792]{1,0:T(8,128)S(1)} %get-tuple-element.32.refs_0_), custom_call_target="tpu_custom_call" | custom-call | tf_op jit(solution)/shard_map/pallas_call | solution.py:227
  25.0 0.4 %collective-permute-done.8.b = f32[32,128]{1,0:T(8,128)S(1)} collective-permute-done((f32[32,128]{1,0:T(8,128)S(1)}, f32[32,128]{1,0:T(8,128)S(1)}, u32[]{:S(2)}, u32[]{:S(2)}) %collective-permute-start.8) | collective-permute-done | bytes 16416 | tf_op jit(solution)/shard_map/ppermute | solution.py:185
  25.5 0.4 %collective-permute-start.11 = (f32[32,2944]{1,0:T(8,128)S(1)}, f32[32,2944]{1,0:T(8,128)S(1)}, u32[]{:S(2)}, u32[]{:S(2)}) collective-permute-start(f32[32,2944]{1,0:T(8,128)S(1)} %get-tuple-element.39), channel_id=1, source_target_pairs={{0,1},{1,0},{2,3},{3,2},{4,5},{5,4},{6,7},{7,6},{8,9},{9,8},{10,11... | collective-permute-start | bytes 1130504 | tf_op jit(solution)/shard_map/ppermute | solution.py:179
  25.9 2.5 %collective-permute-start.9 = (f32[32,128]{1,0:T(8,128)S(1)}, f32[32,128]{1,0:T(8,128)S(1)}, u32[]{:S(2)}, u32[]{:S(2)}) collective-permute-start(f32[32,128]{1,0:T(8,128)S(1)} %shard_map.72._.a), channel_id=1, source_target_pairs={{0,9},{1,8},{2,11},{3,10},{4,13},{5,12},{6,15},{7,14},{8,1},{9,0},... | collective-permute-start | bytes 49160 | tf_op jit(solution)/shard_map/ppermute | solution.py:185
  28.4 1.0 %shard_map.73 = (f32[32,640]{1,0:T(8,128)S(1)}, f32[32,640]{1,0:T(8,128)S(1)}) custom-call(bf16[64,4096]{1,0:T(8,128)(2,1)S(1)} %get-tuple-element.26.x, bf16[4096,3584]{1,0:T(8,128)(2,1)S(1)} %copy-done, f32[32,128]{1,0:T(8,128)S(1)} %shard_map.72._.a), custom_call_target="tpu_custom_call" | custom-call | tf_op jit(solution)/shard_map/pallas_call | solution.py:227
  29.5 0.3 %collective-permute-start.12 = (f32[32,640]{1,0:T(8,128)S(1)}, f32[32,640]{1,0:T(8,128)S(1)}, u32[]{:S(2)}, u32[]{:S(2)}) collective-permute-start(f32[32,640]{1,0:T(8,128)S(1)} %get-tuple-element.40), channel_id=1, source_target_pairs={{0,1},{1,0},{2,3},{3,2},{4,5},{5,4},{6,7},{7,6},{8,9},{9,8},{10,11... | collective-permute-start | bytes 245768 | tf_op jit(solution)/shard_map/ppermute | solution.py:179
  29.8 0.2 collective-permute-done.9.b
  30.0 0.8 %shard_map.75.total = f32[32,3584]{1,0:T(8,128)S(1)} custom-call(f32[32,128]{1,0:T(8,128)S(1)} %shard_map.74.low, f32[64,128]{1,0:T(8,128)S(1)} %get-tuple-element.37.ids, bf16[8,32,3584]{2,1,0:T(8,128)(2,1)S(1)} %copy-done.1, bf16[8,32,3584]{2,1,0:T(8,128)(2,1)S(1)} %collective-permute-done.10.up_peer, f32[32,2944]{1,0:T(8,128)S(1)} %collective-permute-done.11.got, ...), custom_call_target="tpu_custom_call" | custom-call | flops 4294967296 | tf_op jit(solution)/shard_map/pallas_call | solution.py:249
  30.8 0.7 %shard_map.76 = bf16[32,3584]{1,0:T(8,128)(2,1)} custom-call(f32[32,3584]{1,0:T(8,128)S(1)} %shard_map.75.total, f32[32,640]{1,0:T(8,128)S(1)} %collective-permute-done.12.got), custom_call_target="tpu_custom_call" | custom-call | tf_op jit(solution)/shard_map/pallas_call | solution.py:253
  (21 shorter events, 0.2 us)
Async XLA Ops:
  0.0 16.8 %copy-start.1 = (bf16[8,32,3584]{2,1,0:T(8,128)(2,1)S(1)}, bf16[8,32,3584]{2,1,0:T(8,128)(2,1)}, u32[]{:S(2)}) copy-start(bf16[8,32,3584]{2,1,0:T(8,128)(2,1)} %up_own) | copy-start | bytes 5505028
  0.0 16.8 %copy-start.2 = (bf16[1,4096,64]{1,2,0:T(8,128)(2,1)S(1)}, bf16[1,4096,64]{1,2,0:T(8,128)(2,1)}, u32[]{:S(2)}) copy-start(bf16[1,4096,64]{1,2,0:T(8,128)(2,1)} %param.10) | copy-start | bytes 1572868
  0.0 17.3 %copy-start = (bf16[4096,3584]{1,0:T(8,128)(2,1)S(1)}, bf16[4096,3584]{1,0:T(8,128)(2,1)}, u32[]{:S(2)}) copy-start(bf16[4096,3584]{1,0:T(8,128)(2,1)} %w.7) | copy-start | bytes 88080384
  1.0 7.2 %collective-permute-start.2 = (bf16[1,8,4224]{2,1,0:T(8,128)(2,1)S(1)}, bf16[1,8,4224]{2,1,0:T(8,128)(2,1)S(1)}, u32[]{:S(2)}, u32[]{:S(2)}) collective-permute-start(bf16[1,8,4224]{2,1,0:T(8,128)(2,1)S(1)} %get-tuple-element.24.refs_0_), channel_id=1, source_target_pairs={{0,8},{2,10},{4,12},{6,14},{8,0},{10,2},{12,4},{14,6},{1,9},{3,11}... | collective-permute-start | bytes 202760 | tf_op jit(solution)/shard_map/ppermute | solution.py:182
  5.1 4.5 %collective-permute-start.1 = (bf16[1,8,4224]{2,1,0:T(8,128)(2,1)S(1)}, bf16[1,8,4224]{2,1,0:T(8,128)(2,1)S(1)}, u32[]{:S(2)}, u32[]{:S(2)}) collective-permute-start(bf16[1,8,4224]{2,1,0:T(8,128)(2,1)S(1)} %get-tuple-element.24.refs_0_), channel_id=1, source_target_pairs={{0,4},{2,6},{4,0},{6,2},{8,12},{10,14},{12,8},{14,10},{1,5},{3,7},... | collective-permute-start | bytes 202760 | tf_op jit(solution)/shard_map/ppermute | solution.py:182
  6.7 4.5 %collective-permute-start = (bf16[1,8,4224]{2,1,0:T(8,128)(2,1)S(1)}, bf16[1,8,4224]{2,1,0:T(8,128)(2,1)S(1)}, u32[]{:S(2)}, u32[]{:S(2)}) collective-permute-start(bf16[1,8,4224]{2,1,0:T(8,128)(2,1)S(1)} %get-tuple-element.24.refs_0_), channel_id=1, source_target_pairs={{0,2},{2,0},{4,6},{6,4},{8,10},{10,8},{12,14},{14,12},{1,3},{3,1},... | collective-permute-start | bytes 202760 | tf_op jit(solution)/shard_map/ppermute | solution.py:182
  8.2 4.3 %collective-permute-start.3 = (bf16[1,8,4224]{2,1,0:T(8,128)(2,1)S(1)}, bf16[1,8,4224]{2,1,0:T(8,128)(2,1)S(1)}, u32[]{:S(2)}, u32[]{:S(2)}) collective-permute-start(bf16[1,8,4224]{2,1,0:T(8,128)(2,1)S(1)} %collective-permute-done.2.refs_1_.refs_3_), channel_id=1, source_target_pairs={{0,4},{2,6},{4,0},{6,2},{8,12},{10,14},{12,8},{14,10},{1,5},{3,7},... | collective-permute-start | bytes 202760 | tf_op jit(solution)/shard_map/ppermute | solution.py:182
  9.6 7.2 %collective-permute-start.4 = (bf16[2,8,4224]{2,1,0:T(8,128)(2,1)S(1)}, bf16[2,8,4224]{2,1,0:T(8,128)(2,1)S(1)}, u32[]{:S(2)}, u32[]{:S(2)}) collective-permute-start(bf16[2,8,4224]{2,1,0:T(8,128)(2,1)S(1)} %shard_map.65), channel_id=1, source_target_pairs={{0,2},{2,0},{4,6},{6,4},{8,10},{10,8},{12,14},{14,12},{1,3},{3,1},... | collective-permute-start | bytes 405512 | tf_op jit(solution)/shard_map/ppermute | solution.py:182
  12.5 4.3 %collective-permute-start.5 = (bf16[1,8,4224]{2,1,0:T(8,128)(2,1)S(1)}, bf16[1,8,4224]{2,1,0:T(8,128)(2,1)S(1)}, u32[]{:S(2)}, u32[]{:S(2)}) collective-permute-start(bf16[1,8,4224]{2,1,0:T(8,128)(2,1)S(1)} %collective-permute-done.3.refs_4_), channel_id=1, source_target_pairs={{0,2},{2,0},{4,6},{6,4},{8,10},{10,8},{12,14},{14,12},{1,3},{3,1},... | collective-permute-start | bytes 202760 | tf_op jit(solution)/shard_map/ppermute | solution.py:182
  17.3 1.2 %collective-permute-start.6 = (f32[32,128]{1,0:T(8,128)S(1)}, f32[32,128]{1,0:T(8,128)S(1)}, u32[]{:S(2)}, u32[]{:S(2)}) collective-permute-start(f32[32,128]{1,0:T(8,128)S(1)} %get-tuple-element.27._.a), channel_id=1, source_target_pairs={{0,1},{1,0},{2,3},{3,2},{4,5},{5,4},{6,7},{7,6},{8,9},{9,8},{10,11... | collective-permute-start | bytes 49160 | tf_op jit(solution)/shard_map/ppermute | solution.py:179
  18.5 11.5 %collective-permute-start.10 = (bf16[8,32,3584]{2,1,0:T(8,128)(2,1)S(1)}, bf16[8,32,3584]{2,1,0:T(8,128)(2,1)S(1)}, u32[]{:S(2)}, u32[]{:S(2)}) collective-permute-start(bf16[8,32,3584]{2,1,0:T(8,128)(2,1)S(1)} %copy-done.1), channel_id=1, source_target_pairs={{0,1},{1,0},{2,3},{3,2},{4,5},{5,4},{6,7},{7,6},{8,9},{9,8},{10,11... | collective-permute-start | bytes 5505032 | tf_op jit(solution)/shard_map/ppermute | solution.py:179
  18.9 3.3 %collective-permute-start.7 = (f32[32,128]{1,0:T(8,128)S(1)}, f32[32,128]{1,0:T(8,128)S(1)}, u32[]{:S(2)}, u32[]{:S(2)}) collective-permute-start(f32[32,128]{1,0:T(8,128)S(1)} %shard_map.68._.a), channel_id=1, source_target_pairs={{0,3},{1,2},{2,1},{3,0},{4,7},{5,6},{6,5},{7,4},{8,11},{9,10},{10,... | collective-permute-start | bytes 49160 | tf_op jit(solution)/shard_map/ppermute | solution.py:185
  22.2 3.2 %collective-permute-start.8 = (f32[32,128]{1,0:T(8,128)S(1)}, f32[32,128]{1,0:T(8,128)S(1)}, u32[]{:S(2)}, u32[]{:S(2)}) collective-permute-start(f32[32,128]{1,0:T(8,128)S(1)} %shard_map.70._.a), channel_id=1, source_target_pairs={{0,5},{1,4},{2,7},{3,6},{4,1},{5,0},{6,3},{7,2},{8,13},{9,12},{10,... | collective-permute-start | bytes 49160 | tf_op jit(solution)/shard_map/ppermute | solution.py:185
  25.5 4.5 %collective-permute-start.11 = (f32[32,2944]{1,0:T(8,128)S(1)}, f32[32,2944]{1,0:T(8,128)S(1)}, u32[]{:S(2)}, u32[]{:S(2)}) collective-permute-start(f32[32,2944]{1,0:T(8,128)S(1)} %get-tuple-element.39), channel_id=1, source_target_pairs={{0,1},{1,0},{2,3},{3,2},{4,5},{5,4},{6,7},{7,6},{8,9},{9,8},{10,11... | collective-permute-start | bytes 1130504 | tf_op jit(solution)/shard_map/ppermute | solution.py:179
  25.9 4.1 %collective-permute-start.9 = (f32[32,128]{1,0:T(8,128)S(1)}, f32[32,128]{1,0:T(8,128)S(1)}, u32[]{:S(2)}, u32[]{:S(2)}) collective-permute-start(f32[32,128]{1,0:T(8,128)S(1)} %shard_map.72._.a), channel_id=1, source_target_pairs={{0,9},{1,8},{2,11},{3,10},{4,13},{5,12},{6,15},{7,14},{8,1},{9,0},... | collective-permute-start | bytes 49160 | tf_op jit(solution)/shard_map/ppermute | solution.py:185
  29.5 1.4 %collective-permute-start.12 = (f32[32,640]{1,0:T(8,128)S(1)}, f32[32,640]{1,0:T(8,128)S(1)}, u32[]{:S(2)}, u32[]{:S(2)}) collective-permute-start(f32[32,640]{1,0:T(8,128)S(1)} %get-tuple-element.40), channel_id=1, source_target_pairs={{0,1},{1,0},{2,3},{3,2},{4,5},{5,4},{6,7},{7,6},{8,9},{9,8},{10,11... | collective-permute-start | bytes 245768 | tf_op jit(solution)/shard_map/ppermute | solution.py:179

commit v5 on v4

--- a/solution.py
+++ b/solution.py
@@ -127,16 +127,17 @@
         return jnp.where(picked, values, 0.0).astype(BF16)
 
     a, b = spread(w), spread(1 - w)
-    c = 0
+    at = 0
     for o in own:
-        s = o.shape[1]
-        delta = jnp.dot(a, up_own[:, :, c : c + s].reshape(count * part, s), preferred_element_type=F32)
-        delta = delta + jnp.dot(b, up_peer[:, :, c : c + s].reshape(count * part, s), preferred_element_type=F32)
-        total = o[...] + delta
-        if c < got.shape[1]:
-            total = total + got[:, c : c + s]
-        out[:, c : c + s] = total
-        c += s
+        for c in range(0, o.shape[1], LANES):
+            s = slice(at + c, at + c + LANES)
+            total = o[:, c : c + LANES]
+            total = total + jnp.dot(a, up_own[:, :, s].reshape(count * part, LANES), preferred_element_type=F32)
+            total = total + jnp.dot(b, up_peer[:, :, s].reshape(count * part, LANES), preferred_element_type=F32)
+            if s.stop <= got.shape[1]:
+                total = total + got[:, s]
+            out[:, s] = total
+        at += o.shape[1]
 
 
 def finish_kernel(total, got, out):
@@ -225,7 +226,7 @@
         last = i == len(steps) - 1
         kept = [] if sent is None or last else [sent]
         o, s = call(
-            functools.partial(base_kernel, a, 512),
+            functools.partial(base_kernel, a, 128),
             [
                 jax.ShapeDtypeStruct((half, b - a), F32),
                 jax.ShapeDtypeStruct((half, b - a if last else b), F32),

time: 31.7 us -> 31.3 us (0.987)
  Pallas kernels: 8.47 us -> 7.75 us
  waiting for transfers between devices: 4.49 us -> 4.86 us
    pallas_call x4, Pallas kernels: 5.45 us -> 4.75 us  [small(): call(functools.partial(base_kernel, a, 128), [jax.ShapeDtypeStruct((half,...]
  transfers between devices with their start and end apart: 13 -> 13, of which waited for: 5 -> 5; matrix products, arithmetic and copies ran while one was open for 0% -> 0% of each run, Pallas kernels for 20% -> 18%
where the time goes in v5:
time: 31.3 us; the launch traced here: 31.1 us
  starting transfers between devices  18.4 us (59%)
  Pallas kernels  7.75 us (25%)
  waiting for transfers between devices  4.86 us (16%)
    ppermute x6, starting transfers between devices, partner(): return lax.ppermute(v, 'ffn', [(i, i ^ k) for i in range(n)])  12 us
    ppermute x3, starting transfers between devices, across(): lax.ppermute(v, both, [(2 * i + w, 2 * (i ^ k) + 1 - w) for i in range(n)...  5.37 us
    pallas_call x4, Pallas kernels, small(): call(functools.partial(base_kernel, a, 128), [jax.ShapeDtypeStruct((half,...  4.75 us
    ppermute x6, waiting for transfers between devices, partner(): return lax.ppermute(v, 'ffn', [(i, i ^ k) for i in range(n)])  3.74 us
    pallas_call x1, Pallas kernels, small(): call(pack_kernel, [jax.ShapeDtypeStruct((1, rows, wide + LANES), BF16), j...  1.02 us
    ppermute x4, starting transfers between devices, swap(): return lax.ppermute(v, 'width', [(0, 1), (1, 0)])  1.01 us
    ppermute x3, waiting for transfers between devices, across(): lax.ppermute(v, both, [(2 * i + w, 2 * (i ^ k) + 1 - w) for i in range(n)...  0.85 us
    pallas_call x1, Pallas kernels, small(): call(delta_kernel, jax.ShapeDtypeStruct((half, columns), F32), [VMEM] * (...  0.79 us
  transfers between devices with their start and end apart: 13, of which 5 were waited for; matrix products, arithmetic and copies ran while one was open for 0% of the time, Pallas kernels for 18%

profile of v5, /device:TPU:0, one launch (start us, length us, event | category | flops | bytes accessed | tf_op | source)
XLA Modules:
  0.0 31.1 jit_solution(12462188176314739492)
XLA Ops:
  0.0 1.0 %shard_map.64 = (bf16[1,8,4224]{2,1,0:T(8,128)(2,1)S(1)}, f32[8,128]{1,0:T(8,128)S(1)}) custom-call(s32[8]{0:T(128)} %ids_far.1, s32[8]{0:T(128)} %holder_far.1, bf16[8,4096]{1,0:T(8,128)(2,1)} %tokens.1), custom_call_target="tpu_custom_call" | custom-call | flops 42949672960 | bytes 131072 | tf_op jit(solution)/shard_map/pallas_call | solution.py:192
  1.0 4.1 %collective-permute-start.2 = (bf16[1,8,4224]{2,1,0:T(8,128)(2,1)S(1)}, bf16[1,8,4224]{2,1,0:T(8,128)(2,1)S(1)}, u32[]{:S(2)}, u32[]{:S(2)}) collective-permute-start(bf16[1,8,4224]{2,1,0:T(8,128)(2,1)S(1)} %get-tuple-element.24.refs_0_), channel_id=1, source_target_pairs={{0,8},{2,10},{4,12},{6,14},{8,0},{10,2},{12,4},{14,6},{1,9},{3,11}... | collective-permute-start | bytes 202760 | tf_op jit(solution)/shard_map/ppermute | solution.py:183
  5.1 1.6 %collective-permute-start.1 = (bf16[1,8,4224]{2,1,0:T(8,128)(2,1)S(1)}, bf16[1,8,4224]{2,1,0:T(8,128)(2,1)S(1)}, u32[]{:S(2)}, u32[]{:S(2)}) collective-permute-start(bf16[1,8,4224]{2,1,0:T(8,128)(2,1)S(1)} %get-tuple-element.24.refs_0_), channel_id=1, source_target_pairs={{0,4},{2,6},{4,0},{6,2},{8,12},{10,14},{12,8},{14,10},{1,5},{3,7},... | collective-permute-start | bytes 202760 | tf_op jit(solution)/shard_map/ppermute | solution.py:183
  6.7 1.5 %collective-permute-start = (bf16[1,8,4224]{2,1,0:T(8,128)(2,1)S(1)}, bf16[1,8,4224]{2,1,0:T(8,128)(2,1)S(1)}, u32[]{:S(2)}, u32[]{:S(2)}) collective-permute-start(bf16[1,8,4224]{2,1,0:T(8,128)(2,1)S(1)} %get-tuple-element.24.refs_0_), channel_id=1, source_target_pairs={{0,2},{2,0},{4,6},{6,4},{8,10},{10,8},{12,14},{14,12},{1,3},{3,1},... | collective-permute-start | bytes 202760 | tf_op jit(solution)/shard_map/ppermute | solution.py:183
  8.2 1.4 %collective-permute-start.3 = (bf16[1,8,4224]{2,1,0:T(8,128)(2,1)S(1)}, bf16[1,8,4224]{2,1,0:T(8,128)(2,1)S(1)}, u32[]{:S(2)}, u32[]{:S(2)}) collective-permute-start(bf16[1,8,4224]{2,1,0:T(8,128)(2,1)S(1)} %collective-permute-done.2.refs_1_.refs_3_), channel_id=1, source_target_pairs={{0,4},{2,6},{4,0},{6,2},{8,12},{10,14},{12,8},{14,10},{1,5},{3,7},... | collective-permute-start | bytes 202760 | tf_op jit(solution)/shard_map/ppermute | solution.py:183
  9.6 1.6 %collective-permute-start.4 = (bf16[2,8,4224]{2,1,0:T(8,128)(2,1)S(1)}, bf16[2,8,4224]{2,1,0:T(8,128)(2,1)S(1)}, u32[]{:S(2)}, u32[]{:S(2)}) collective-permute-start(bf16[2,8,4224]{2,1,0:T(8,128)(2,1)S(1)} %shard_map.65), channel_id=1, source_target_pairs={{0,2},{2,0},{4,6},{6,4},{8,10},{10,8},{12,14},{14,12},{1,3},{3,1},... | collective-permute-start | bytes 405512 | tf_op jit(solution)/shard_map/ppermute | solution.py:183
  11.2 1.3 %collective-permute-done.3.refs_4_ = bf16[1,8,4224]{2,1,0:T(8,128)(2,1)S(1)} collective-permute-done((bf16[1,8,4224]{2,1,0:T(8,128)(2,1)S(1)}, bf16[1,8,4224]{2,1,0:T(8,128)(2,1)S(1)}, u32[]{:S(2)}, u32[]{:S(2)}) %collective-permute-start.3) | collective-permute-done | bytes 67616 | tf_op jit(solution)/shard_map/ppermute | solution.py:183
  12.5 1.9 %collective-permute-start.5 = (bf16[1,8,4224]{2,1,0:T(8,128)(2,1)S(1)}, bf16[1,8,4224]{2,1,0:T(8,128)(2,1)S(1)}, u32[]{:S(2)}, u32[]{:S(2)}) collective-permute-start(bf16[1,8,4224]{2,1,0:T(8,128)(2,1)S(1)} %collective-permute-done.3.refs_4_), channel_id=1, source_target_pairs={{0,2},{2,0},{4,6},{6,4},{8,10},{10,8},{12,14},{14,12},{1,3},{3,1},... | collective-permute-start | bytes 202760 | tf_op jit(solution)/shard_map/ppermute | solution.py:183
  14.4 2.4 %collective-permute-done.5.refs_6_ = bf16[1,8,4224]{2,1,0:T(8,128)(2,1)S(1)} collective-permute-done((bf16[1,8,4224]{2,1,0:T(8,128)(2,1)S(1)}, bf16[1,8,4224]{2,1,0:T(8,128)(2,1)S(1)}, u32[]{:S(2)}, u32[]{:S(2)}) %collective-permute-start.5) | collective-permute-done | bytes 67616 | tf_op jit(solution)/shard_map/ppermute | solution.py:183
  16.8 0.4 %shard_map.66 = (bf16[64,4096]{1,0:T(8,128)(2,1)S(1)}, f32[64,128]{1,0:T(8,128)S(1)}, f32[32,128]{1,0:T(8,128)S(1)}) custom-call(f32[8,128]{1,0:T(8,128)S(1)} %get-tuple-element.23.held, bf16[64,4096]{1,0:T(8,128)(2,1)S(1)} %bitcast.3, bf16[8,32,3584]{2,1,0:T(8,128)(2,1)S(1)} %copy-done.1, bf16[1,8,4224]{2,1,0:T(8,128)(2,1)S(1)} %get-tuple-element.24.refs_0_, ...), custom_call_target="tpu_custom_call" | custom-call | tf_op jit(solution)/shard_map/pallas_call | solution.py:205
  17.3 0.9 %shard_map.67 = (f32[32,640]{1,0:T(8,128)S(1)}, f32[32,640]{1,0:T(8,128)S(1)}) custom-call(bf16[64,4096]{1,0:T(8,128)(2,1)S(1)} %get-tuple-element.26.x, bf16[4096,3584]{1,0:T(8,128)(2,1)S(1)} %copy-done, f32[32,128]{1,0:T(8,128)S(1)} %get-tuple-element.27._.a), custom_call_target="tpu_custom_call" | custom-call | tf_op jit(solution)/shard_map/pallas_call | solution.py:228
  18.5 0.3 collective-permute-start.10
  18.8 1.7 %collective-permute-start.7 = (f32[32,128]{1,0:T(8,128)S(1)}, f32[32,128]{1,0:T(8,128)S(1)}, u32[]{:S(2)}, u32[]{:S(2)}) collective-permute-start(f32[32,128]{1,0:T(8,128)S(1)} %shard_map.68._.a), channel_id=1, source_target_pairs={{0,3},{1,2},{2,1},{3,0},{4,7},{5,6},{6,5},{7,4},{8,11},{9,10},{10,... | collective-permute-start | bytes 49160 | tf_op jit(solution)/shard_map/ppermute | solution.py:186
  20.5 1.5 %shard_map.69 = (f32[32,1152]{1,0:T(8,128)S(1)}, f32[32,1792]{1,0:T(8,128)S(1)}) custom-call(bf16[64,4096]{1,0:T(8,128)(2,1)S(1)} %get-tuple-element.26.x, bf16[4096,3584]{1,0:T(8,128)(2,1)S(1)} %copy-done, f32[32,128]{1,0:T(8,128)S(1)} %shard_map.68._.a, f32[32,640]{1,0:T(8,128)S(1)} %get-tuple-element.30.refs_0_), custom_call_target="tpu_custom_call" | custom-call | tf_op jit(solution)/shard_map/pallas_call | solution.py:228
  22.0 1.2 %collective-permute-start.8 = (f32[32,128]{1,0:T(8,128)S(1)}, f32[32,128]{1,0:T(8,128)S(1)}, u32[]{:S(2)}, u32[]{:S(2)}) collective-permute-start(f32[32,128]{1,0:T(8,128)S(1)} %shard_map.70._.a), channel_id=1, source_target_pairs={{0,5},{1,4},{2,7},{3,6},{4,1},{5,0},{6,3},{7,2},{8,13},{9,12},{10,... | collective-permute-start | bytes 49160 | tf_op jit(solution)/shard_map/ppermute | solution.py:186
  23.1 1.5 %shard_map.71 = (f32[32,1152]{1,0:T(8,128)S(1)}, f32[32,2944]{1,0:T(8,128)S(1)}) custom-call(bf16[64,4096]{1,0:T(8,128)(2,1)S(1)} %get-tuple-element.26.x, bf16[4096,3584]{1,0:T(8,128)(2,1)S(1)} %copy-done, f32[32,128]{1,0:T(8,128)S(1)} %shard_map.70._.a, f32[32,1792]{1,0:T(8,128)S(1)} %get-tuple-element.32.refs_0_), custom_call_target="tpu_custom_call" | custom-call | tf_op jit(solution)/shard_map/pallas_call | solution.py:228
  24.6 0.6 %collective-permute-done.8.b = f32[32,128]{1,0:T(8,128)S(1)} collective-permute-done((f32[32,128]{1,0:T(8,128)S(1)}, f32[32,128]{1,0:T(8,128)S(1)}, u32[]{:S(2)}, u32[]{:S(2)}) %collective-permute-start.8) | collective-permute-done | bytes 16416 | tf_op jit(solution)/shard_map/ppermute | solution.py:186
  25.2 0.3 collective-permute-start.11
  25.5 2.5 %collective-permute-start.9 = (f32[32,128]{1,0:T(8,128)S(1)}, f32[32,128]{1,0:T(8,128)S(1)}, u32[]{:S(2)}, u32[]{:S(2)}) collective-permute-start(f32[32,128]{1,0:T(8,128)S(1)} %shard_map.72._.a), channel_id=1, source_target_pairs={{0,9},{1,8},{2,11},{3,10},{4,13},{5,12},{6,15},{7,14},{8,1},{9,0},... | collective-permute-start | bytes 49160 | tf_op jit(solution)/shard_map/ppermute | solution.py:186
  28.0 0.9 %shard_map.73 = (f32[32,640]{1,0:T(8,128)S(1)}, f32[32,640]{1,0:T(8,128)S(1)}) custom-call(bf16[64,4096]{1,0:T(8,128)(2,1)S(1)} %get-tuple-element.26.x, bf16[4096,3584]{1,0:T(8,128)(2,1)S(1)} %copy-done, f32[32,128]{1,0:T(8,128)S(1)} %shard_map.72._.a), custom_call_target="tpu_custom_call" | custom-call | tf_op jit(solution)/shard_map/pallas_call | solution.py:228
  28.9 0.4 %collective-permute-start.12 = (f32[32,640]{1,0:T(8,128)S(1)}, f32[32,640]{1,0:T(8,128)S(1)}, u32[]{:S(2)}, u32[]{:S(2)}) collective-permute-start(f32[32,640]{1,0:T(8,128)S(1)} %get-tuple-element.40), channel_id=1, source_target_pairs={{0,1},{1,0},{2,3},{3,2},{4,5},{5,4},{6,7},{7,6},{8,9},{9,8},{10,11... | collective-permute-start | bytes 245768 | tf_op jit(solution)/shard_map/ppermute | solution.py:180
  29.3 0.3 collective-permute-done.9.b
  29.6 0.8 %shard_map.75.total = f32[32,3584]{1,0:T(8,128)S(1)} custom-call(f32[32,128]{1,0:T(8,128)S(1)} %shard_map.74.low, f32[64,128]{1,0:T(8,128)S(1)} %get-tuple-element.37.ids, bf16[8,32,3584]{2,1,0:T(8,128)(2,1)S(1)} %copy-done.1, bf16[8,32,3584]{2,1,0:T(8,128)(2,1)S(1)} %collective-permute-done.10.up_peer, f32[32,2944]{1,0:T(8,128)S(1)} %collective-permute-done.11.got, ...), custom_call_target="tpu_custom_call" | custom-call | flops 4294967296 | tf_op jit(solution)/shard_map/pallas_call | solution.py:250
  30.4 0.7 %shard_map.76 = bf16[32,3584]{1,0:T(8,128)(2,1)} custom-call(f32[32,3584]{1,0:T(8,128)S(1)} %shard_map.75.total, f32[32,640]{1,0:T(8,128)S(1)} %collective-permute-done.12.got), custom_call_target="tpu_custom_call" | custom-call | tf_op jit(solution)/shard_map/pallas_call | solution.py:254
  (21 shorter events, 0.4 us)
Async XLA Ops:
  0.0 16.8 %copy-start.1 = (bf16[8,32,3584]{2,1,0:T(8,128)(2,1)S(1)}, bf16[8,32,3584]{2,1,0:T(8,128)(2,1)}, u32[]{:S(2)}) copy-start(bf16[8,32,3584]{2,1,0:T(8,128)(2,1)} %up_own) | copy-start | bytes 5505028
  0.0 16.8 %copy-start.2 = (bf16[1,4096,64]{1,2,0:T(8,128)(2,1)S(1)}, bf16[1,4096,64]{1,2,0:T(8,128)(2,1)}, u32[]{:S(2)}) copy-start(bf16[1,4096,64]{1,2,0:T(8,128)(2,1)} %param.10) | copy-start | bytes 1572868
  0.0 17.3 %copy-start = (bf16[4096,3584]{1,0:T(8,128)(2,1)S(1)}, bf16[4096,3584]{1,0:T(8,128)(2,1)}, u32[]{:S(2)}) copy-start(bf16[4096,3584]{1,0:T(8,128)(2,1)} %w.7) | copy-start | bytes 88080384
  1.0 7.2 %collective-permute-start.2 = (bf16[1,8,4224]{2,1,0:T(8,128)(2,1)S(1)}, bf16[1,8,4224]{2,1,0:T(8,128)(2,1)S(1)}, u32[]{:S(2)}, u32[]{:S(2)}) collective-permute-start(bf16[1,8,4224]{2,1,0:T(8,128)(2,1)S(1)} %get-tuple-element.24.refs_0_), channel_id=1, source_target_pairs={{0,8},{2,10},{4,12},{6,14},{8,0},{10,2},{12,4},{14,6},{1,9},{3,11}... | collective-permute-start | bytes 202760 | tf_op jit(solution)/shard_map/ppermute | solution.py:183
  5.1 4.5 %collective-permute-start.1 = (bf16[1,8,4224]{2,1,0:T(8,128)(2,1)S(1)}, bf16[1,8,4224]{2,1,0:T(8,128)(2,1)S(1)}, u32[]{:S(2)}, u32[]{:S(2)}) collective-permute-start(bf16[1,8,4224]{2,1,0:T(8,128)(2,1)S(1)} %get-tuple-element.24.refs_0_), channel_id=1, source_target_pairs={{0,4},{2,6},{4,0},{6,2},{8,12},{10,14},{12,8},{14,10},{1,5},{3,7},... | collective-permute-start | bytes 202760 | tf_op jit(solution)/shard_map/ppermute | solution.py:183
  6.7 4.5 %collective-permute-start = (bf16[1,8,4224]{2,1,0:T(8,128)(2,1)S(1)}, bf16[1,8,4224]{2,1,0:T(8,128)(2,1)S(1)}, u32[]{:S(2)}, u32[]{:S(2)}) collective-permute-start(bf16[1,8,4224]{2,1,0:T(8,128)(2,1)S(1)} %get-tuple-element.24.refs_0_), channel_id=1, source_target_pairs={{0,2},{2,0},{4,6},{6,4},{8,10},{10,8},{12,14},{14,12},{1,3},{3,1},... | collective-permute-start | bytes 202760 | tf_op jit(solution)/shard_map/ppermute | solution.py:183
  8.2 4.3 %collective-permute-start.3 = (bf16[1,8,4224]{2,1,0:T(8,128)(2,1)S(1)}, bf16[1,8,4224]{2,1,0:T(8,128)(2,1)S(1)}, u32[]{:S(2)}, u32[]{:S(2)}) collective-permute-start(bf16[1,8,4224]{2,1,0:T(8,128)(2,1)S(1)} %collective-permute-done.2.refs_1_.refs_3_), channel_id=1, source_target_pairs={{0,4},{2,6},{4,0},{6,2},{8,12},{10,14},{12,8},{14,10},{1,5},{3,7},... | collective-permute-start | bytes 202760 | tf_op jit(solution)/shard_map/ppermute | solution.py:183
  9.6 7.2 %collective-permute-start.4 = (bf16[2,8,4224]{2,1,0:T(8,128)(2,1)S(1)}, bf16[2,8,4224]{2,1,0:T(8,128)(2,1)S(1)}, u32[]{:S(2)}, u32[]{:S(2)}) collective-permute-start(bf16[2,8,4224]{2,1,0:T(8,128)(2,1)S(1)} %shard_map.65), channel_id=1, source_target_pairs={{0,2},{2,0},{4,6},{6,4},{8,10},{10,8},{12,14},{14,12},{1,3},{3,1},... | collective-permute-start | bytes 405512 | tf_op jit(solution)/shard_map/ppermute | solution.py:183
  12.5 4.3 %collective-permute-start.5 = (bf16[1,8,4224]{2,1,0:T(8,128)(2,1)S(1)}, bf16[1,8,4224]{2,1,0:T(8,128)(2,1)S(1)}, u32[]{:S(2)}, u32[]{:S(2)}) collective-permute-start(bf16[1,8,4224]{2,1,0:T(8,128)(2,1)S(1)} %collective-permute-done.3.refs_4_), channel_id=1, source_target_pairs={{0,2},{2,0},{4,6},{6,4},{8,10},{10,8},{12,14},{14,12},{1,3},{3,1},... | collective-permute-start | bytes 202760 | tf_op jit(solution)/shard_map/ppermute | solution.py:183
  17.3 1.2 %collective-permute-start.6 = (f32[32,128]{1,0:T(8,128)S(1)}, f32[32,128]{1,0:T(8,128)S(1)}, u32[]{:S(2)}, u32[]{:S(2)}) collective-permute-start(f32[32,128]{1,0:T(8,128)S(1)} %get-tuple-element.27._.a), channel_id=1, source_target_pairs={{0,1},{1,0},{2,3},{3,2},{4,5},{5,4},{6,7},{7,6},{8,9},{9,8},{10,11... | collective-permute-start | bytes 49160 | tf_op jit(solution)/shard_map/ppermute | solution.py:180
  18.5 11.1 %collective-permute-start.10 = (bf16[8,32,3584]{2,1,0:T(8,128)(2,1)S(1)}, bf16[8,32,3584]{2,1,0:T(8,128)(2,1)S(1)}, u32[]{:S(2)}, u32[]{:S(2)}) collective-permute-start(bf16[8,32,3584]{2,1,0:T(8,128)(2,1)S(1)} %copy-done.1), channel_id=1, source_target_pairs={{0,1},{1,0},{2,3},{3,2},{4,5},{5,4},{6,7},{7,6},{8,9},{9,8},{10,11... | collective-permute-start | bytes 5505032 | tf_op jit(solution)/shard_map/ppermute | solution.py:180
  18.8 3.2 %collective-permute-start.7 = (f32[32,128]{1,0:T(8,128)S(1)}, f32[32,128]{1,0:T(8,128)S(1)}, u32[]{:S(2)}, u32[]{:S(2)}) collective-permute-start(f32[32,128]{1,0:T(8,128)S(1)} %shard_map.68._.a), channel_id=1, source_target_pairs={{0,3},{1,2},{2,1},{3,0},{4,7},{5,6},{6,5},{7,4},{8,11},{9,10},{10,... | collective-permute-start | bytes 49160 | tf_op jit(solution)/shard_map/ppermute | solution.py:186
  22.0 3.2 %collective-permute-start.8 = (f32[32,128]{1,0:T(8,128)S(1)}, f32[32,128]{1,0:T(8,128)S(1)}, u32[]{:S(2)}, u32[]{:S(2)}) collective-permute-start(f32[32,128]{1,0:T(8,128)S(1)} %shard_map.70._.a), channel_id=1, source_target_pairs={{0,5},{1,4},{2,7},{3,6},{4,1},{5,0},{6,3},{7,2},{8,13},{9,12},{10,... | collective-permute-start | bytes 49160 | tf_op jit(solution)/shard_map/ppermute | solution.py:186
  25.2 4.4 %collective-permute-start.11 = (f32[32,2944]{1,0:T(8,128)S(1)}, f32[32,2944]{1,0:T(8,128)S(1)}, u32[]{:S(2)}, u32[]{:S(2)}) collective-permute-start(f32[32,2944]{1,0:T(8,128)S(1)} %get-tuple-element.39), channel_id=1, source_target_pairs={{0,1},{1,0},{2,3},{3,2},{4,5},{5,4},{6,7},{7,6},{8,9},{9,8},{10,11... | collective-permute-start | bytes 1130504 | tf_op jit(solution)/shard_map/ppermute | solution.py:180
  25.5 4.1 %collective-permute-start.9 = (f32[32,128]{1,0:T(8,128)S(1)}, f32[32,128]{1,0:T(8,128)S(1)}, u32[]{:S(2)}, u32[]{:S(2)}) collective-permute-start(f32[32,128]{1,0:T(8,128)S(1)} %shard_map.72._.a), channel_id=1, source_target_pairs={{0,9},{1,8},{2,11},{3,10},{4,13},{5,12},{6,15},{7,14},{8,1},{9,0},... | collective-permute-start | bytes 49160 | tf_op jit(solution)/shard_map/ppermute | solution.py:186
  28.9 1.5 %collective-permute-start.12 = (f32[32,640]{1,0:T(8,128)S(1)}, f32[32,640]{1,0:T(8,128)S(1)}, u32[]{:S(2)}, u32[]{:S(2)}) collective-permute-start(f32[32,640]{1,0:T(8,128)S(1)} %get-tuple-element.40), channel_id=1, source_target_pairs={{0,1},{1,0},{2,3},{3,2},{4,5},{5,4},{6,7},{7,6},{8,9},{9,8},{10,11... | collective-permute-start | bytes 245768 | tf_op jit(solution)/shard_map/ppermute | solution.py:180

commit v6 on v5

--- a/solution.py
+++ b/solution.py
@@ -11,7 +11,6 @@
 F32, BF16 = jnp.float32, jnp.bfloat16
 VMEM = pl.BlockSpec(memory_space=pltpu.VMEM)
 SMEM = pl.BlockSpec(memory_space=pltpu.SMEM)
-HBM = pl.BlockSpec(memory_space=pltpu.HBM)
 ANY = pl.BlockSpec(memory_space=pl.ANY)
 LANES = 128
 SPLITS = {2: (20, 28), 3: (10, 22, 28), 4: (5, 14, 23, 28)}
@@ -39,28 +38,19 @@
     return pltpu.with_memory_space_constraint(array, pltpu.HBM)
 
 
-def pack_kernel(ids_far, holder_far, tokens, message, held, ids, holder, sems):
+def pack_kernel(ids, holder, tokens, message, held):
     rows, wide = tokens.shape
-    copies = [
-        pltpu.make_async_copy(ids_far, ids, sems.at[0]),
-        pltpu.make_async_copy(holder_far, holder, sems.at[1]),
-        pltpu.make_async_copy(tokens, message.at[0, :, pl.ds(0, wide)], sems.at[2]),
-    ]
-    for copy in copies:
-        copy.start()
-    copies[0].wait()
+    message[0, :, :wide] = tokens[...]
     place = lax.broadcasted_iota(jnp.int32, (rows, LANES), 0)
     value = jnp.zeros((rows, LANES), jnp.int32)
     for i in range(rows):
         value = jnp.where(place == i, ids[i], value)
     message[0, :, wide:] = value.astype(F32).astype(BF16)
-    copies[1].wait()
     me = lax.axis_index("ffn")
     mine = jnp.int32(0)
     for a in range(holder.shape[0]):
         mine = mine + jnp.where(holder[a] == me, a, 0)
     held[...] = jnp.full(held.shape, mine, jnp.int32).astype(F32)
-    copies[2].wait()
 
 
 def join_kernel(*refs):
@@ -192,13 +182,10 @@
     message, held = call(
         pack_kernel,
         [jax.ShapeDtypeStruct((1, rows, wide + LANES), BF16), jax.ShapeDtypeStruct((8, LANES), F32)],
-        [HBM, HBM, HBM],
+        [SMEM, SMEM, VMEM],
         1 << 20,
-        scratch=[
-            pltpu.SMEM(row_ids.shape, jnp.int32),
-            pltpu.SMEM(holder.shape, jnp.int32),
-            pltpu.SemaphoreType.DMA((3,)),
-        ], flops=40 << 30, bytes_accessed=1 << 17,
+        flops=40 << 30,
+        bytes_accessed=1 << 17,
     )(far(row_ids), far(holder), far(tokens))
     parts, order = gather(n, message, partner, across, swap)
 
@@ -226,7 +213,7 @@
         last = i == len(steps) - 1
         kept = [] if sent is None or last else [sent]
         o, s = call(
-            functools.partial(base_kernel, a, 128),
+            functools.partial(base_kernel, a, LANES),
             [
                 jax.ShapeDtypeStruct((half, b - a), F32),
                 jax.ShapeDtypeStruct((half, b - a if last else b), F32),
@@ -290,7 +277,7 @@
 
 def solution(mesh):
     n, cores = mesh.shape["ffn"], mesh.shape["width"]
-    short = n <= 8 and n & (n - 1) == 0 and n > 1 and cores == 2
+    short = n in (2, 4, 8) and cores == 2
     placed = (
         P(("groups", "ffn"), "width"),
         P("width", "ffn"),

time: 31.3 us -> 31.3 us (level)
  no operation moved by 1% of the time
where the time goes in v6:
time: 31.3 us; the launch traced here: 31.1 us
  starting transfers between devices  18.4 us (59%)
  Pallas kernels  7.75 us (25%)
  waiting for transfers between devices  4.86 us (16%)
    ppermute x6, starting transfers between devices, partner(): return lax.ppermute(v, 'ffn', [(i, i ^ k) for i in range(n)])  12 us
    ppermute x3, starting transfers between devices, across(): lax.ppermute(v, both, [(2 * i + w, 2 * (i ^ k) + 1 - w) for i in range(n)...  5.37 us
    pallas_call x4, Pallas kernels, small(): call(functools.partial(base_kernel, a, LANES), [jax.ShapeDtypeStruct((hal...  4.75 us
    ppermute x6, waiting for transfers between devices, partner(): return lax.ppermute(v, 'ffn', [(i, i ^ k) for i in range(n)])  3.74 us
    pallas_call x1, Pallas kernels, small(): call(pack_kernel, [jax.ShapeDtypeStruct((1, rows, wide + LANES), BF16), j...  1.02 us
    ppermute x4, starting transfers between devices, swap(): return lax.ppermute(v, 'width', [(0, 1), (1, 0)])  1.01 us
    ppermute x3, waiting for transfers between devices, across(): lax.ppermute(v, both, [(2 * i + w, 2 * (i ^ k) + 1 - w) for i in range(n)...  0.86 us
    pallas_call x1, Pallas kernels, small(): call(delta_kernel, jax.ShapeDtypeStruct((half, columns), F32), [VMEM] * (...  0.79 us
  transfers between devices with their start and end apart: 13, of which 5 were waited for; matrix products, arithmetic and copies ran while one was open for 0% of the time, Pallas kernels for 18%

profile of v6, /device:TPU:0, one launch (start us, length us, event | category | flops | bytes accessed | tf_op | source)
XLA Modules:
  0.0 31.1 jit_solution(3962197967595733903)
XLA Ops:
  0.0 1.0 %shard_map.64 = (bf16[1,8,4224]{2,1,0:T(8,128)(2,1)S(1)}, f32[8,128]{1,0:T(8,128)S(1)}) custom-call(s32[8]{0:T(128)} %ids.1, s32[8]{0:T(128)} %holder.1, bf16[8,4096]{1,0:T(8,128)(2,1)} %tokens.1), custom_call_target="tpu_custom_call" | custom-call | flops 42949672960 | bytes 131072 | tf_op jit(solution)/shard_map/pallas_call | solution.py:182
  1.0 4.1 %collective-permute-start.2 = (bf16[1,8,4224]{2,1,0:T(8,128)(2,1)S(1)}, bf16[1,8,4224]{2,1,0:T(8,128)(2,1)S(1)}, u32[]{:S(2)}, u32[]{:S(2)}) collective-permute-start(bf16[1,8,4224]{2,1,0:T(8,128)(2,1)S(1)} %get-tuple-element.24.refs_0_), channel_id=1, source_target_pairs={{0,8},{2,10},{4,12},{6,14},{8,0},{10,2},{12,4},{14,6},{1,9},{3,11}... | collective-permute-start | bytes 202760 | tf_op jit(solution)/shard_map/ppermute | solution.py:173
  5.1 1.6 %collective-permute-start.1 = (bf16[1,8,4224]{2,1,0:T(8,128)(2,1)S(1)}, bf16[1,8,4224]{2,1,0:T(8,128)(2,1)S(1)}, u32[]{:S(2)}, u32[]{:S(2)}) collective-permute-start(bf16[1,8,4224]{2,1,0:T(8,128)(2,1)S(1)} %get-tuple-element.24.refs_0_), channel_id=1, source_target_pairs={{0,4},{2,6},{4,0},{6,2},{8,12},{10,14},{12,8},{14,10},{1,5},{3,7},... | collective-permute-start | bytes 202760 | tf_op jit(solution)/shard_map/ppermute | solution.py:173
  6.7 1.5 %collective-permute-start = (bf16[1,8,4224]{2,1,0:T(8,128)(2,1)S(1)}, bf16[1,8,4224]{2,1,0:T(8,128)(2,1)S(1)}, u32[]{:S(2)}, u32[]{:S(2)}) collective-permute-start(bf16[1,8,4224]{2,1,0:T(8,128)(2,1)S(1)} %get-tuple-element.24.refs_0_), channel_id=1, source_target_pairs={{0,2},{2,0},{4,6},{6,4},{8,10},{10,8},{12,14},{14,12},{1,3},{3,1},... | collective-permute-start | bytes 202760 | tf_op jit(solution)/shard_map/ppermute | solution.py:173
  8.2 1.4 %collective-permute-start.3 = (bf16[1,8,4224]{2,1,0:T(8,128)(2,1)S(1)}, bf16[1,8,4224]{2,1,0:T(8,128)(2,1)S(1)}, u32[]{:S(2)}, u32[]{:S(2)}) collective-permute-start(bf16[1,8,4224]{2,1,0:T(8,128)(2,1)S(1)} %collective-permute-done.2.refs_1_.refs_3_), channel_id=1, source_target_pairs={{0,4},{2,6},{4,0},{6,2},{8,12},{10,14},{12,8},{14,10},{1,5},{3,7},... | collective-permute-start | bytes 202760 | tf_op jit(solution)/shard_map/ppermute | solution.py:173
  9.6 1.6 %collective-permute-start.4 = (bf16[2,8,4224]{2,1,0:T(8,128)(2,1)S(1)}, bf16[2,8,4224]{2,1,0:T(8,128)(2,1)S(1)}, u32[]{:S(2)}, u32[]{:S(2)}) collective-permute-start(bf16[2,8,4224]{2,1,0:T(8,128)(2,1)S(1)} %shard_map.65), channel_id=1, source_target_pairs={{0,2},{2,0},{4,6},{6,4},{8,10},{10,8},{12,14},{14,12},{1,3},{3,1},... | collective-permute-start | bytes 405512 | tf_op jit(solution)/shard_map/ppermute | solution.py:173
  11.2 1.3 %collective-permute-done.3.refs_4_ = bf16[1,8,4224]{2,1,0:T(8,128)(2,1)S(1)} collective-permute-done((bf16[1,8,4224]{2,1,0:T(8,128)(2,1)S(1)}, bf16[1,8,4224]{2,1,0:T(8,128)(2,1)S(1)}, u32[]{:S(2)}, u32[]{:S(2)}) %collective-permute-start.3) | collective-permute-done | bytes 67616 | tf_op jit(solution)/shard_map/ppermute | solution.py:173
  12.5 1.9 %collective-permute-start.5 = (bf16[1,8,4224]{2,1,0:T(8,128)(2,1)S(1)}, bf16[1,8,4224]{2,1,0:T(8,128)(2,1)S(1)}, u32[]{:S(2)}, u32[]{:S(2)}) collective-permute-start(bf16[1,8,4224]{2,1,0:T(8,128)(2,1)S(1)} %collective-permute-done.3.refs_4_), channel_id=1, source_target_pairs={{0,2},{2,0},{4,6},{6,4},{8,10},{10,8},{12,14},{14,12},{1,3},{3,1},... | collective-permute-start | bytes 202760 | tf_op jit(solution)/shard_map/ppermute | solution.py:173
  14.4 2.4 %collective-permute-done.5.refs_6_ = bf16[1,8,4224]{2,1,0:T(8,128)(2,1)S(1)} collective-permute-done((bf16[1,8,4224]{2,1,0:T(8,128)(2,1)S(1)}, bf16[1,8,4224]{2,1,0:T(8,128)(2,1)S(1)}, u32[]{:S(2)}, u32[]{:S(2)}) %collective-permute-start.5) | collective-permute-done | bytes 67616 | tf_op jit(solution)/shard_map/ppermute | solution.py:173
  16.8 0.4 %shard_map.66 = (bf16[64,4096]{1,0:T(8,128)(2,1)S(1)}, f32[64,128]{1,0:T(8,128)S(1)}, f32[32,128]{1,0:T(8,128)S(1)}) custom-call(f32[8,128]{1,0:T(8,128)S(1)} %get-tuple-element.23.held, bf16[64,4096]{1,0:T(8,128)(2,1)S(1)} %bitcast.3, bf16[8,32,3584]{2,1,0:T(8,128)(2,1)S(1)} %copy-done.1, bf16[1,8,4224]{2,1,0:T(8,128)(2,1)S(1)} %get-tuple-element.24.refs_0_, ...), custom_call_target="tpu_custom_call" | custom-call | tf_op jit(solution)/shard_map/pallas_call | solution.py:192
  17.3 0.9 %shard_map.67 = (f32[32,640]{1,0:T(8,128)S(1)}, f32[32,640]{1,0:T(8,128)S(1)}) custom-call(bf16[64,4096]{1,0:T(8,128)(2,1)S(1)} %get-tuple-element.26.x, bf16[4096,3584]{1,0:T(8,128)(2,1)S(1)} %copy-done, f32[32,128]{1,0:T(8,128)S(1)} %get-tuple-element.27._.a), custom_call_target="tpu_custom_call" | custom-call | tf_op jit(solution)/shard_map/pallas_call | solution.py:215
  18.5 0.3 collective-permute-start.10
  18.8 1.7 %collective-permute-start.7 = (f32[32,128]{1,0:T(8,128)S(1)}, f32[32,128]{1,0:T(8,128)S(1)}, u32[]{:S(2)}, u32[]{:S(2)}) collective-permute-start(f32[32,128]{1,0:T(8,128)S(1)} %shard_map.68._.a), channel_id=1, source_target_pairs={{0,3},{1,2},{2,1},{3,0},{4,7},{5,6},{6,5},{7,4},{8,11},{9,10},{10,... | collective-permute-start | bytes 49160 | tf_op jit(solution)/shard_map/ppermute | solution.py:176
  20.5 1.5 %shard_map.69 = (f32[32,1152]{1,0:T(8,128)S(1)}, f32[32,1792]{1,0:T(8,128)S(1)}) custom-call(bf16[64,4096]{1,0:T(8,128)(2,1)S(1)} %get-tuple-element.26.x, bf16[4096,3584]{1,0:T(8,128)(2,1)S(1)} %copy-done, f32[32,128]{1,0:T(8,128)S(1)} %shard_map.68._.a, f32[32,640]{1,0:T(8,128)S(1)} %get-tuple-element.30.refs_0_), custom_call_target="tpu_custom_call" | custom-call | tf_op jit(solution)/shard_map/pallas_call | solution.py:215
  22.0 1.2 %collective-permute-start.8 = (f32[32,128]{1,0:T(8,128)S(1)}, f32[32,128]{1,0:T(8,128)S(1)}, u32[]{:S(2)}, u32[]{:S(2)}) collective-permute-start(f32[32,128]{1,0:T(8,128)S(1)} %shard_map.70._.a), channel_id=1, source_target_pairs={{0,5},{1,4},{2,7},{3,6},{4,1},{5,0},{6,3},{7,2},{8,13},{9,12},{10,... | collective-permute-start | bytes 49160 | tf_op jit(solution)/shard_map/ppermute | solution.py:176
  23.1 1.5 %shard_map.71 = (f32[32,1152]{1,0:T(8,128)S(1)}, f32[32,2944]{1,0:T(8,128)S(1)}) custom-call(bf16[64,4096]{1,0:T(8,128)(2,1)S(1)} %get-tuple-element.26.x, bf16[4096,3584]{1,0:T(8,128)(2,1)S(1)} %copy-done, f32[32,128]{1,0:T(8,128)S(1)} %shard_map.70._.a, f32[32,1792]{1,0:T(8,128)S(1)} %get-tuple-element.32.refs_0_), custom_call_target="tpu_custom_call" | custom-call | tf_op jit(solution)/shard_map/pallas_call | solution.py:215
  24.6 0.6 %collective-permute-done.8.b = f32[32,128]{1,0:T(8,128)S(1)} collective-permute-done((f32[32,128]{1,0:T(8,128)S(1)}, f32[32,128]{1,0:T(8,128)S(1)}, u32[]{:S(2)}, u32[]{:S(2)}) %collective-permute-start.8) | collective-permute-done | bytes 16416 | tf_op jit(solution)/shard_map/ppermute | solution.py:176
  25.2 0.3 collective-permute-start.11
  25.5 2.5 %collective-permute-start.9 = (f32[32,128]{1,0:T(8,128)S(1)}, f32[32,128]{1,0:T(8,128)S(1)}, u32[]{:S(2)}, u32[]{:S(2)}) collective-permute-start(f32[32,128]{1,0:T(8,128)S(1)} %shard_map.72._.a), channel_id=1, source_target_pairs={{0,9},{1,8},{2,11},{3,10},{4,13},{5,12},{6,15},{7,14},{8,1},{9,0},... | collective-permute-start | bytes 49160 | tf_op jit(solution)/shard_map/ppermute | solution.py:176
  28.0 0.9 %shard_map.73 = (f32[32,640]{1,0:T(8,128)S(1)}, f32[32,640]{1,0:T(8,128)S(1)}) custom-call(bf16[64,4096]{1,0:T(8,128)(2,1)S(1)} %get-tuple-element.26.x, bf16[4096,3584]{1,0:T(8,128)(2,1)S(1)} %copy-done, f32[32,128]{1,0:T(8,128)S(1)} %shard_map.72._.a), custom_call_target="tpu_custom_call" | custom-call | tf_op jit(solution)/shard_map/pallas_call | solution.py:215
  28.9 0.4 %collective-permute-start.12 = (f32[32,640]{1,0:T(8,128)S(1)}, f32[32,640]{1,0:T(8,128)S(1)}, u32[]{:S(2)}, u32[]{:S(2)}) collective-permute-start(f32[32,640]{1,0:T(8,128)S(1)} %get-tuple-element.40), channel_id=1, source_target_pairs={{0,1},{1,0},{2,3},{3,2},{4,5},{5,4},{6,7},{7,6},{8,9},{9,8},{10,11... | collective-permute-start | bytes 245768 | tf_op jit(solution)/shard_map/ppermute | solution.py:170
  29.3 0.3 collective-permute-done.9.b
  29.6 0.8 %shard_map.75.total = f32[32,3584]{1,0:T(8,128)S(1)} custom-call(f32[32,128]{1,0:T(8,128)S(1)} %shard_map.74.low, f32[64,128]{1,0:T(8,128)S(1)} %get-tuple-element.37.ids, bf16[8,32,3584]{2,1,0:T(8,128)(2,1)S(1)} %copy-done.1, bf16[8,32,3584]{2,1,0:T(8,128)(2,1)S(1)} %collective-permute-done.10.up_peer, f32[32,2944]{1,0:T(8,128)S(1)} %collective-permute-done.11.got, ...), custom_call_target="tpu_custom_call" | custom-call | flops 4294967296 | tf_op jit(solution)/shard_map/pallas_call | solution.py:237
  30.4 0.7 %shard_map.76 = bf16[32,3584]{1,0:T(8,128)(2,1)} custom-call(f32[32,3584]{1,0:T(8,128)S(1)} %shard_map.75.total, f32[32,640]{1,0:T(8,128)S(1)} %collective-permute-done.12.got), custom_call_target="tpu_custom_call" | custom-call | tf_op jit(solution)/shard_map/pallas_call | solution.py:241
  (21 shorter events, 0.4 us)
Async XLA Ops:
  0.0 16.8 %copy-start.1 = (bf16[8,32,3584]{2,1,0:T(8,128)(2,1)S(1)}, bf16[8,32,3584]{2,1,0:T(8,128)(2,1)}, u32[]{:S(2)}) copy-start(bf16[8,32,3584]{2,1,0:T(8,128)(2,1)} %up_own) | copy-start | bytes 5505028
  0.0 16.8 %copy-start.2 = (bf16[1,4096,64]{1,2,0:T(8,128)(2,1)S(1)}, bf16[1,4096,64]{1,2,0:T(8,128)(2,1)}, u32[]{:S(2)}) copy-start(bf16[1,4096,64]{1,2,0:T(8,128)(2,1)} %param.10) | copy-start | bytes 1572868
  0.0 17.3 %copy-start = (bf16[4096,3584]{1,0:T(8,128)(2,1)S(1)}, bf16[4096,3584]{1,0:T(8,128)(2,1)}, u32[]{:S(2)}) copy-start(bf16[4096,3584]{1,0:T(8,128)(2,1)} %w.7) | copy-start | bytes 88080384
  1.0 7.2 %collective-permute-start.2 = (bf16[1,8,4224]{2,1,0:T(8,128)(2,1)S(1)}, bf16[1,8,4224]{2,1,0:T(8,128)(2,1)S(1)}, u32[]{:S(2)}, u32[]{:S(2)}) collective-permute-start(bf16[1,8,4224]{2,1,0:T(8,128)(2,1)S(1)} %get-tuple-element.24.refs_0_), channel_id=1, source_target_pairs={{0,8},{2,10},{4,12},{6,14},{8,0},{10,2},{12,4},{14,6},{1,9},{3,11}... | collective-permute-start | bytes 202760 | tf_op jit(solution)/shard_map/ppermute | solution.py:173
  5.1 4.5 %collective-permute-start.1 = (bf16[1,8,4224]{2,1,0:T(8,128)(2,1)S(1)}, bf16[1,8,4224]{2,1,0:T(8,128)(2,1)S(1)}, u32[]{:S(2)}, u32[]{:S(2)}) collective-permute-start(bf16[1,8,4224]{2,1,0:T(8,128)(2,1)S(1)} %get-tuple-element.24.refs_0_), channel_id=1, source_target_pairs={{0,4},{2,6},{4,0},{6,2},{8,12},{10,14},{12,8},{14,10},{1,5},{3,7},... | collective-permute-start | bytes 202760 | tf_op jit(solution)/shard_map/ppermute | solution.py:173
  6.7 4.5 %collective-permute-start = (bf16[1,8,4224]{2,1,0:T(8,128)(2,1)S(1)}, bf16[1,8,4224]{2,1,0:T(8,128)(2,1)S(1)}, u32[]{:S(2)}, u32[]{:S(2)}) collective-permute-start(bf16[1,8,4224]{2,1,0:T(8,128)(2,1)S(1)} %get-tuple-element.24.refs_0_), channel_id=1, source_target_pairs={{0,2},{2,0},{4,6},{6,4},{8,10},{10,8},{12,14},{14,12},{1,3},{3,1},... | collective-permute-start | bytes 202760 | tf_op jit(solution)/shard_map/ppermute | solution.py:173
  8.2 4.3 %collective-permute-start.3 = (bf16[1,8,4224]{2,1,0:T(8,128)(2,1)S(1)}, bf16[1,8,4224]{2,1,0:T(8,128)(2,1)S(1)}, u32[]{:S(2)}, u32[]{:S(2)}) collective-permute-start(bf16[1,8,4224]{2,1,0:T(8,128)(2,1)S(1)} %collective-permute-done.2.refs_1_.refs_3_), channel_id=1, source_target_pairs={{0,4},{2,6},{4,0},{6,2},{8,12},{10,14},{12,8},{14,10},{1,5},{3,7},... | collective-permute-start | bytes 202760 | tf_op jit(solution)/shard_map/ppermute | solution.py:173
  9.6 7.2 %collective-permute-start.4 = (bf16[2,8,4224]{2,1,0:T(8,128)(2,1)S(1)}, bf16[2,8,4224]{2,1,0:T(8,128)(2,1)S(1)}, u32[]{:S(2)}, u32[]{:S(2)}) collective-permute-start(bf16[2,8,4224]{2,1,0:T(8,128)(2,1)S(1)} %shard_map.65), channel_id=1, source_target_pairs={{0,2},{2,0},{4,6},{6,4},{8,10},{10,8},{12,14},{14,12},{1,3},{3,1},... | collective-permute-start | bytes 405512 | tf_op jit(solution)/shard_map/ppermute | solution.py:173
  12.5 4.3 %collective-permute-start.5 = (bf16[1,8,4224]{2,1,0:T(8,128)(2,1)S(1)}, bf16[1,8,4224]{2,1,0:T(8,128)(2,1)S(1)}, u32[]{:S(2)}, u32[]{:S(2)}) collective-permute-start(bf16[1,8,4224]{2,1,0:T(8,128)(2,1)S(1)} %collective-permute-done.3.refs_4_), channel_id=1, source_target_pairs={{0,2},{2,0},{4,6},{6,4},{8,10},{10,8},{12,14},{14,12},{1,3},{3,1},... | collective-permute-start | bytes 202760 | tf_op jit(solution)/shard_map/ppermute | solution.py:173
  17.3 1.2 %collective-permute-start.6 = (f32[32,128]{1,0:T(8,128)S(1)}, f32[32,128]{1,0:T(8,128)S(1)}, u32[]{:S(2)}, u32[]{:S(2)}) collective-permute-start(f32[32,128]{1,0:T(8,128)S(1)} %get-tuple-element.27._.a), channel_id=1, source_target_pairs={{0,1},{1,0},{2,3},{3,2},{4,5},{5,4},{6,7},{7,6},{8,9},{9,8},{10,11... | collective-permute-start | bytes 49160 | tf_op jit(solution)/shard_map/ppermute | solution.py:170
  18.5 11.1 %collective-permute-start.10 = (bf16[8,32,3584]{2,1,0:T(8,128)(2,1)S(1)}, bf16[8,32,3584]{2,1,0:T(8,128)(2,1)S(1)}, u32[]{:S(2)}, u32[]{:S(2)}) collective-permute-start(bf16[8,32,3584]{2,1,0:T(8,128)(2,1)S(1)} %copy-done.1), channel_id=1, source_target_pairs={{0,1},{1,0},{2,3},{3,2},{4,5},{5,4},{6,7},{7,6},{8,9},{9,8},{10,11... | collective-permute-start | bytes 5505032 | tf_op jit(solution)/shard_map/ppermute | solution.py:170
  18.8 3.2 %collective-permute-start.7 = (f32[32,128]{1,0:T(8,128)S(1)}, f32[32,128]{1,0:T(8,128)S(1)}, u32[]{:S(2)}, u32[]{:S(2)}) collective-permute-start(f32[32,128]{1,0:T(8,128)S(1)} %shard_map.68._.a), channel_id=1, source_target_pairs={{0,3},{1,2},{2,1},{3,0},{4,7},{5,6},{6,5},{7,4},{8,11},{9,10},{10,... | collective-permute-start | bytes 49160 | tf_op jit(solution)/shard_map/ppermute | solution.py:176
  22.0 3.2 %collective-permute-start.8 = (f32[32,128]{1,0:T(8,128)S(1)}, f32[32,128]{1,0:T(8,128)S(1)}, u32[]{:S(2)}, u32[]{:S(2)}) collective-permute-start(f32[32,128]{1,0:T(8,128)S(1)} %shard_map.70._.a), channel_id=1, source_target_pairs={{0,5},{1,4},{2,7},{3,6},{4,1},{5,0},{6,3},{7,2},{8,13},{9,12},{10,... | collective-permute-start | bytes 49160 | tf_op jit(solution)/shard_map/ppermute | solution.py:176
  25.2 4.4 %collective-permute-start.11 = (f32[32,2944]{1,0:T(8,128)S(1)}, f32[32,2944]{1,0:T(8,128)S(1)}, u32[]{:S(2)}, u32[]{:S(2)}) collective-permute-start(f32[32,2944]{1,0:T(8,128)S(1)} %get-tuple-element.39), channel_id=1, source_target_pairs={{0,1},{1,0},{2,3},{3,2},{4,5},{5,4},{6,7},{7,6},{8,9},{9,8},{10,11... | collective-permute-start | bytes 1130504 | tf_op jit(solution)/shard_map/ppermute | solution.py:170
  25.5 4.1 %collective-permute-start.9 = (f32[32,128]{1,0:T(8,128)S(1)}, f32[32,128]{1,0:T(8,128)S(1)}, u32[]{:S(2)}, u32[]{:S(2)}) collective-permute-start(f32[32,128]{1,0:T(8,128)S(1)} %shard_map.72._.a), channel_id=1, source_target_pairs={{0,9},{1,8},{2,11},{3,10},{4,13},{5,12},{6,15},{7,14},{8,1},{9,0},... | collective-permute-start | bytes 49160 | tf_op jit(solution)/shard_map/ppermute | solution.py:176
  28.9 1.5 %collective-permute-start.12 = (f32[32,640]{1,0:T(8,128)S(1)}, f32[32,640]{1,0:T(8,128)S(1)}, u32[]{:S(2)}, u32[]{:S(2)}) collective-permute-start(f32[32,640]{1,0:T(8,128)S(1)} %get-tuple-element.40), channel_id=1, source_target_pairs={{0,1},{1,0},{2,3},{3,2},{4,5},{5,4},{6,7},{7,6},{8,9},{9,8},{10,11... | collective-permute-start | bytes 245768 | tf_op jit(solution)/shard_map/ppermute | solution.py:170

commit v7 on v6

--- a/solution.py
+++ b/solution.py
@@ -16,7 +16,7 @@
 SPLITS = {2: (20, 28), 3: (10, 22, 28), 4: (5, 14, 23, 28)}
 
 
-def call(kernel, out, in_specs, vmem, scratch=(), flops=0, bytes_accessed=0, aliases=None):
+def call(kernel, out, in_specs, vmem, scratch=(), flops=0, bytes_accessed=0):
     many = isinstance(out, (list, tuple))
     return pl.pallas_call(
         kernel,
@@ -24,7 +24,6 @@
         in_specs=in_specs,
         out_specs=[VMEM] * len(out) if many else VMEM,
         scratch_shapes=list(scratch),
-        input_output_aliases=aliases or {},
         compiler_params=pltpu.CompilerParams(vmem_limit_bytes=vmem),
         cost_estimate=pl.CostEstimate(flops=flops, bytes_accessed=bytes_accessed, transcendentals=0),
     )
@@ -220,6 +219,7 @@
             ],
             [VMEM, VMEM, ANY] + [VMEM] * len(kept),
             4 << 20,
+            flops=64 << 30 if last else 0,
         )(x, weight, low, *kept)
         own.append(o)
         low = add(low, other, o)
@@ -227,12 +227,9 @@
             late = swap(s)
         else:
             sent = s
-            if i == 0:
-                up_own, low = lax.optimization_barrier((up_own, low))
-                up_peer = swap(up_own)
             if i == len(steps) - 2:
-                sent, low = lax.optimization_barrier((sent, low))
-                early = swap(sent)
+                up_own, sent = lax.optimization_barrier((up_own, sent))
+                up_peer, early = swap(up_own), swap(sent)
 
     total = call(
         delta_kernel, jax.ShapeDtypeStruct((half, columns), F32), [VMEM] * (5 + len(own)), 8 << 20,

time: 31.3 us -> 31.2 us (level)
  waiting for transfers between devices: 4.86 us -> 4.19 us
  starting transfers between devices: 18.4 us -> 19 us
    ppermute x3, waiting for transfers between devices: 0.86 us -> 0.18 us  [across(): lax.ppermute(v, both, [(2 * i + w, 2 * (i ^ k) + 1 - w) for i in range(n)...]
    ppermute x3, starting transfers between devices: 5.37 us -> 6.03 us  [across(): lax.ppermute(v, both, [(2 * i + w, 2 * (i ^ k) + 1 - w) for i in range(n)...]
  transfers between devices with their start and end apart: 13 -> 13, of which waited for: 5 -> 4; matrix products, arithmetic and copies ran while one was open for 0% -> 0% of each run, Pallas kernels for 18% -> 18%
where the time goes in v7:
time: 31.2 us; the launch traced here: 31.1 us
  starting transfers between devices  19 us (61%)
  Pallas kernels  7.75 us (25%)
  waiting for transfers between devices  4.19 us (13%)
    ppermute x6, starting transfers between devices, partner(): return lax.ppermute(v, 'ffn', [(i, i ^ k) for i in range(n)])  12 us
    ppermute x3, starting transfers between devices, across(): lax.ppermute(v, both, [(2 * i + w, 2 * (i ^ k) + 1 - w) for i in range(n)...  6.03 us
    pallas_call x4, Pallas kernels, small(): call(functools.partial(base_kernel, a, LANES), [jax.ShapeDtypeStruct((hal...  4.75 us
    ppermute x6, waiting for transfers between devices, partner(): return lax.ppermute(v, 'ffn', [(i, i ^ k) for i in range(n)])  3.74 us
    pallas_call x1, Pallas kernels, small(): call(pack_kernel, [jax.ShapeDtypeStruct((1, rows, wide + LANES), BF16), j...  1.02 us
    ppermute x4, starting transfers between devices, swap(): return lax.ppermute(v, 'width', [(0, 1), (1, 0)])  0.97 us
    pallas_call x1, Pallas kernels, small(): call(delta_kernel, jax.ShapeDtypeStruct((half, columns), F32), [VMEM] * (...  0.79 us
    pallas_call x1, Pallas kernels, small(): call(finish_kernel, jax.ShapeDtypeStruct((half, columns), BF16), [VMEM, V...  0.72 us
  transfers between devices with their start and end apart: 13, of which 4 were waited for; matrix products, arithmetic and copies ran while one was open for 0% of the time, Pallas kernels for 18%

profile of v7, /device:TPU:0, one launch (start us, length us, event | category | flops | bytes accessed | tf_op | source)
XLA Modules:
  0.0 31.1 jit_solution(183302009840649660)
XLA Ops:
  0.0 1.0 %shard_map.64 = (bf16[1,8,4224]{2,1,0:T(8,128)(2,1)S(1)}, f32[8,128]{1,0:T(8,128)S(1)}) custom-call(s32[8]{0:T(128)} %ids.1, s32[8]{0:T(128)} %holder.1, bf16[8,4096]{1,0:T(8,128)(2,1)} %tokens.1), custom_call_target="tpu_custom_call" | custom-call | flops 42949672960 | bytes 131072 | tf_op jit(solution)/shard_map/pallas_call | solution.py:181
  1.0 4.1 %collective-permute-start.2 = (bf16[1,8,4224]{2,1,0:T(8,128)(2,1)S(1)}, bf16[1,8,4224]{2,1,0:T(8,128)(2,1)S(1)}, u32[]{:S(2)}, u32[]{:S(2)}) collective-permute-start(bf16[1,8,4224]{2,1,0:T(8,128)(2,1)S(1)} %get-tuple-element.22.refs_0_), channel_id=1, source_target_pairs={{0,8},{2,10},{4,12},{6,14},{8,0},{10,2},{12,4},{14,6},{1,9},{3,11}... | collective-permute-start | bytes 202760 | tf_op jit(solution)/shard_map/ppermute | solution.py:172
  5.1 1.6 %collective-permute-start.1 = (bf16[1,8,4224]{2,1,0:T(8,128)(2,1)S(1)}, bf16[1,8,4224]{2,1,0:T(8,128)(2,1)S(1)}, u32[]{:S(2)}, u32[]{:S(2)}) collective-permute-start(bf16[1,8,4224]{2,1,0:T(8,128)(2,1)S(1)} %get-tuple-element.22.refs_0_), channel_id=1, source_target_pairs={{0,4},{2,6},{4,0},{6,2},{8,12},{10,14},{12,8},{14,10},{1,5},{3,7},... | collective-permute-start | bytes 202760 | tf_op jit(solution)/shard_map/ppermute | solution.py:172
  6.7 1.5 %collective-permute-start = (bf16[1,8,4224]{2,1,0:T(8,128)(2,1)S(1)}, bf16[1,8,4224]{2,1,0:T(8,128)(2,1)S(1)}, u32[]{:S(2)}, u32[]{:S(2)}) collective-permute-start(bf16[1,8,4224]{2,1,0:T(8,128)(2,1)S(1)} %get-tuple-element.22.refs_0_), channel_id=1, source_target_pairs={{0,2},{2,0},{4,6},{6,4},{8,10},{10,8},{12,14},{14,12},{1,3},{3,1},... | collective-permute-start | bytes 202760 | tf_op jit(solution)/shard_map/ppermute | solution.py:172
  8.2 1.4 %collective-permute-start.3 = (bf16[1,8,4224]{2,1,0:T(8,128)(2,1)S(1)}, bf16[1,8,4224]{2,1,0:T(8,128)(2,1)S(1)}, u32[]{:S(2)}, u32[]{:S(2)}) collective-permute-start(bf16[1,8,4224]{2,1,0:T(8,128)(2,1)S(1)} %collective-permute-done.2.refs_1_.refs_3_), channel_id=1, source_target_pairs={{0,4},{2,6},{4,0},{6,2},{8,12},{10,14},{12,8},{14,10},{1,5},{3,7},... | collective-permute-start | bytes 202760 | tf_op jit(solution)/shard_map/ppermute | solution.py:172
  9.6 1.6 %collective-permute-start.4 = (bf16[2,8,4224]{2,1,0:T(8,128)(2,1)S(1)}, bf16[2,8,4224]{2,1,0:T(8,128)(2,1)S(1)}, u32[]{:S(2)}, u32[]{:S(2)}) collective-permute-start(bf16[2,8,4224]{2,1,0:T(8,128)(2,1)S(1)} %shard_map.65), channel_id=1, source_target_pairs={{0,2},{2,0},{4,6},{6,4},{8,10},{10,8},{12,14},{14,12},{1,3},{3,1},... | collective-permute-start | bytes 405512 | tf_op jit(solution)/shard_map/ppermute | solution.py:172
  11.2 1.3 %collective-permute-done.3.refs_4_ = bf16[1,8,4224]{2,1,0:T(8,128)(2,1)S(1)} collective-permute-done((bf16[1,8,4224]{2,1,0:T(8,128)(2,1)S(1)}, bf16[1,8,4224]{2,1,0:T(8,128)(2,1)S(1)}, u32[]{:S(2)}, u32[]{:S(2)}) %collective-permute-start.3) | collective-permute-done | bytes 67616 | tf_op jit(solution)/shard_map/ppermute | solution.py:172
  12.5 1.9 %collective-permute-start.5 = (bf16[1,8,4224]{2,1,0:T(8,128)(2,1)S(1)}, bf16[1,8,4224]{2,1,0:T(8,128)(2,1)S(1)}, u32[]{:S(2)}, u32[]{:S(2)}) collective-permute-start(bf16[1,8,4224]{2,1,0:T(8,128)(2,1)S(1)} %collective-permute-done.3.refs_4_), channel_id=1, source_target_pairs={{0,2},{2,0},{4,6},{6,4},{8,10},{10,8},{12,14},{14,12},{1,3},{3,1},... | collective-permute-start | bytes 202760 | tf_op jit(solution)/shard_map/ppermute | solution.py:172
  14.4 2.4 %collective-permute-done.5.refs_6_ = bf16[1,8,4224]{2,1,0:T(8,128)(2,1)S(1)} collective-permute-done((bf16[1,8,4224]{2,1,0:T(8,128)(2,1)S(1)}, bf16[1,8,4224]{2,1,0:T(8,128)(2,1)S(1)}, u32[]{:S(2)}, u32[]{:S(2)}) %collective-permute-start.5) | collective-permute-done | bytes 67616 | tf_op jit(solution)/shard_map/ppermute | solution.py:172
  16.8 0.4 %shard_map.66 = (bf16[64,4096]{1,0:T(8,128)(2,1)S(1)}, f32[64,128]{1,0:T(8,128)S(1)}, f32[32,128]{1,0:T(8,128)S(1)}) custom-call(f32[8,128]{1,0:T(8,128)S(1)} %get-tuple-element.21.held, bf16[64,4096]{1,0:T(8,128)(2,1)S(1)} %bitcast.3, bf16[8,32,3584]{2,1,0:T(8,128)(2,1)S(1)} %copy-done.1, bf16[1,8,4224]{2,1,0:T(8,128)(2,1)S(1)} %get-tuple-element.22.refs_0_, ...), custom_call_target="tpu_custom_call" | custom-call | tf_op jit(solution)/shard_map/pallas_call | solution.py:191
  17.3 0.9 %shard_map.67 = (f32[32,640]{1,0:T(8,128)S(1)}, f32[32,640]{1,0:T(8,128)S(1)}) custom-call(bf16[64,4096]{1,0:T(8,128)(2,1)S(1)} %get-tuple-element.25.x, bf16[4096,3584]{1,0:T(8,128)(2,1)S(1)} %copy-done, f32[32,128]{1,0:T(8,128)S(1)} %get-tuple-element.24._.a), custom_call_target="tpu_custom_call" | custom-call | tf_op jit(solution)/shard_map/pallas_call | solution.py:214
  18.2 0.3 collective-permute-done.6.b
  18.5 1.8 %collective-permute-start.7 = (f32[32,128]{1,0:T(8,128)S(1)}, f32[32,128]{1,0:T(8,128)S(1)}, u32[]{:S(2)}, u32[]{:S(2)}) collective-permute-start(f32[32,128]{1,0:T(8,128)S(1)} %shard_map.68._.a), channel_id=1, source_target_pairs={{0,3},{1,2},{2,1},{3,0},{4,7},{5,6},{6,5},{7,4},{8,11},{9,10},{10,... | collective-permute-start | bytes 49160 | tf_op jit(solution)/shard_map/ppermute | solution.py:175
  20.3 1.5 %shard_map.69 = (f32[32,1152]{1,0:T(8,128)S(1)}, f32[32,1792]{1,0:T(8,128)S(1)}) custom-call(bf16[64,4096]{1,0:T(8,128)(2,1)S(1)} %get-tuple-element.25.x, bf16[4096,3584]{1,0:T(8,128)(2,1)S(1)} %copy-done, f32[32,128]{1,0:T(8,128)S(1)} %shard_map.68._.a, f32[32,640]{1,0:T(8,128)S(1)} %get-tuple-element.27.refs_0_), custom_call_target="tpu_custom_call" | custom-call | tf_op jit(solution)/shard_map/pallas_call | solution.py:214
  21.8 1.2 %collective-permute-start.8 = (f32[32,128]{1,0:T(8,128)S(1)}, f32[32,128]{1,0:T(8,128)S(1)}, u32[]{:S(2)}, u32[]{:S(2)}) collective-permute-start(f32[32,128]{1,0:T(8,128)S(1)} %shard_map.70._.a), channel_id=1, source_target_pairs={{0,5},{1,4},{2,7},{3,6},{4,1},{5,0},{6,3},{7,2},{8,13},{9,12},{10,... | collective-permute-start | bytes 49160 | tf_op jit(solution)/shard_map/ppermute | solution.py:175
  22.9 1.5 %shard_map.71 = (f32[32,1152]{1,0:T(8,128)S(1)}, f32[32,2944]{1,0:T(8,128)S(1)}) custom-call(bf16[64,4096]{1,0:T(8,128)(2,1)S(1)} %get-tuple-element.25.x, bf16[4096,3584]{1,0:T(8,128)(2,1)S(1)} %copy-done, f32[32,128]{1,0:T(8,128)S(1)} %shard_map.70._.a, f32[32,1792]{1,0:T(8,128)S(1)} %get-tuple-element.29.refs_0_), custom_call_target="tpu_custom_call" | custom-call | tf_op jit(solution)/shard_map/pallas_call | solution.py:214
  24.4 0.3 collective-permute-start.11
  24.7 0.3 collective-permute-start.10
  25.0 3.1 %collective-permute-start.9 = (f32[32,128]{1,0:T(8,128)S(1)}, f32[32,128]{1,0:T(8,128)S(1)}, u32[]{:S(2)}, u32[]{:S(2)}) collective-permute-start(f32[32,128]{1,0:T(8,128)S(1)} %shard_map.72._.a), channel_id=1, source_target_pairs={{0,9},{1,8},{2,11},{3,10},{4,13},{5,12},{6,15},{7,14},{8,1},{9,0},... | collective-permute-start | bytes 49160 | tf_op jit(solution)/shard_map/ppermute | solution.py:175
  28.1 0.9 %shard_map.73 = (f32[32,640]{1,0:T(8,128)S(1)}, f32[32,640]{1,0:T(8,128)S(1)}) custom-call(bf16[64,4096]{1,0:T(8,128)(2,1)S(1)} %get-tuple-element.25.x, bf16[4096,3584]{1,0:T(8,128)(2,1)S(1)} %copy-done, f32[32,128]{1,0:T(8,128)S(1)} %shard_map.72._.a), custom_call_target="tpu_custom_call" | custom-call | flops 68719476736 | tf_op jit(solution)/shard_map/pallas_call | solution.py:214
  29.0 0.4 %collective-permute-start.12 = (f32[32,640]{1,0:T(8,128)S(1)}, f32[32,640]{1,0:T(8,128)S(1)}, u32[]{:S(2)}, u32[]{:S(2)}) collective-permute-start(f32[32,640]{1,0:T(8,128)S(1)} %get-tuple-element.36), channel_id=1, source_target_pairs={{0,1},{1,0},{2,3},{3,2},{4,5},{5,4},{6,7},{7,6},{8,9},{9,8},{10,11... | collective-permute-start | bytes 245768 | tf_op jit(solution)/shard_map/ppermute | solution.py:169
  29.4 0.2 collective-permute-done.9.b
  29.5 0.8 %shard_map.75.total = f32[32,3584]{1,0:T(8,128)S(1)} custom-call(f32[32,128]{1,0:T(8,128)S(1)} %shard_map.74.low, f32[64,128]{1,0:T(8,128)S(1)} %get-tuple-element.32.ids, bf16[8,32,3584]{2,1,0:T(8,128)(2,1)S(1)} %copy-done.1, bf16[8,32,3584]{2,1,0:T(8,128)(2,1)S(1)} %collective-permute-done.10.up_peer, f32[32,2944]{1,0:T(8,128)S(1)} %collective-permute-done.11.got, ...), custom_call_target="tpu_custom_call" | custom-call | flops 4294967296 | tf_op jit(solution)/shard_map/pallas_call | solution.py:234
  30.4 0.7 %shard_map.76 = bf16[32,3584]{1,0:T(8,128)(2,1)} custom-call(f32[32,3584]{1,0:T(8,128)S(1)} %shard_map.75.total, f32[32,640]{1,0:T(8,128)S(1)} %collective-permute-done.12.got), custom_call_target="tpu_custom_call" | custom-call | tf_op jit(solution)/shard_map/pallas_call | solution.py:238
  (21 shorter events, 0.1 us)
Async XLA Ops:
  0.0 16.8 %copy-start.1 = (bf16[8,32,3584]{2,1,0:T(8,128)(2,1)S(1)}, bf16[8,32,3584]{2,1,0:T(8,128)(2,1)}, u32[]{:S(2)}) copy-start(bf16[8,32,3584]{2,1,0:T(8,128)(2,1)} %up_own) | copy-start | bytes 5505028
  0.0 16.8 %copy-start.2 = (bf16[1,4096,64]{1,2,0:T(8,128)(2,1)S(1)}, bf16[1,4096,64]{1,2,0:T(8,128)(2,1)}, u32[]{:S(2)}) copy-start(bf16[1,4096,64]{1,2,0:T(8,128)(2,1)} %param.10) | copy-start | bytes 1572868
  0.0 17.3 %copy-start = (bf16[4096,3584]{1,0:T(8,128)(2,1)S(1)}, bf16[4096,3584]{1,0:T(8,128)(2,1)}, u32[]{:S(2)}) copy-start(bf16[4096,3584]{1,0:T(8,128)(2,1)} %w.7) | copy-start | bytes 88080384
  1.0 7.2 %collective-permute-start.2 = (bf16[1,8,4224]{2,1,0:T(8,128)(2,1)S(1)}, bf16[1,8,4224]{2,1,0:T(8,128)(2,1)S(1)}, u32[]{:S(2)}, u32[]{:S(2)}) collective-permute-start(bf16[1,8,4224]{2,1,0:T(8,128)(2,1)S(1)} %get-tuple-element.22.refs_0_), channel_id=1, source_target_pairs={{0,8},{2,10},{4,12},{6,14},{8,0},{10,2},{12,4},{14,6},{1,9},{3,11}... | collective-permute-start | bytes 202760 | tf_op jit(solution)/shard_map/ppermute | solution.py:172
  5.1 4.5 %collective-permute-start.1 = (bf16[1,8,4224]{2,1,0:T(8,128)(2,1)S(1)}, bf16[1,8,4224]{2,1,0:T(8,128)(2,1)S(1)}, u32[]{:S(2)}, u32[]{:S(2)}) collective-permute-start(bf16[1,8,4224]{2,1,0:T(8,128)(2,1)S(1)} %get-tuple-element.22.refs_0_), channel_id=1, source_target_pairs={{0,4},{2,6},{4,0},{6,2},{8,12},{10,14},{12,8},{14,10},{1,5},{3,7},... | collective-permute-start | bytes 202760 | tf_op jit(solution)/shard_map/ppermute | solution.py:172
  6.7 4.5 %collective-permute-start = (bf16[1,8,4224]{2,1,0:T(8,128)(2,1)S(1)}, bf16[1,8,4224]{2,1,0:T(8,128)(2,1)S(1)}, u32[]{:S(2)}, u32[]{:S(2)}) collective-permute-start(bf16[1,8,4224]{2,1,0:T(8,128)(2,1)S(1)} %get-tuple-element.22.refs_0_), channel_id=1, source_target_pairs={{0,2},{2,0},{4,6},{6,4},{8,10},{10,8},{12,14},{14,12},{1,3},{3,1},... | collective-permute-start | bytes 202760 | tf_op jit(solution)/shard_map/ppermute | solution.py:172
  8.2 4.3 %collective-permute-start.3 = (bf16[1,8,4224]{2,1,0:T(8,128)(2,1)S(1)}, bf16[1,8,4224]{2,1,0:T(8,128)(2,1)S(1)}, u32[]{:S(2)}, u32[]{:S(2)}) collective-permute-start(bf16[1,8,4224]{2,1,0:T(8,128)(2,1)S(1)} %collective-permute-done.2.refs_1_.refs_3_), channel_id=1, source_target_pairs={{0,4},{2,6},{4,0},{6,2},{8,12},{10,14},{12,8},{14,10},{1,5},{3,7},... | collective-permute-start | bytes 202760 | tf_op jit(solution)/shard_map/ppermute | solution.py:172
  9.6 7.2 %collective-permute-start.4 = (bf16[2,8,4224]{2,1,0:T(8,128)(2,1)S(1)}, bf16[2,8,4224]{2,1,0:T(8,128)(2,1)S(1)}, u32[]{:S(2)}, u32[]{:S(2)}) collective-permute-start(bf16[2,8,4224]{2,1,0:T(8,128)(2,1)S(1)} %shard_map.65), channel_id=1, source_target_pairs={{0,2},{2,0},{4,6},{6,4},{8,10},{10,8},{12,14},{14,12},{1,3},{3,1},... | collective-permute-start | bytes 405512 | tf_op jit(solution)/shard_map/ppermute | solution.py:172
  12.5 4.3 %collective-permute-start.5 = (bf16[1,8,4224]{2,1,0:T(8,128)(2,1)S(1)}, bf16[1,8,4224]{2,1,0:T(8,128)(2,1)S(1)}, u32[]{:S(2)}, u32[]{:S(2)}) collective-permute-start(bf16[1,8,4224]{2,1,0:T(8,128)(2,1)S(1)} %collective-permute-done.3.refs_4_), channel_id=1, source_target_pairs={{0,2},{2,0},{4,6},{6,4},{8,10},{10,8},{12,14},{14,12},{1,3},{3,1},... | collective-permute-start | bytes 202760 | tf_op jit(solution)/shard_map/ppermute | solution.py:172
  17.3 1.2 %collective-permute-start.6 = (f32[32,128]{1,0:T(8,128)S(1)}, f32[32,128]{1,0:T(8,128)S(1)}, u32[]{:S(2)}, u32[]{:S(2)}) collective-permute-start(f32[32,128]{1,0:T(8,128)S(1)} %get-tuple-element.24._.a), channel_id=1, source_target_pairs={{0,1},{1,0},{2,3},{3,2},{4,5},{5,4},{6,7},{7,6},{8,9},{9,8},{10,11... | collective-permute-start | bytes 49160 | tf_op jit(solution)/shard_map/ppermute | solution.py:169
  18.5 3.3 %collective-permute-start.7 = (f32[32,128]{1,0:T(8,128)S(1)}, f32[32,128]{1,0:T(8,128)S(1)}, u32[]{:S(2)}, u32[]{:S(2)}) collective-permute-start(f32[32,128]{1,0:T(8,128)S(1)} %shard_map.68._.a), channel_id=1, source_target_pairs={{0,3},{1,2},{2,1},{3,0},{4,7},{5,6},{6,5},{7,4},{8,11},{9,10},{10,... | collective-permute-start | bytes 49160 | tf_op jit(solution)/shard_map/ppermute | solution.py:175
  21.8 3.2 %collective-permute-start.8 = (f32[32,128]{1,0:T(8,128)S(1)}, f32[32,128]{1,0:T(8,128)S(1)}, u32[]{:S(2)}, u32[]{:S(2)}) collective-permute-start(f32[32,128]{1,0:T(8,128)S(1)} %shard_map.70._.a), channel_id=1, source_target_pairs={{0,5},{1,4},{2,7},{3,6},{4,1},{5,0},{6,3},{7,2},{8,13},{9,12},{10,... | collective-permute-start | bytes 49160 | tf_op jit(solution)/shard_map/ppermute | solution.py:175
  24.4 5.1 %collective-permute-start.11 = (f32[32,2944]{1,0:T(8,128)S(1)}, f32[32,2944]{1,0:T(8,128)S(1)}, u32[]{:S(2)}, u32[]{:S(2)}) collective-permute-start(f32[32,2944]{1,0:T(8,128)S(1)} %get-tuple-element.35), channel_id=1, source_target_pairs={{0,1},{1,0},{2,3},{3,2},{4,5},{5,4},{6,7},{7,6},{8,9},{9,8},{10,11... | collective-permute-start | bytes 1130504 | tf_op jit(solution)/shard_map/ppermute | solution.py:169
  24.7 4.8 %collective-permute-start.10 = (bf16[8,32,3584]{2,1,0:T(8,128)(2,1)S(1)}, bf16[8,32,3584]{2,1,0:T(8,128)(2,1)S(1)}, u32[]{:S(2)}, u32[]{:S(2)}) collective-permute-start(bf16[8,32,3584]{2,1,0:T(8,128)(2,1)S(1)} %copy-done.1), channel_id=1, source_target_pairs={{0,1},{1,0},{2,3},{3,2},{4,5},{5,4},{6,7},{7,6},{8,9},{9,8},{10,11... | collective-permute-start | bytes 5505032 | tf_op jit(solution)/shard_map/ppermute | solution.py:169
  25.0 4.5 %collective-permute-start.9 = (f32[32,128]{1,0:T(8,128)S(1)}, f32[32,128]{1,0:T(8,128)S(1)}, u32[]{:S(2)}, u32[]{:S(2)}) collective-permute-start(f32[32,128]{1,0:T(8,128)S(1)} %shard_map.72._.a), channel_id=1, source_target_pairs={{0,9},{1,8},{2,11},{3,10},{4,13},{5,12},{6,15},{7,14},{8,1},{9,0},... | collective-permute-start | bytes 49160 | tf_op jit(solution)/shard_map/ppermute | solution.py:175
  29.0 1.4 %collective-permute-start.12 = (f32[32,640]{1,0:T(8,128)S(1)}, f32[32,640]{1,0:T(8,128)S(1)}, u32[]{:S(2)}, u32[]{:S(2)}) collective-permute-start(f32[32,640]{1,0:T(8,128)S(1)} %get-tuple-element.36), channel_id=1, source_target_pairs={{0,1},{1,0},{2,3},{3,2},{4,5},{5,4},{6,7},{7,6},{8,9},{9,8},{10,11... | collective-permute-start | bytes 245768 | tf_op jit(solution)/shard_map/ppermute | solution.py:169
